TPU v7x, 32 devices: a whole 2x2x4 slice. The times are simulated.
32 devices in a mesh: src: 16 (over z, y, x), seg: 2 (over core).
Axes of the slice: x: 2, y: 2, z: 4, core: 2. Of those that a mesh axis runs over, the one named last changes fastest.
Arguments:
- spectra: bfloat16 [4096, 2, 2, 2048], P('src', 'seg'), may hold values from -6 to 6
- pairs: int32 [32, 2], P('src'), may hold values from 0 to 15, as said below
- pair_count: int32 [16], P('src'), may hold values from 1 to 2, as said below
Outputs:
- stacks: float32 [32, 256, 1536], P('src', 'seg')
Inputs may be any that keep to these rules, and one draw needn't show every extreme that they name: pairs[p] = (i, j) with d <= i <= j <= min(d + 4, 15) where d = p // 2; every owner d with d + 4 < 16 has a slot with j = d + 4. `pair_count`: at least one owner has all 2 slots live.
All inputs are finite; a program needn't handle non-finite values.
Results may differ from a plain program's by a relative error of at most 0.0011.
Values may be sent and summed in bfloat16 or wider, within the bound.
No kernel may reach another device: no remote copies, remote signals or barrier semaphores. Data moves between devices by JAX's collectives and lax.ppermute only.
A program may use at most 128 MiB of HBM per device.

v0:
```python
import jax
import jax.numpy as jnp
from jax import lax
from jax.sharding import PartitionSpec as P

LAGS = 6
REACH = 4


def from_behind(block, axis, distance):
    devices = range(lax.axis_size(axis))
    route = [(i - distance, i) for i in devices if i - distance in devices]
    return lax.ppermute(block, axis, route)


def lag_tables(freqs, lags):
    freq = jnp.arange(freqs, dtype=jnp.int32)
    lagval = jnp.arange(lags, dtype=jnp.int32) - lags // 2
    phase = lagval[:, None] * freq[None, :] % (2 * freqs)
    theta = phase.astype(jnp.float32) * (jnp.pi / freqs)
    return (jnp.cos(theta), jnp.sin(theta))


def build_rotated(block, cosine, sine):
    lags = cosine.shape[0]
    real_part = block[:, :, 0, :].astype(jnp.float32)[:, None]
    imag_part = block[:, :, 1, :].astype(jnp.float32)[:, None]
    cos_b = cosine[None, :, None, :]
    sin_b = sine[None, :, None, :]
    first = real_part * cos_b - imag_part * sin_b
    second = imag_part * cos_b + real_part * sin_b
    stacked = jnp.stack([first, second], axis=3)
    return stacked.reshape(block.shape[0] * lags, -1).astype(jnp.bfloat16)


def slot_product(first, right, live, cosine, sine, count):
    lags = cosine.shape[0]
    rotated = build_rotated(first, cosine, sine)
    prod = lax.dot_general(
        rotated, right, (((1,), (1,)), ((), ())), preferred_element_type=jnp.float32
    )
    width = right.shape[0]
    prod = jnp.transpose(prod.reshape(count, lags, width), (0, 2, 1)).reshape(count, width * lags)
    return jnp.where(live, prod, jnp.zeros_like(prod))


def shards(spectra, pairs, pair_count):
    blk = spectra.shape[0]
    freqs = spectra.shape[3]
    cosine, sine = lag_tables(freqs, LAGS)
    me_index = lax.axis_index("src")
    blocks = [spectra]
    for step in range(1, REACH + 1):
        blocks.append(from_behind(spectra, "src", -step))
    window = jnp.stack(blocks, axis=0)
    hours_all = spectra.shape[1] * lax.axis_size("seg")
    scale = float(hours_all * freqs) ** (-0.5)
    num_slots = pairs.shape[0]
    firsts = []
    rights = []
    lives = []
    for slot in range(num_slots):
        first = lax.dynamic_index_in_dim(window, pairs[slot, 0] - me_index, 0, keepdims=False)
        second = lax.dynamic_index_in_dim(window, pairs[slot, 1] - me_index, 0, keepdims=False)
        firsts.append(first)
        rights.append(second.reshape(blk, -1))
        lives.append(slot < pair_count[0])
    share = blk // lax.axis_size("seg")
    results = [
        slot_product(firsts[s], rights[s], lives[s], cosine, sine, share * lax.axis_size("seg"))
        for s in range(num_slots)
    ]
    summed = lax.psum_scatter(jnp.stack(results, axis=1), "seg", scatter_dimension=0, tiled=True)
    stacked = jnp.transpose(summed, (1, 0, 2))
    return stacked * scale


def solution(mesh):
    in_specs = (P("src", "seg", None, None), P("src", None), P("src"))
    out_specs = P("src", "seg", None)
    return jax.shard_map(shards, mesh=mesh, in_specs=in_specs, out_specs=out_specs, check_vma=False)
```

profile of v0, /device:TPU:0, one launch (start us, length us, event | category | flops | bytes accessed | tf_op | source)
XLA Modules:
  0.0 467.3 jit_solution(13302762447399007137)
XLA Ops:
  6.5 4.0 copy.17
  10.5 1.3 collective-permute-start
  11.8 1.3 collective-permute-start.1
  13.1 1.3 collective-permute-start.2
  14.4 1.3 collective-permute-start.3
  20.6 40.7 %collective-permute-done = bf16[256,1,2,2048]{3,0,2,1:T(8,128)(2,1)} collective-permute-done((bf16[256,1,2,2048]{3,0,2,1:T(8,128)(2,1)}, bf16[256,1,2,2048]{3,0,2,1:T(8,128)(2,1)}, u32[]{:S(2)}, u32[]{:S(2)}) %collective-permute-start) | collective-permute-done | bytes 2097184 | tf_op jit(solution)/shard_map/ppermute | solution.py:13
  61.3 1.7 bitcast_dynamic-update-slice_fusion.3
  63.0 46.3 %collective-permute-done.1 = bf16[256,1,2,2048]{3,0,2,1:T(8,128)(2,1)} collective-permute-done((bf16[256,1,2,2048]{3,0,2,1:T(8,128)(2,1)}, bf16[256,1,2,2048]{3,0,2,1:T(8,128)(2,1)}, u32[]{:S(2)}, u32[]{:S(2)}) %collective-permute-start.1) | collective-permute-done | bytes 2097184 | tf_op jit(solution)/shard_map/ppermute | solution.py:13
  109.3 1.7 bitcast_dynamic-update-slice_fusion.2
  111.1 1.7 bitcast_dynamic-update-slice_fusion.1
  112.8 155.8 %collective-permute-done.3 = bf16[256,1,2,2048]{3,0,2,1:T(8,128)(2,1)} collective-permute-done((bf16[256,1,2,2048]{3,0,2,1:T(8,128)(2,1)}, bf16[256,1,2,2048]{3,0,2,1:T(8,128)(2,1)}, u32[]{:S(2)}, u32[]{:S(2)}) %collective-permute-start.3) | collective-permute-done | bytes 2097184 | tf_op jit(solution)/shard_map/ppermute | solution.py:13
  268.6 1.7 bitcast_dynamic-update-slice_fusion
  270.3 2.6 constant_dynamic-slice_fusion.1
  273.9 9.5 %fusion = (bf16[256,6,1,1,2048]{4,0,3,2,1:T(8,128)(2,1)S(1)}, bf16[256,6,1,1,2048]{4,0,3,2,1:T(8,128)(2,1)S(1)}, bf16[256,6,1,1,2048]{4,0,1,3,2:T(8,128)(2,1)}, bf16[256,6,1,1,2048]{4,0,1,3,2:T(8,128)(2,1)}) fusion(f32[6,2048]{1,0:T(8,128)S(1)} %get-tuple-element.24, f32[256,2048]{1,0:T(8,128)S(1)} %get-tuple-element.25, f32[6,2048]{1,0:T(8,128)S(1)} %get-tuple-element.23, ...), kind=kLoop, calls=%fused_computation.6 | loop fusion | flops 50331648 | bytes 33652736 | tf_op jit(solution)/shard_map/stack | solution.py:32
  284.6 37.2 %copy.22 = bf16[256,6,1,2,2048]{4,3,0,1,2:T(2,128)(2,1)} copy(bf16[256,6,1,2,2048]{4,0,3,2,1:T(8,128)(2,1)S(1)} %pad_maximum_fusion) | data formatting | bytes 25165824 | tf_op jit(solution)/shard_map/stack | solution.py:32
  321.8 21.0 %convert_element_type.75 = bf16[256,6,4096]{2,0,1:T(8,128)(2,1)} reshape(bf16[256,6,1,2,2048]{4,3,0,1,2:T(2,128)(2,1)} %copy.22) | data formatting | bytes 25165824 | tf_op jit(solution)/shard_map/convert_element_type | solution.py:33
  342.8 5.0 %copy.23 = bf16[1,256,1,2,2048]{4,3,1,2,0:T(2,128)(2,1)} copy(bf16[1,256,1,2,2048]{4,1,3,2,0:T(8,128)(2,1)} %get-tuple-element.5) | data formatting | bytes 4194304 | tf_op jit(solution)/shard_map/jit(dynamic_index_in_dim)/dynamic_slice | solution.py:64
  347.9 4.5 reshape.231
  352.4 7.1 %select_bitcast_fusion.1 = f32[256,256,6]{0,1,2:T(8,128)S(1)} fusion(bf16[256,6,4096]{2,0,1:T(8,128)(2,1)} %convert_element_type.75, bf16[256,4096,1]{1,0,2:T(8,128)(2,1)} %reshape.231, pred[]{:T(512)} %bitcast), kind=kOutput, calls=%fused_computation.20 | convolution fusion | flops 3221618688 | bytes 16252929 | tf_op jit(solution)/shard_map/dot_general | solution.py:39
  359.5 2.3 copy.24
  361.7 2.6 select_n.87
  364.3 6.1 %pad_maximum_fusion.1 = bf16[256,6,1,2,2048]{4,0,1,3,2:T(8,128)(2,1)S(1)} fusion(bf16[256,6,1,1,2048]{4,0,1,3,2:T(8,128)(2,1)} %get-tuple-element.17, bf16[256,6,1,1,2048]{4,0,1,3,2:T(8,128)(2,1)} %get-tuple-element.18), kind=kLoop, calls=%fused_computation.1 | loop fusion | flops 6291456 | bytes 25165824 | tf_op jit(solution)/shard_map/stack | solution.py:32
  370.4 37.2 %copy.25 = bf16[256,6,1,2,2048]{4,3,0,1,2:T(2,128)(2,1)} copy(bf16[256,6,1,2,2048]{4,0,1,3,2:T(8,128)(2,1)S(1)} %pad_maximum_fusion.1) | data formatting | bytes 25165824 | tf_op jit(solution)/shard_map/stack | solution.py:32
  407.6 21.0 %convert_element_type.76 = bf16[256,6,4096]{2,0,1:T(8,128)(2,1)} reshape(bf16[256,6,1,2,2048]{4,3,0,1,2:T(2,128)(2,1)} %copy.25) | data formatting | bytes 25165824 | tf_op jit(solution)/shard_map/convert_element_type | solution.py:33
  428.6 3.5 copy.26
  432.1 3.3 reshape.232
  435.4 6.5 %select_bitcast_fusion = f32[256,256,6]{0,1,2:T(8,128)S(1)} fusion(bf16[256,6,4096]{2,0,1:T(8,128)(2,1)} %convert_element_type.76, bf16[256,4096,1]{1,0,2:T(8,128)(2,1)S(1)} %reshape.232, pred[]{:T(512)} %bitcast.14), kind=kOutput, calls=%fused_computation.19 | convolution fusion | flops 3221618688 | bytes 16252929 | tf_op jit(solution)/shard_map/dot_general | solution.py:39
  442.8 1.4 select_n.93
  444.2 3.7 pad_maximum_fusion.2
  447.9 9.4 %reduce-scatter.2.cloned.1.call-done = f32[128,2,1536]{0,2,1:T(8,128)} async-done(((f32[256,2,1536]{0,2,1:T(8,128)}), f32[128,2,1536]{0,2,1:T(8,128)}) %reduce-scatter.2.cloned.1.call-update) | async-done | bytes 1572880 | tf_op jit(solution)/shard_map/reduce_scatter | solution.py:73
  457.3 1.5 multiply_bitcast_fusion
  458.8 1.6 copy.28
  (14 shorter events, 5.1 us)
Async XLA Ops:
  6.5 12.9 %copy-start = (bf16[256,1,2,2048]{3,2,1,0:T(2,128)(2,1)S(1)}, bf16[256,1,2,2048]{3,2,1,0:T(2,128)(2,1)}, u32[]{:S(2)}) copy-start(bf16[256,1,2,2048]{3,2,1,0:T(2,128)(2,1)} %param.3) | copy-start | bytes 6291460
  6.5 9.2 %copy-start.1 = (s32[2,2]{1,0:T(2,128)S(1)}, s32[2,2]{1,0:T(2,128)}, u32[]{:S(2)}) copy-start(s32[2,2]{1,0:T(2,128)} %param.4) | copy-start | bytes 52
  6.5 450.8 %reduce-scatter.2.cloned.1.call-start = ((), (), s32[]{:S(2)}) async-start(), calls=%async_computation.1 | async-start | bytes 4718592 | tf_op jit(solution)/shard_map/reduce_scatter | solution.py:73
  10.5 50.8 %collective-permute-start = (bf16[256,1,2,2048]{3,0,2,1:T(8,128)(2,1)}, bf16[256,1,2,2048]{3,0,2,1:T(8,128)(2,1)}, u32[]{:S(2)}, u32[]{:S(2)}) collective-permute-start(bf16[256,1,2,2048]{3,0,2,1:T(8,128)(2,1)} %copy.17), channel_id=1, source_target_pairs={{2,0},{4,2},{6,4},{8,6},{10,8},{12,10},{14,12},{16,14},{18,16},{20... | collective-permute-start | bytes 6291464 | tf_op jit(solution)/shard_map/ppermute | solution.py:13
  11.8 97.5 %collective-permute-start.1 = (bf16[256,1,2,2048]{3,0,2,1:T(8,128)(2,1)}, bf16[256,1,2,2048]{3,0,2,1:T(8,128)(2,1)}, u32[]{:S(2)}, u32[]{:S(2)}) collective-permute-start(bf16[256,1,2,2048]{3,0,2,1:T(8,128)(2,1)} %copy.17), channel_id=1, source_target_pairs={{4,0},{6,2},{8,4},{10,6},{12,8},{14,10},{16,12},{18,14},{20,16},{2... | collective-permute-start | bytes 6291464 | tf_op jit(solution)/shard_map/ppermute | solution.py:13
  13.1 98.0 %collective-permute-start.2 = (bf16[256,1,2,2048]{3,0,2,1:T(8,128)(2,1)}, bf16[256,1,2,2048]{3,0,2,1:T(8,128)(2,1)}, u32[]{:S(2)}, u32[]{:S(2)}) collective-permute-start(bf16[256,1,2,2048]{3,0,2,1:T(8,128)(2,1)} %copy.17), channel_id=1, source_target_pairs={{6,0},{8,2},{10,4},{12,6},{14,8},{16,10},{18,12},{20,14},{22,16},{... | collective-permute-start | bytes 6291464 | tf_op jit(solution)/shard_map/ppermute | solution.py:13
  14.4 254.2 %collective-permute-start.3 = (bf16[256,1,2,2048]{3,0,2,1:T(8,128)(2,1)}, bf16[256,1,2,2048]{3,0,2,1:T(8,128)(2,1)}, u32[]{:S(2)}, u32[]{:S(2)}) collective-permute-start(bf16[256,1,2,2048]{3,0,2,1:T(8,128)(2,1)} %copy.17), channel_id=1, source_target_pairs={{8,0},{10,2},{12,4},{14,6},{16,8},{18,10},{20,12},{22,14},{24,16},... | collective-permute-start | bytes 6291464 | tf_op jit(solution)/shard_map/ppermute | solution.py:13
Sparse Core Ops, SparseCore 0:
  448.0 9.2 reduce-scatter.1
where the time goes:
time: 469 us; the launch traced here: 467 us
  waiting for transfers between devices  252 us (54%)
  local copies, waits for them, and re-layouts  156 us (33%)
  other arithmetic  23.4 us (5%)
  between operations  16.6 us (4%)
  matrix products  13.6 us (3%)
  starting transfers between devices  5.16 us (1%)
    ppermute x4, waiting for transfers between devices, from_behind(): return lax.ppermute(block, axis, route)  243 us
    another operation x2, local copies, waits for them, and re-layouts, build_rotated(): stacked = jnp.stack([first, second], axis=3)  74.3 us
    convert_element_type x2, local copies, waits for them, and re-layouts, build_rotated(): return stacked.reshape(block.shape[0] * lags, -1).astype(jnp.bfloat16)  42 us
    another operation x3, other arithmetic, build_rotated(): stacked = jnp.stack([first, second], axis=3)  16.8 us
    dot_general x2, matrix products, slot_product(): lax.dot_general(rotated, right, (((1,), (1,)), ((), ())), preferred_eleme...  13.6 us
    dynamic_slice x3, local copies, waits for them, and re-layouts, shards(): lax.dynamic_index_in_dim(window, pairs[slot, 1] - me_index, 0, keepdims=F...  11.1 us
    unnamed x9, local copies, waits for them, and re-layouts  9.99 us
    reduce_scatter x1, waiting for transfers between devices, shards(): lax.psum_scatter(jnp.stack(results, axis=1), 'seg', scatter_dimension=0,...  9.4 us
  transfers between devices with their start and end apart: 5, of which 4 were waited for; matrix products, arithmetic and copies ran while one was open for 1% of the time, Pallas kernels for 0%

commit v1 on v0

v1 whole, which is shorter than its diff:
```python
import functools

import jax
import jax.numpy as jnp
from jax import lax
from jax.experimental import pallas as pl
from jax.experimental.pallas import tpu as pltpu
from jax.sharding import PartitionSpec as P

LAGS = 6
REACH = 4
SLOTS = 2
WINDOW = 6
VMEM = 56 * 1024 * 1024


def routes(axis, move):
    size = lax.axis_size(axis)
    return [(i, move(i)) for i in range(size) if 0 <= move(i) < size]


def to_pair(value):
    return lax.ppermute(value, "src", routes("src", lambda d: d ^ 1))


def to_row(value):
    return lax.ppermute(value, "src", routes("src", lambda d: d ^ 2))


def to_below(value):
    return lax.ppermute(value, "src", routes("src", lambda d: d - REACH))


def lag_tables(freqs, lags):
    freq = jnp.arange(freqs, dtype=jnp.int32)
    lagval = jnp.arange(lags, dtype=jnp.int32) - lags // 2
    phase = lagval[:, None] * freq[None, :] % (2 * freqs)
    theta = phase.astype(jnp.float32) * (jnp.pi / freqs)
    return (jnp.cos(theta), jnp.sin(theta))


def rotate_into(x_ref, real, imag, table, rows, row, cols, half):
    height = real.shape[0]
    other = pl.ds(half + cols, real.shape[1])
    here = pl.ds(cols, real.shape[1])

    def put(lag, first, second):
        at = pl.ds(lag * rows + row, height)
        x_ref[at, here] = first.astype(jnp.bfloat16)
        x_ref[at, other] = second.astype(jnp.bfloat16)

    put(3, real, imag)
    for plus, minus, row_c in ((0, None, 0), (4, 2, 1), (5, 1, 2)):
        cos, sin = table(row_c), table(row_c + 3)
        rc, im_s, ic, rs = real * cos, imag * sin, imag * cos, real * sin
        put(plus, rc - im_s, ic + rs)
        if minus is not None:
            put(minus, rc + im_s, ic - rs)


def corr_kernel(count, meta, table, *refs):
    held = refs[:WINDOW]
    outs = refs[WINDOW : WINDOW + count]
    left, right, x_ref, sems = refs[WINDOW + count :]
    slot, part = pl.program_id(0), pl.program_id(1)
    now = lax.rem(slot, 2)
    slots = pl.num_programs(0)

    def fetch(which, buffer):
        for side, target in ((0, left), (1, right)):
            name = meta[2 * which + side]
            for k in range(WINDOW):

                @pl.when(name == k)
                def _():
                    pltpu.make_async_copy(held[k], target.at[buffer], sems.at[side, buffer]).start()

    @pl.when((slot == 0) & (part == 0))
    def _():
        fetch(0, 0)

    @pl.when(part == 0)
    def _():
        @pl.when(slot + 1 < slots)
        def _():
            fetch(slot + 1, 1 - now)

        for side, target in ((0, left), (1, right)):
            pltpu.make_async_copy(held[0], target.at[now], sems.at[side, now]).wait()

    rows = outs[0].shape[2]
    half = left.shape[2] // 2
    seg = lax.rem(meta[2 * slots] + part, count)
    wide, high = 256, 16

    for cols in range(0, half, wide):
        def step(at, carry):
            src = pl.ds(pl.multiple_of(seg * rows + at * high, high), high)
            real = left[now, src, pl.ds(cols, wide)].astype(jnp.float32)
            imag = left[now, src, pl.ds(half + cols, wide)].astype(jnp.float32)
            look = lambda r: table[pl.ds(r, 1), pl.ds(cols, wide)]
            rotate_into(x_ref, real, imag, look, rows, pl.multiple_of(at * high, high), cols, half)
            return carry

        lax.fori_loop(0, rows // high, step, 0, unroll=True)

    product = lax.dot_general(
        x_ref[...], right[now], (((1,), (1,)), ((), ())), preferred_element_type=jnp.float32
    )
    for k in range(count):

        @pl.when(part == k)
        def _():
            outs[k][0] = product.reshape(LAGS, rows, right.shape[1])


def correlate(meta, table, held, count, slots):
    height, width = held[0].shape
    rows = height // count
    shape = jax.ShapeDtypeStruct((slots, LAGS, rows, height), jnp.float32)
    return pl.pallas_call(
        functools.partial(corr_kernel, count),
        out_shape=[shape] * count,
        grid=(slots, count),
        in_specs=[pl.BlockSpec(memory_space=pltpu.SMEM), pl.BlockSpec(memory_space=pltpu.VMEM)]
        + [pl.BlockSpec(memory_space=pl.ANY)] * WINDOW,
        out_specs=[pl.BlockSpec((1, LAGS, rows, height), lambda s, k: (s, 0, 0, 0))] * count,
        scratch_shapes=[
            pltpu.VMEM((2, height, width), jnp.bfloat16),
            pltpu.VMEM((2, height, width), jnp.bfloat16),
            pltpu.VMEM((LAGS * rows, width), jnp.bfloat16),
            pltpu.SemaphoreType.DMA((2, 2)),
        ],
        compiler_params=pltpu.CompilerParams(vmem_limit_bytes=VMEM),
        cost_estimate=pl.CostEstimate(
            flops=2 * slots * LAGS * height * height * width, bytes_accessed=4 * slots * height * width, transcendentals=0
        ),
    )(meta, table, *held)


def finish_kernel(count, scale, live, spread, *refs):
    parts, out = refs[: count + 1], refs[count + 1]
    slot = pl.program_id(0)
    rows, width = parts[0].shape[2], parts[0].shape[3]
    step = spread.shape[0] // LAGS
    high, low = [], []
    for at in range(0, width, step):
        lags = []
        for lag in range(LAGS):
            total = parts[0][0, lag, :, at : at + step]
            for part in parts[1:]:
                total = total + part[0, lag, :, at : at + step]
            lags.append(total)
        total = jnp.concatenate(lags, axis=1)
        top = total.astype(jnp.bfloat16)
        high.append(top)
        low.append((total - top.astype(jnp.float32)).astype(jnp.bfloat16))
    stacked = jnp.concatenate(high + low, axis=0)
    moved = jnp.dot(stacked, spread[...], preferred_element_type=jnp.float32)
    keep = live[slot] > 0
    for k in range(width // step):
        both = moved[k * rows : (k + 1) * rows] + moved[(k + width // step) * rows : (k + width // step + 1) * rows]
        out[0, :, k * step * LAGS : (k + 1) * step * LAGS] = jnp.where(keep, both * scale, jnp.zeros_like(both))


def finish(live, parts, scale):
    slots, _, rows, width = parts[-1].shape
    step = min(128, width)
    lag_of, chan_of = jnp.arange(LAGS * step) // step, jnp.arange(LAGS * step) % step
    spread = (jnp.arange(LAGS * step)[None, :] == (chan_of * LAGS + lag_of)[:, None]).astype(jnp.bfloat16)
    return pl.pallas_call(
        functools.partial(finish_kernel, len(parts) - 1, scale),
        out_shape=jax.ShapeDtypeStruct((slots, rows, width * LAGS), jnp.float32),
        grid=(slots,),
        in_specs=[pl.BlockSpec(memory_space=pltpu.SMEM), pl.BlockSpec(memory_space=pltpu.VMEM)]
        + [pl.BlockSpec((1, LAGS, rows, width), lambda s: (s, 0, 0, 0))] * len(parts),
        out_specs=pl.BlockSpec((1, rows, width * LAGS), lambda s: (s, 0, 0)),
        compiler_params=pltpu.CompilerParams(vmem_limit_bytes=VMEM),
    )(live, spread, *parts)


def shards(spectra, pairs, pair_count):
    blk, freqs = spectra.shape[0], spectra.shape[3]
    half = freqs // 2
    count = lax.axis_size("seg")
    me = lax.axis_index("src")
    seg = lax.axis_index("seg")
    side, row = me & 1, (me >> 1) & 1
    slots = pairs.shape[0]

    cosine, sine = lag_tables(freqs, LAGS)
    rows = jnp.array([0, 4, 5])
    table = jnp.concatenate([cosine[rows], sine[rows], cosine[rows][:2]], axis=0)
    table = lax.dynamic_slice_in_dim(table, side * half, half, 1)
    named = jnp.concatenate([pairs, to_pair(pairs)], axis=0) - (me & ~1)
    local = (named & ~1) + ((named & 1) ^ side)
    meta = jnp.concatenate([local.reshape(-1), seg[None]]).astype(jnp.int32)
    live = (jnp.arange(slots) < pair_count[0]).astype(jnp.int32)

    halves = spectra[:, 0].reshape(blk, 2, 2, half)
    mine = lax.dynamic_index_in_dim(halves, side, 2, keepdims=False).reshape(blk, 2 * half)
    theirs = lax.dynamic_index_in_dim(halves, 1 - side, 2, keepdims=False).reshape(blk, 2 * half)

    cuts = 4
    held = []
    for cut in range(cuts):
        span = slice(cut * blk // cuts, (cut + 1) * blk // cuts)
        own = mine[span]
        swapped = to_pair(theirs[span])
        above, above_swapped = to_below(own), to_below(swapped)
        beside = to_row(jnp.where(row == 1, own, above))
        beside_swapped = to_row(jnp.where(row == 1, swapped, above_swapped))
        held.append((own, swapped, beside, beside_swapped, above, above_swapped))
    held = [mine] + [jnp.concatenate([h[k] for h in held], axis=0) for k in range(1, WINDOW)]

    shares = correlate(meta, table, held, count, 2 * slots)
    parts = [shares[0]]
    for k in range(1, count):
        parts.append(lax.ppermute(shares[k], "seg", routes("seg", lambda i: (i + k) % count)))
    other = sum(p[slots:] for p in parts)
    own = [p[:slots] for p in parts] + [to_pair(other)]
    scale = float(count * spectra.shape[1] * freqs) ** (-0.5)
    return finish(live, own, scale)


def solution(mesh):
    in_specs = (P("src", "seg", None, None), P("src", None), P("src"))
    out_specs = P("src", "seg", None)
    return jax.shard_map(shards, mesh=mesh, in_specs=in_specs, out_specs=out_specs, check_vma=False)
```

time: 469 us -> 184 us (0.39)
  waiting for transfers between devices: 252 us -> 98.8 us
  local copies, waits for them, and re-layouts: 156 us -> 24.6 us
  starting transfers between devices: 5.16 us -> 26.8 us
  Pallas kernels: 0 us -> 17.9 us
  between operations: 16.6 us -> 0.98 us
  matrix products: 13.6 us -> 0 us
  other arithmetic: 23.4 us -> 15.1 us
    ppermute x4 -> x23, waiting for transfers between devices: 243 us -> 98.8 us  [the longest x8 44.6 us: to_below(): return lax.ppermute(value, 'src', routes('src', lambda d: d - REACH))]
    another operation x3 -> x1, local copies, waits for them, and re-layouts: 76.1 us -> 6.24 us  [shards(): halves = spectra[:, 0].reshape(blk, 2, 2, half)]
    convert_element_type x2 -> x0, local copies, waits for them, and re-layouts: 42 us -> none  [build_rotated(): return stacked.reshape(block.shape[0] * lags, -1).astype(jnp.bfloat16)]
    ppermute x4 -> x23, starting transfers between devices: 5.16 us -> 26.8 us  [the longest x8 10.3 us: to_below(): return lax.ppermute(value, 'src', routes('src', lambda d: d - REACH))]
    another operation x4 -> x0, other arithmetic: 20.5 us -> none  [the longest x3 16.8 us: build_rotated(): stacked = jnp.stack([first, second], axis=3)]
    pallas_call x0 -> x2, Pallas kernels: none -> 17.9 us  [the longest x1 13.1 us: correlate(): pl.pallas_call(functools.partial(corr_kernel, count), out_shape=[shape] *...]
    dot_general x2 -> x0, matrix products: 13.6 us -> none  [slot_product(): lax.dot_general(rotated, right, (((1,), (1,)), ((), ())), preferred_eleme...]
    reduce_scatter x1 -> x0, waiting for transfers between devices: 9.4 us -> none  [shards(): lax.psum_scatter(jnp.stack(results, axis=1), 'seg', scatter_dimension=0,...]
  transfers between devices with their start and end apart: 5 -> 23, of which waited for: 4 -> 14; matrix products, arithmetic and copies ran while one was open for 1% -> 10% of each run, Pallas kernels for 0% -> 0%
where the time goes in v1:
time: 184 us
  waiting for transfers between devices  98.8 us (54%)
  starting transfers between devices  26.8 us (15%)
  local copies, waits for them, and re-layouts  24.6 us (13%)
  Pallas kernels  17.9 us (10%)
  other arithmetic  15.1 us (8%)
    ppermute x8, waiting for transfers between devices, to_below(): return lax.ppermute(value, 'src', routes('src', lambda d: d - REACH))  44.6 us
    ppermute x6, waiting for transfers between devices, to_pair(): return lax.ppermute(value, 'src', routes('src', lambda d: d ^ 1))  37.9 us
    pallas_call x1, Pallas kernels, correlate(): pl.pallas_call(functools.partial(corr_kernel, count), out_shape=[shape] *...  13.1 us
    ppermute x8, waiting for transfers between devices, to_row(): return lax.ppermute(value, 'src', routes('src', lambda d: d ^ 2))  10.4 us
    ppermute x8, starting transfers between devices, to_below(): return lax.ppermute(value, 'src', routes('src', lambda d: d - REACH))  10.3 us
    ppermute x8, starting transfers between devices, to_row(): return lax.ppermute(value, 'src', routes('src', lambda d: d ^ 2))  9.51 us
    slice x1, local copies, waits for them, and re-layouts, shards(): swapped = to_pair(theirs[span])  7.31 us
    ppermute x6, starting transfers between devices, to_pair(): return lax.ppermute(value, 'src', routes('src', lambda d: d ^ 1))  6.97 us
  transfers between devices with their start and end apart: 23, of which 14 were waited for; matrix products, arithmetic and copies ran while one was open for 10% of the time, Pallas kernels for 0%

profile of v1, /device:TPU:0, one launch (start us, length us, event | category | flops | bytes accessed | tf_op | source)
XLA Modules:
  0.0 184.2 jit_solution(737733099438996024)
XLA Ops:
  0.0 6.2 %reshape_squeeze.3 = bf16[256,2,2,1024]{3,2,1,0:T(2,128)(2,1)S(1)} reshape(bf16[256,1,2,2048]{3,2,1,0:T(2,128)(2,1)} %param.4) | data formatting | bytes 4194304 | tf_op jit(solution)/shard_map/reshape;squeeze | solution.py:200
  6.2 7.3 %dynamic-slice_reduce_fusion.3 = (bf16[64,2,1024]{2,1,0:T(2,128)(2,1)S(1)}, bf16[64,2,1024]{2,1,0:T(2,128)(2,1)S(1)}, bf16[64,2,1024]{2,1,0:T(2,128)(2,1)S(1)}, bf16[64,2,1024]{2,1,0:T(2,128)(2,1)S(1)}) fusion(bf16[256,2,2,1024]{3,2,1,0:T(2,128)(2,1)S(1)} %reshape_squeeze.3, s32[]{:T(128)S(6)} %select_n.85, s32[]{:T(128)S(6)} %add.79, s32[]{:T(128)S(6)} %add.78, ...), kind=kLoop, calls=%fused_computation.13 | loop fusion | bytes 2097168 | tf_op jit(solution)/shard_map/slice | solution.py:209
  14.3 2.9 %collective-permute-start.1 = (bf16[64,2048]{1,0:T(8,128)(2,1)}, bf16[64,2048]{1,0:T(8,128)(2,1)S(1)}, u32[]{:S(2)}, u32[]{:S(2)}) collective-permute-start(bf16[64,2048]{1,0:T(8,128)(2,1)} %bitcast.7), channel_id=1, source_target_pairs={{0,2},{2,0},{4,6},{6,4},{8,10},{10,8},{12,14},{14,12},{16,18},{18,... | collective-permute-start | bytes 786440 | tf_op jit(solution)/shard_map/ppermute | solution.py:23
  18.8 2.0 %collective-permute-start.3 = (bf16[64,2048]{1,0:T(8,128)(2,1)}, bf16[64,2048]{1,0:T(8,128)(2,1)S(1)}, u32[]{:S(2)}, u32[]{:S(2)}) collective-permute-start(bf16[64,2048]{1,0:T(8,128)(2,1)} %bitcast.11), channel_id=1, source_target_pairs={{0,2},{2,0},{4,6},{6,4},{8,10},{10,8},{12,14},{14,12},{16,18},{18,... | collective-permute-start | bytes 786440 | tf_op jit(solution)/shard_map/ppermute | solution.py:23
  20.8 2.2 %constant_dynamic-slice_fusion = bf16[256,2,1,1024]{3,2,1,0:T(2,128)(2,1)S(1)} fusion(bf16[256,2,2,1024]{3,2,1,0:T(2,128)(2,1)S(1)} %reshape_squeeze.3, s32[]{:T(128)S(6)} %select_n.84), kind=kLoop, calls=%fused_computation.53 | loop fusion | bytes 2097156 | tf_op jit(solution)/shard_map/jit(dynamic_index_in_dim)/dynamic_slice | solution.py:201
  25.0 1.3 collective-permute-start.9
  30.9 4.2 %collective-permute-done = s32[2,2]{1,0:T(2,128)S(1)} collective-permute-done((s32[2,2]{1,0:T(2,128)S(1)}, s32[2,2]{1,0:T(2,128)S(1)}, u32[]{:S(2)}, u32[]{:S(2)}) %collective-permute-start) | collective-permute-done | bytes 48 | tf_op jit(solution)/shard_map/ppermute | solution.py:23
  35.1 1.7 collective-permute-start.4
  37.5 1.3 collective-permute-start.11
  39.8 6.5 %collective-permute-done.11 = bf16[64,2048]{1,0:T(8,128)(2,1)S(1)} collective-permute-done((bf16[64,2048]{1,0:T(8,128)(2,1)S(1)}, bf16[64,2048]{1,0:T(8,128)(2,1)S(1)}, u32[]{:S(2)}, u32[]{:S(2)}) %collective-permute-start.11) | collective-permute-done | bytes 262176 | tf_op jit(solution)/shard_map/ppermute | solution.py:31
  46.2 1.3 collective-permute-start.5
  47.6 6.9 %collective-permute-done.5 = bf16[64,2048]{1,0:T(8,128)(2,1)S(1)} collective-permute-done((bf16[64,2048]{1,0:T(8,128)(2,1)S(1)}, bf16[64,2048]{1,0:T(8,128)(2,1)S(1)}, u32[]{:S(2)}, u32[]{:S(2)}) %collective-permute-start.5) | collective-permute-done | bytes 262176 | tf_op jit(solution)/shard_map/ppermute | solution.py:31
  55.8 1.6 collective-permute-start.10
  57.4 5.4 %collective-permute-done.7 = bf16[64,2048]{1,0:T(8,128)(2,1)S(1)} collective-permute-done((bf16[64,2048]{1,0:T(8,128)(2,1)S(1)}, bf16[64,2048]{1,0:T(8,128)(2,1)S(1)}, u32[]{:S(2)}, u32[]{:S(2)}) %collective-permute-start.7) | collective-permute-done | bytes 262176 | tf_op jit(solution)/shard_map/ppermute | solution.py:31
  64.1 2.0 %pad_maximum_fusion.3.refs_4_ = bf16[256,2048]{1,0:T(8,128)(2,1)} fusion(bf16[64,2048]{1,0:T(8,128)(2,1)S(1)} %collective-permute-done.11, bf16[64,2048]{1,0:T(8,128)(2,1)} %collective-permute-done.9, bf16[64,2048]{1,0:T(8,128)(2,1)S(1)} %collective-permute-done.7, bf16[64,2048]{1,0:T(8,128)(2,1)S(1)} %collective-permute-done.5), kind=kLoop, calls=%fused_computation.8 | loop fusion | flops 4194304 | bytes 2097152 | tf_op jit(solution)/shard_map/concatenate | solution.py:214
  66.1 1.5 collective-permute-start.12
  68.2 1.5 collective-permute-start.8
  72.9 8.2 %collective-permute-done.15 = bf16[64,2048]{1,0:T(8,128)(2,1)S(1)} collective-permute-done((bf16[64,2048]{1,0:T(8,128)(2,1)S(1)}, bf16[64,2048]{1,0:T(8,128)(2,1)S(1)}, u32[]{:S(2)}, u32[]{:S(2)}) %collective-permute-start.15) | collective-permute-done | bytes 262176 | tf_op jit(solution)/shard_map/ppermute | solution.py:31
  82.4 9.8 %collective-permute-done.17 = bf16[64,2048]{1,0:T(8,128)(2,1)S(1)} collective-permute-done((bf16[64,2048]{1,0:T(8,128)(2,1)S(1)}, bf16[64,2048]{1,0:T(8,128)(2,1)S(1)}, u32[]{:S(2)}, u32[]{:S(2)}) %collective-permute-start.17) | collective-permute-done | bytes 262176 | tf_op jit(solution)/shard_map/ppermute | solution.py:31
  93.6 7.1 %collective-permute-done.19 = bf16[64,2048]{1,0:T(8,128)(2,1)S(1)} collective-permute-done((bf16[64,2048]{1,0:T(8,128)(2,1)S(1)}, bf16[64,2048]{1,0:T(8,128)(2,1)S(1)}, u32[]{:S(2)}, u32[]{:S(2)}) %collective-permute-start.19) | collective-permute-done | bytes 262176 | tf_op jit(solution)/shard_map/ppermute | solution.py:31
  100.7 2.2 %collective-permute-start.14 = (bf16[64,2048]{1,0:T(8,128)(2,1)S(1)}, bf16[64,2048]{1,0:T(8,128)(2,1)S(1)}, u32[]{:S(2)}, u32[]{:S(2)}) collective-permute-start(bf16[64,2048]{1,0:T(8,128)(2,1)S(1)} %broadcast_select_fusion.3), channel_id=1, source_target_pairs={{0,4},{2,6},{4,0},{6,2},{8,12},{10,14},{12,8},{14,10},{16,20},{18,... | collective-permute-start | bytes 786440 | tf_op jit(solution)/shard_map/ppermute | solution.py:27
  103.0 2.0 %collective-permute-start.18 = (bf16[64,2048]{1,0:T(8,128)(2,1)S(1)}, bf16[64,2048]{1,0:T(8,128)(2,1)S(1)}, u32[]{:S(2)}, u32[]{:S(2)}) collective-permute-start(bf16[64,2048]{1,0:T(8,128)(2,1)S(1)} %broadcast_select_fusion.1), channel_id=1, source_target_pairs={{0,4},{2,6},{4,0},{6,2},{8,12},{10,14},{12,8},{14,10},{16,20},{18,... | collective-permute-start | bytes 786440 | tf_op jit(solution)/shard_map/ppermute | solution.py:27
  107.4 2.0 %collective-permute-done.14 = bf16[64,2048]{1,0:T(8,128)(2,1)S(1)} collective-permute-done((bf16[64,2048]{1,0:T(8,128)(2,1)S(1)}, bf16[64,2048]{1,0:T(8,128)(2,1)S(1)}, u32[]{:S(2)}, u32[]{:S(2)}) %collective-permute-start.14) | collective-permute-done | bytes 262176 | tf_op jit(solution)/shard_map/ppermute | solution.py:27
  109.3 2.8 %collective-permute-done.16 = bf16[64,2048]{1,0:T(8,128)(2,1)S(1)} collective-permute-done((bf16[64,2048]{1,0:T(8,128)(2,1)S(1)}, bf16[64,2048]{1,0:T(8,128)(2,1)S(1)}, u32[]{:S(2)}, u32[]{:S(2)}) %collective-permute-start.16) | collective-permute-done | bytes 262176 | tf_op jit(solution)/shard_map/ppermute | solution.py:27
  112.1 2.8 %collective-permute-done.18 = bf16[64,2048]{1,0:T(8,128)(2,1)S(1)} collective-permute-done((bf16[64,2048]{1,0:T(8,128)(2,1)S(1)}, bf16[64,2048]{1,0:T(8,128)(2,1)S(1)}, u32[]{:S(2)}, u32[]{:S(2)}) %collective-permute-start.18) | collective-permute-done | bytes 262176 | tf_op jit(solution)/shard_map/ppermute | solution.py:27
  114.9 2.8 %collective-permute-done.20 = bf16[64,2048]{1,0:T(8,128)(2,1)S(1)} collective-permute-done((bf16[64,2048]{1,0:T(8,128)(2,1)S(1)}, bf16[64,2048]{1,0:T(8,128)(2,1)S(1)}, u32[]{:S(2)}, u32[]{:S(2)}) %collective-permute-start.20) | collective-permute-done | bytes 262176 | tf_op jit(solution)/shard_map/ppermute | solution.py:27
  118.8 13.1 %shard_map.46 = (f32[4,6,128,256]{3,2,1,0:T(8,128)}, f32[4,6,128,256]{3,2,1,0:T(8,128)}) custom-call(s32[9]{0:T(128)} %pad_add_fusion.meta, f32[8,1024]{1,0:T(8,128)} %fusion.8.table, bf16[256,2048]{1,0:T(8,128)(2,1)} %bitcast.32, bf16[256,2048]{1,0:T(8,128)(2,1)} %pad_maximum_fusion.refs_1_, bf16[256,2048]{1,0:T(8,128)(2,1)} %pad_maximum_fusion.1.refs_2_, ...), custom_call_target="tpu_custom_call" | custom-call | flops 6442450944 | bytes 8388608 | tf_op jit(solution)/shard_map/pallas_call | solution.py:121
  132.0 5.9 %collective-permute-done.21 = f32[4,6,128,256]{3,2,1,0:T(8,128)S(1)} collective-permute-done((f32[4,6,128,256]{3,2,1,0:T(8,128)}, f32[4,6,128,256]{3,2,1,0:T(8,128)S(1)}, u32[]{:S(2)}, u32[]{:S(2)}) %collective-permute-start.21) | collective-permute-done | bytes 3145760 | tf_op jit(solution)/shard_map/ppermute | solution.py:219
  137.9 4.0 %slice_add_fusion = (f32[2,6,128,256]{3,2,1,0:T(8,128)S(1)}, f32[2,6,128,256]{3,2,1,0:T(8,128)}, f32[2,6,128,256]{3,2,1,0:T(8,128)}) fusion(f32[4,6,128,256]{3,2,1,0:T(8,128)S(1)} %collective-permute-done.21, f32[4,6,128,256]{3,2,1,0:T(8,128)} %get-tuple-element.7), kind=kLoop, calls=%fused_computation.4 | loop fusion | flops 393216 | bytes 11010048 | tf_op jit(solution)/shard_map/add | solution.py:220
  143.3 1.3 fusion.spread
  144.6 33.7 %collective-permute-done.22.refs_2_ = f32[2,6,128,256]{3,2,1,0:T(8,128)S(1)} collective-permute-done((f32[2,6,128,256]{3,2,1,0:T(8,128)S(1)}, f32[2,6,128,256]{3,2,1,0:T(8,128)S(1)}, u32[]{:S(2)}, u32[]{:S(2)}) %collective-permute-start.22) | collective-permute-done | bytes 1572896 | tf_op jit(solution)/shard_map/ppermute | solution.py:23
  179.4 4.8 %shard_map.47 = f32[2,128,1536]{2,1,0:T(8,128)} custom-call(s32[2]{0:T(128)} %compare_convert_fusion.live, bf16[768,768]{1,0:T(8,128)(2,1)} %fusion.spread, f32[2,6,128,256]{3,2,1,0:T(8,128)} %get-tuple-element.14.refs_0_, f32[2,6,128,256]{3,2,1,0:T(8,128)} %get-tuple-element.15.refs_1_, f32[2,6,128,256]{3,2,1,0:T(8,128)} %copy-done), custom_call_target="tpu_custom_call" | custom-call | tf_op jit(solution)/shard_map/pallas_call | solution.py:171
  (65 shorter events, 24.9 us)
Async XLA Ops:
  14.3 41.5 %collective-permute-start.1 = (bf16[64,2048]{1,0:T(8,128)(2,1)}, bf16[64,2048]{1,0:T(8,128)(2,1)S(1)}, u32[]{:S(2)}, u32[]{:S(2)}) collective-permute-start(bf16[64,2048]{1,0:T(8,128)(2,1)} %bitcast.7), channel_id=1, source_target_pairs={{0,2},{2,0},{4,6},{6,4},{8,10},{10,8},{12,14},{14,12},{16,18},{18,... | collective-permute-start | bytes 786440 | tf_op jit(solution)/shard_map/ppermute | solution.py:23
  18.0 48.1 %collective-permute-start.2 = (bf16[64,2048]{1,0:T(8,128)(2,1)}, bf16[64,2048]{1,0:T(8,128)(2,1)S(1)}, u32[]{:S(2)}, u32[]{:S(2)}) collective-permute-start(bf16[64,2048]{1,0:T(8,128)(2,1)} %bitcast.9), channel_id=1, source_target_pairs={{0,2},{2,0},{4,6},{6,4},{8,10},{10,8},{12,14},{14,12},{16,18},{18,... | collective-permute-start | bytes 786440 | tf_op jit(solution)/shard_map/ppermute | solution.py:23
  18.8 48.9 %collective-permute-start.3 = (bf16[64,2048]{1,0:T(8,128)(2,1)}, bf16[64,2048]{1,0:T(8,128)(2,1)S(1)}, u32[]{:S(2)}, u32[]{:S(2)}) collective-permute-start(bf16[64,2048]{1,0:T(8,128)(2,1)} %bitcast.11), channel_id=1, source_target_pairs={{0,2},{2,0},{4,6},{6,4},{8,10},{10,8},{12,14},{14,12},{16,18},{18,... | collective-permute-start | bytes 786440 | tf_op jit(solution)/shard_map/ppermute | solution.py:23
  24.0 2.3 %copy-start.2 = (s32[2,2]{1,0:T(2,128)S(1)}, s32[2,2]{1,0:T(2,128)}, u32[]{:S(2)}) copy-start(s32[2,2]{1,0:T(2,128)} %param.5) | copy-start | bytes 52
  24.1 2.7 %copy-start.3 = (s32[3]{0:T(128)S(1)}, s32[3]{0:T(128)}, u32[]{:S(2)}) copy-start(s32[3]{0:T(128)} %constant.91) | copy-start | bytes 40
  25.0 12.5 %collective-permute-start.9 = (bf16[64,2048]{1,0:T(8,128)(2,1)S(1)}, bf16[64,2048]{1,0:T(8,128)(2,1)}, u32[]{:S(2)}, u32[]{:S(2)}) collective-permute-start(bf16[64,2048]{1,0:T(8,128)(2,1)S(1)} %bitcast.33), channel_id=1, source_target_pairs={{8,0},{10,2},{12,4},{14,6},{16,8},{18,10},{20,12},{22,14},{24,16},... | collective-permute-start | bytes 786440 | tf_op jit(solution)/shard_map/ppermute | solution.py:31
  26.3 8.7 %collective-permute-start = (s32[2,2]{1,0:T(2,128)S(1)}, s32[2,2]{1,0:T(2,128)S(1)}, u32[]{:S(2)}, u32[]{:S(2)}) collective-permute-start(s32[2,2]{1,0:T(2,128)S(1)} %copy-done.2), channel_id=1, source_target_pairs={{0,2},{2,0},{4,6},{6,4},{8,10},{10,8},{12,14},{14,12},{16,18},{18,... | collective-permute-start | bytes 56 | tf_op jit(solution)/shard_map/ppermute | solution.py:23
  29.6 5.5 %copy-start.1 = (bf16[8,8,2,1024]{3,1,2,0:T(8,128)(2,1)S(1)}, bf16[8,8,2,1024]{3,1,2,0:T(8,128)(2,1)}, u32[]{:S(2)}) copy-start(bf16[8,8,2,1024]{3,1,2,0:T(8,128)(2,1)} %copy.19) | copy-start | bytes 786436
  35.1 33.1 %collective-permute-start.4 = (bf16[64,2048]{1,0:T(8,128)(2,1)S(1)}, bf16[64,2048]{1,0:T(8,128)(2,1)S(1)}, u32[]{:S(2)}, u32[]{:S(2)}) collective-permute-start(bf16[64,2048]{1,0:T(8,128)(2,1)S(1)} %bitcast.49), channel_id=1, source_target_pairs={{0,2},{2,0},{4,6},{6,4},{8,10},{10,8},{12,14},{14,12},{16,18},{18,... | collective-permute-start | bytes 786440 | tf_op jit(solution)/shard_map/ppermute | solution.py:23
  37.5 8.7 %collective-permute-start.11 = (bf16[64,2048]{1,0:T(8,128)(2,1)S(1)}, bf16[64,2048]{1,0:T(8,128)(2,1)S(1)}, u32[]{:S(2)}, u32[]{:S(2)}) collective-permute-start(bf16[64,2048]{1,0:T(8,128)(2,1)S(1)} %bitcast.39), channel_id=1, source_target_pairs={{8,0},{10,2},{12,4},{14,6},{16,8},{18,10},{20,12},{22,14},{24,16},... | collective-permute-start | bytes 786440 | tf_op jit(solution)/shard_map/ppermute | solution.py:31
  46.2 8.3 %collective-permute-start.5 = (bf16[64,2048]{1,0:T(8,128)(2,1)S(1)}, bf16[64,2048]{1,0:T(8,128)(2,1)S(1)}, u32[]{:S(2)}, u32[]{:S(2)}) collective-permute-start(bf16[64,2048]{1,0:T(8,128)(2,1)S(1)} %bitcast.37), channel_id=1, source_target_pairs={{8,0},{10,2},{12,4},{14,6},{16,8},{18,10},{20,12},{22,14},{24,16},... | collective-permute-start | bytes 786440 | tf_op jit(solution)/shard_map/ppermute | solution.py:31
  54.5 8.3 %collective-permute-start.7 = (bf16[64,2048]{1,0:T(8,128)(2,1)S(1)}, bf16[64,2048]{1,0:T(8,128)(2,1)S(1)}, u32[]{:S(2)}, u32[]{:S(2)}) collective-permute-start(bf16[64,2048]{1,0:T(8,128)(2,1)S(1)} %bitcast.35), channel_id=1, source_target_pairs={{8,0},{10,2},{12,4},{14,6},{16,8},{18,10},{20,12},{22,14},{24,16},... | collective-permute-start | bytes 786440 | tf_op jit(solution)/shard_map/ppermute | solution.py:31
  55.8 47.1 %collective-permute-start.10 = (bf16[64,2048]{1,0:T(8,128)(2,1)S(1)}, bf16[64,2048]{1,0:T(8,128)(2,1)S(1)}, u32[]{:S(2)}, u32[]{:S(2)}) collective-permute-start(bf16[64,2048]{1,0:T(8,128)(2,1)S(1)} %broadcast_select_fusion.5), channel_id=1, source_target_pairs={{0,4},{2,6},{4,0},{6,2},{8,12},{10,14},{12,8},{14,10},{16,20},{18,... | collective-permute-start | bytes 786440 | tf_op jit(solution)/shard_map/ppermute | solution.py:27
  62.8 8.7 %collective-permute-start.13 = (bf16[64,2048]{1,0:T(8,128)(2,1)S(1)}, bf16[64,2048]{1,0:T(8,128)(2,1)S(1)}, u32[]{:S(2)}, u32[]{:S(2)}) collective-permute-start(bf16[64,2048]{1,0:T(8,128)(2,1)S(1)} %collective-permute-done.1), channel_id=1, source_target_pairs={{8,0},{10,2},{12,4},{14,6},{16,8},{18,10},{20,12},{22,14},{24,16},... | collective-permute-start | bytes 786440 | tf_op jit(solution)/shard_map/ppermute | solution.py:31
  66.1 36.9 %collective-permute-start.12 = (bf16[64,2048]{1,0:T(8,128)(2,1)S(1)}, bf16[64,2048]{1,0:T(8,128)(2,1)S(1)}, u32[]{:S(2)}, u32[]{:S(2)}) collective-permute-start(bf16[64,2048]{1,0:T(8,128)(2,1)S(1)} %broadcast_select_fusion.4), channel_id=1, source_target_pairs={{0,4},{2,6},{4,0},{6,2},{8,12},{10,14},{12,8},{14,10},{16,20},{18,... | collective-permute-start | bytes 786440 | tf_op jit(solution)/shard_map/ppermute | solution.py:27
  67.6 37.4 %collective-permute-start.6 = (bf16[64,2048]{1,0:T(8,128)(2,1)S(1)}, bf16[64,2048]{1,0:T(8,128)(2,1)S(1)}, u32[]{:S(2)}, u32[]{:S(2)}) collective-permute-start(bf16[64,2048]{1,0:T(8,128)(2,1)S(1)} %broadcast_select_fusion.7), channel_id=1, source_target_pairs={{0,4},{2,6},{4,0},{6,2},{8,12},{10,14},{12,8},{14,10},{16,20},{18,... | collective-permute-start | bytes 786440 | tf_op jit(solution)/shard_map/ppermute | solution.py:27
  68.2 38.1 %collective-permute-start.8 = (bf16[64,2048]{1,0:T(8,128)(2,1)S(1)}, bf16[64,2048]{1,0:T(8,128)(2,1)S(1)}, u32[]{:S(2)}, u32[]{:S(2)}) collective-permute-start(bf16[64,2048]{1,0:T(8,128)(2,1)S(1)} %broadcast_select_fusion.6), channel_id=1, source_target_pairs={{0,4},{2,6},{4,0},{6,2},{8,12},{10,14},{12,8},{14,10},{16,20},{18,... | collective-permute-start | bytes 786440 | tf_op jit(solution)/shard_map/ppermute | solution.py:27
  71.5 9.5 %collective-permute-start.15 = (bf16[64,2048]{1,0:T(8,128)(2,1)S(1)}, bf16[64,2048]{1,0:T(8,128)(2,1)S(1)}, u32[]{:S(2)}, u32[]{:S(2)}) collective-permute-start(bf16[64,2048]{1,0:T(8,128)(2,1)S(1)} %collective-permute-done.2), channel_id=1, source_target_pairs={{8,0},{10,2},{12,4},{14,6},{16,8},{18,10},{20,12},{22,14},{24,16},... | collective-permute-start | bytes 786440 | tf_op jit(solution)/shard_map/ppermute | solution.py:31
  81.1 11.2 %collective-permute-start.17 = (bf16[64,2048]{1,0:T(8,128)(2,1)S(1)}, bf16[64,2048]{1,0:T(8,128)(2,1)S(1)}, u32[]{:S(2)}, u32[]{:S(2)}) collective-permute-start(bf16[64,2048]{1,0:T(8,128)(2,1)S(1)} %collective-permute-done.3), channel_id=1, source_target_pairs={{8,0},{10,2},{12,4},{14,6},{16,8},{18,10},{20,12},{22,14},{24,16},... | collective-permute-start | bytes 786440 | tf_op jit(solution)/shard_map/ppermute | solution.py:31
  92.2 8.5 %collective-permute-start.19 = (bf16[64,2048]{1,0:T(8,128)(2,1)S(1)}, bf16[64,2048]{1,0:T(8,128)(2,1)S(1)}, u32[]{:S(2)}, u32[]{:S(2)}) collective-permute-start(bf16[64,2048]{1,0:T(8,128)(2,1)S(1)} %collective-permute-done.4), channel_id=1, source_target_pairs={{8,0},{10,2},{12,4},{14,6},{16,8},{18,10},{20,12},{22,14},{24,16},... | collective-permute-start | bytes 786440 | tf_op jit(solution)/shard_map/ppermute | solution.py:31
  100.7 8.6 %collective-permute-start.14 = (bf16[64,2048]{1,0:T(8,128)(2,1)S(1)}, bf16[64,2048]{1,0:T(8,128)(2,1)S(1)}, u32[]{:S(2)}, u32[]{:S(2)}) collective-permute-start(bf16[64,2048]{1,0:T(8,128)(2,1)S(1)} %broadcast_select_fusion.3), channel_id=1, source_target_pairs={{0,4},{2,6},{4,0},{6,2},{8,12},{10,14},{12,8},{14,10},{16,20},{18,... | collective-permute-start | bytes 786440 | tf_op jit(solution)/shard_map/ppermute | solution.py:27
  102.9 9.2 %collective-permute-start.16 = (bf16[64,2048]{1,0:T(8,128)(2,1)S(1)}, bf16[64,2048]{1,0:T(8,128)(2,1)S(1)}, u32[]{:S(2)}, u32[]{:S(2)}) collective-permute-start(bf16[64,2048]{1,0:T(8,128)(2,1)S(1)} %broadcast_select_fusion.2), channel_id=1, source_target_pairs={{0,4},{2,6},{4,0},{6,2},{8,12},{10,14},{12,8},{14,10},{16,20},{18,... | collective-permute-start | bytes 786440 | tf_op jit(solution)/shard_map/ppermute | solution.py:27
  103.0 11.9 %collective-permute-start.18 = (bf16[64,2048]{1,0:T(8,128)(2,1)S(1)}, bf16[64,2048]{1,0:T(8,128)(2,1)S(1)}, u32[]{:S(2)}, u32[]{:S(2)}) collective-permute-start(bf16[64,2048]{1,0:T(8,128)(2,1)S(1)} %broadcast_select_fusion.1), channel_id=1, source_target_pairs={{0,4},{2,6},{4,0},{6,2},{8,12},{10,14},{12,8},{14,10},{16,20},{18,... | collective-permute-start | bytes 786440 | tf_op jit(solution)/shard_map/ppermute | solution.py:27
  105.0 12.7 %collective-permute-start.20 = (bf16[64,2048]{1,0:T(8,128)(2,1)S(1)}, bf16[64,2048]{1,0:T(8,128)(2,1)S(1)}, u32[]{:S(2)}, u32[]{:S(2)}) collective-permute-start(bf16[64,2048]{1,0:T(8,128)(2,1)S(1)} %broadcast_select_fusion), channel_id=1, source_target_pairs={{0,4},{2,6},{4,0},{6,2},{8,12},{10,14},{12,8},{14,10},{16,20},{18,... | collective-permute-start | bytes 786440 | tf_op jit(solution)/shard_map/ppermute | solution.py:27
  131.9 5.9 %collective-permute-start.21 = (f32[4,6,128,256]{3,2,1,0:T(8,128)}, f32[4,6,128,256]{3,2,1,0:T(8,128)S(1)}, u32[]{:S(2)}, u32[]{:S(2)}) collective-permute-start(f32[4,6,128,256]{3,2,1,0:T(8,128)} %get-tuple-element.8), channel_id=1, source_target_pairs={{0,1},{1,0},{2,3},{3,2},{4,5},{5,4},{6,7},{7,6},{8,9},{9,8},{10,11... | collective-permute-start | bytes 9437192 | tf_op jit(solution)/shard_map/ppermute | solution.py:219
  141.8 36.4 %collective-permute-start.22 = (f32[2,6,128,256]{3,2,1,0:T(8,128)S(1)}, f32[2,6,128,256]{3,2,1,0:T(8,128)S(1)}, u32[]{:S(2)}, u32[]{:S(2)}) collective-permute-start(f32[2,6,128,256]{3,2,1,0:T(8,128)S(1)} %get-tuple-element.13), channel_id=1, source_target_pairs={{0,2},{2,0},{4,6},{6,4},{8,10},{10,8},{12,14},{14,12},{16,18},{18,... | collective-permute-start | bytes 4718600 | tf_op jit(solution)/shard_map/ppermute | solution.py:23
  178.3 1.2 copy-start

commit v2 on v0

v2 whole, which is shorter than its diff:
```python
import functools

import jax
import jax.numpy as jnp
from jax import lax
from jax.experimental import pallas as pl
from jax.experimental.pallas import tpu as pltpu
from jax.sharding import PartitionSpec as P

LAGS = 6
REACH = 4
SLOTS = 2
WINDOW = 6
LANES = 128
VMEM = 56 * 1024 * 1024


def routes(axis, move):
    size = lax.axis_size(axis)
    return [(i, move(i)) for i in range(size) if 0 <= move(i) < size]


def to_pair(value):
    return lax.ppermute(value, "src", routes("src", lambda d: d ^ 1))


def to_row(value):
    return lax.ppermute(value, "src", routes("src", lambda d: d ^ 2))


def to_site(value):
    size = lax.axis_size("src")
    return lax.ppermute(value, "src", routes("src", lambda d: (d + REACH) % size if d >> 1 & 1 else d - REACH))


def to_partner_site(value):
    size = lax.axis_size("src")
    return lax.ppermute(value, "src", routes("src", lambda d: ((d + REACH) % size if d >> 1 & 1 else d) ^ 1))


def to_owner(value):
    size = lax.axis_size("src")
    return lax.ppermute(value, "src", routes("src", lambda d: (d - REACH) % size if d >> 1 & 1 else -1))


def lag_tables(freqs, lags):
    freq = jnp.arange(freqs, dtype=jnp.int32)
    lagval = jnp.arange(lags, dtype=jnp.int32) - lags // 2
    phase = lagval[:, None] * freq[None, :] % (2 * freqs)
    theta = phase.astype(jnp.float32) * (jnp.pi / freqs)
    return (jnp.cos(theta), jnp.sin(theta))


def rotate_into(x_ref, real, imag, table, rows, row, cols, half):
    height = real.shape[0]
    other = pl.ds(half + cols, real.shape[1])
    here = pl.ds(cols, real.shape[1])

    def put(lag, first, second):
        at = pl.ds(lag * rows + row, height)
        x_ref[at, here] = first.astype(jnp.bfloat16)
        x_ref[at, other] = second.astype(jnp.bfloat16)

    put(3, real, imag)
    for plus, minus, row_c in ((0, None, 0), (4, 2, 1), (5, 1, 2)):
        cos, sin = table(row_c), table(row_c + 3)
        rc, im_s, ic, rs = real * cos, imag * sin, imag * cos, real * sin
        put(plus, rc - im_s, ic + rs)
        if minus is not None:
            put(minus, rc + im_s, ic - rs)


def stage_tiles(stage):
    return [(a, stage) for a in range(stage)] + [(stage, b) for b in range(stage + 1)]


def corr_kernel(count, stage, first, sets, layout, meta, table, *refs):
    parts = stage + 1
    arrays = 1 + max(item[0] for items in layout for item in items)
    blocks, outs = refs[:arrays], refs[arrays:-4]
    left, right, x_ref, sems = refs[-4:]
    at = pl.program_id(0)
    now = lax.rem(at, 2)
    half = left.shape[3]
    size = left.shape[2] // parts
    piece = size // count

    def copy(item, buffer, p, side):
        ref, source, start, rows = item
        span = pl.ds(start, rows)
        target = left.at[buffer, p, span] if side == 0 else right.at[buffer, span, pl.ds(p * half, half)]
        return pltpu.make_async_copy(blocks[ref].at[p, pl.ds(source, rows)], target, sems.at[side, buffer])

    def fetch(which, buffer):
        for side in range(2):
            name = meta[2 * (first + which) + side]
            for k, items in enumerate(layout):

                @pl.when(name == k)
                def _():
                    for item in items:
                        for p in range(2):
                            copy(item, buffer, p, side).start()

    @pl.when(at == 0)
    def _():
        fetch(0, 0)

    @pl.when(at + 1 < pl.num_programs(0))
    def _():
        fetch(at + 1, 1 - now)

    for side in range(2):
        target = left.at[now] if side == 0 else right.at[now]
        pltpu.make_async_copy(target, target, sems.at[side, now]).wait()

    wide, high = 256, 16
    for c in range(parts):
        for k in range(count):
            base = c * size + lax.rem(meta[8] + k, count) * piece
            block = (c * count + k) * LAGS * piece
            for cols in range(0, half, wide):
                for step in range(0, piece, high):
                    src = pl.ds(pl.multiple_of(base + step, high), high)
                    real = left[now, 0, src, pl.ds(cols, wide)].astype(jnp.float32)
                    imag = left[now, 1, src, pl.ds(cols, wide)].astype(jnp.float32)
                    look = lambda r: table[pl.ds(r, 1), pl.ds(cols, wide)]
                    rotate_into(x_ref, real, imag, look, piece, block + step, cols, half)
    product = lax.dot_general(
        x_ref[...], right[now], (((1,), (1,)), ((), ())), preferred_element_type=jnp.float32
    )
    for n, tiles in enumerate(sets):

        @pl.when(at // SLOTS == n)
        def _():
            for k in range(count):
                for tile, (a, b) in enumerate(tiles):
                    block = (a * count + k) * LAGS * piece
                    out = product[block : block + LAGS * piece, b * size : (b + 1) * size]
                    outs[n * count + k][0, :, tile * piece : (tile + 1) * piece] = out.reshape(LAGS, piece, size)


def correlate(meta, table, sources, count, stage, width, first, sets):
    size, half, parts = width, sources[0][0][0].shape[2], stage + 1
    piece = size // count
    layout, blocks = [], []
    for spans in sources:
        items, start = [], 0
        for array, source, rows in spans:
            rows = min(rows, parts * size - start)
            if rows > 0:
                if not any(array is block for block in blocks):
                    blocks.append(array)
                at = [array is block for block in blocks].index(True)
                items.append((at, source, start, rows))
                start += rows
        layout.append(tuple(items))
    shapes = [(SLOTS, LAGS, len(tiles) * piece, size) for tiles in sets for _ in range(count)]
    outs = pl.pallas_call(
        functools.partial(corr_kernel, count, stage, first, sets, tuple(layout)),
        out_shape=[jax.ShapeDtypeStruct(shape, jnp.float32) for shape in shapes],
        grid=(SLOTS * len(sets),),
        in_specs=[pl.BlockSpec(memory_space=pltpu.SMEM), pl.BlockSpec(memory_space=pltpu.VMEM)]
        + [pl.BlockSpec(memory_space=pl.ANY)] * len(blocks),
        out_specs=[
            pl.BlockSpec((1,) + shape[1:], lambda s, n=n // count: (jnp.clip(s - n * SLOTS, 0, SLOTS - 1), 0, 0, 0))
            for n, shape in enumerate(shapes)
        ],
        scratch_shapes=[
            pltpu.VMEM((2, 2, parts * size, half), jnp.bfloat16),
            pltpu.VMEM((2, parts * size, 2 * half), jnp.bfloat16),
            pltpu.VMEM((parts * LAGS * size, 2 * half), jnp.bfloat16),
            pltpu.SemaphoreType.DMA((2, 2)),
        ],
        compiler_params=pltpu.CompilerParams(vmem_limit_bytes=VMEM),
        cost_estimate=pl.CostEstimate(flops=10**13, bytes_accessed=10**10, transcendentals=0),
    )(meta, table, *blocks)
    return [outs[n * count : (n + 1) * count] for n in range(len(sets))]


def finish_kernel(count, piece, stages, slot, scale, layout, meta, spread, *refs):
    out = refs[-1]
    away = meta[0] > 0

    def find(stage, lag, at):
        ref, first = layout[stage][lag]
        return jnp.where(away, refs[2 * ref + 1][0, lag - first, at], refs[2 * ref][0, lag - first, at])

    tiles = [(stage, t, a, b) for stage in range(stages) for t, (a, b) in enumerate(stage_tiles(stage))]
    high, low = [], []
    for stage, t, _, _ in tiles:
        at = slice(t * piece, (t + 1) * piece)
        total = jnp.concatenate([find(stage, lag, at) for lag in range(LAGS)], axis=1)
        top = total.astype(jnp.bfloat16)
        high.append(top)
        low.append((total - top.astype(jnp.float32)).astype(jnp.bfloat16))
    moved = jnp.dot(jnp.concatenate(high + low, axis=0), spread[...], preferred_element_type=jnp.float32)
    keep = slot < meta[1]
    run = piece * LAGS
    for n, (_, _, a, b) in enumerate(tiles):
        m = n + len(tiles)
        both = (moved[n * piece : (n + 1) * piece] + moved[m * piece : (m + 1) * piece]) * scale
        both = jnp.where(keep, both, jnp.zeros_like(both))
        for seg in range(count):
            col = (seg * stages + b) * run
            out[0, a * piece : (a + 1) * piece, col : col + run] = both[:, seg * run : (seg + 1) * run]


def finish(meta, spread, stacks, slot, count, piece, scale, result):
    layout, arrays = [], []
    for pieces in stacks:
        where = []
        for first, here, back in pieces:
            where += [(len(arrays) // 2, first)] * here.shape[1]
            arrays += [here, back]
        layout.append(tuple(where))
    stages = len(stacks)
    shape = (SLOTS, stages * piece, stages * piece * count * LAGS)
    specs = [pl.BlockSpec((1,) + x.shape[1:], lambda i, at=min(slot, x.shape[0] - 1): (at, 0, 0, 0)) for x in arrays]
    more = [] if result is None else [result]
    return pl.pallas_call(
        functools.partial(finish_kernel, count, piece, stages, slot, scale, tuple(layout)),
        out_shape=jax.ShapeDtypeStruct(shape, jnp.float32),
        grid=(1,),
        in_specs=[pl.BlockSpec(memory_space=pltpu.SMEM), pl.BlockSpec(memory_space=pltpu.VMEM)]
        + specs
        + [pl.BlockSpec(memory_space=pl.ANY)] * len(more),
        out_specs=pl.BlockSpec((1,) + shape[1:], lambda i: (slot, 0, 0)),
        input_output_aliases={2 + len(arrays): 0} if more else {},
        compiler_params=pltpu.CompilerParams(vmem_limit_bytes=VMEM),
        cost_estimate=pl.CostEstimate(flops=1, bytes_accessed=1, transcendentals=0),
    )(meta, spread, *arrays, *more)


def after(value, *done):
    return lax.optimization_barrier((value, *done))[0] if done else value


def over_segments(shares, count):
    parts = [shares[0]]
    for k in range(1, count):
        parts.append(lax.ppermute(shares[k], "seg", routes("seg", lambda i: (i + k) % count)))
    return parts


def shards(spectra, pairs, pair_count):
    blk, freqs = spectra.shape[0], spectra.shape[3]
    half = freqs // 2
    count = lax.axis_size("seg")
    me = lax.axis_index("src")
    seg = lax.axis_index("seg")
    side, row = me & 1, (me >> 1) & 1
    stages = 2
    width = blk // stages
    piece = width // count

    rows = spectra.reshape(count, stages, piece, 2, freqs).transpose(3, 1, 0, 2, 4).reshape(2, blk, freqs)
    rows = lax.optimization_barrier(rows)
    own, theirs = [lax.dynamic_slice_in_dim(rows, which * half, half, 2) for which in (side, 1 - side)]

    with jax.named_scope("pairs_along"):
        site_pairs = jnp.where(row == 1, to_site(pairs), pairs)
    with jax.named_scope("pairs_across"):
        named = jnp.concatenate([to_partner_site(pairs), site_pairs], axis=0)
    own, named = lax.optimization_barrier((own, named))

    sources = [[] for _ in range(WINDOW)]
    swapped, beside, along = [], [], []
    for c in range(stages):
        with jax.named_scope(f"swap{c}"):
            swapped.append(to_pair(after(theirs[:, c * width : (c + 1) * width], *swapped)))
    for c in range(stages):
        for kind in range(2):
            block = (own[:, c * width : (c + 1) * width], swapped[c])[kind]
            with jax.named_scope(f"along_{kind}_{c}"):
                along.append(to_site(after(block, *along[-2:-1])))
            with jax.named_scope(f"beside_{kind}_{c}"):
                beside.append(to_row(after(block, *beside[-2:-1])))
            for group, array in enumerate((block, beside[-1], along[-1])):
                sources[2 * group + kind].append((array, 0, width))

    owners = lax.axis_size("src")
    owner = jnp.where(row == 1, (me + owners - REACH) % owners, me)
    named = jnp.clip(named - (owner & ~1), 0, WINDOW - 1)
    group = jnp.where(row == 1, 2 - (named >> 1), named >> 1)
    meta = jnp.concatenate([(2 * group + ((named & 1) ^ side)).reshape(-1), seg[None]]).astype(jnp.int32)

    cosine, sine = lag_tables(freqs, LAGS)
    table = jnp.concatenate([part[at : at + 1] for part in (cosine, sine) for at in (0, 4, 5)] + [cosine[:2]], axis=0)
    table = lax.dynamic_slice_in_dim(table, side * half, half, 1)

    here, back = [], []

    def over_all(shares, name):
        with jax.named_scope(f"segments_{name}"):
            return sum(over_segments(shares, count))

    def exchange(total, name):
        with jax.named_scope(f"partner_stacks_{name}"):
            return to_pair(total)

    def give_back(mine, came, name):
        total = mine + came
        with jax.named_scope(f"stacks_back_{name}"):
            return total, to_owner(total)

    (partner,) = correlate(meta, table, sources, count, 0, width, 0, (stage_tiles(0),))
    sent = over_all(partner, "0")
    came = [exchange(sent, "0")]
    meta = after(meta, sent)
    every = stage_tiles(0) + stage_tiles(1)
    partner, mine = correlate(meta, table, sources, count, 1, width, 0, (stage_tiles(1), every))
    total = over_all([after(x, came[0]) for x in partner], "1")
    lag_parts = ((0, LAGS // 2), (LAGS // 2, LAGS))
    pieces = [(slot, *lags) for slot in range(SLOTS) for lags in lag_parts]
    came += [exchange(total[slot : slot + 1, low:high], f"1_{slot}_{low}") for slot, low, high in pieces]
    mine = over_all([after(x, total) for x in mine], "own")
    place = jnp.arange(LAGS * width)
    spread = (place[None, :] == (place % width * LAGS + place // width)[:, None]).astype(jnp.bfloat16)
    scale = float(count * spectra.shape[1] * freqs) ** (-0.5)
    meta = jnp.stack([row, pair_count[0]]).astype(jnp.int32)
    first = give_back(mine[:, :, :piece], came[0], "0")
    last = []
    for (slot, low, high), stacks in zip(pieces, came[1:]):
        mine = after(mine, first[0] if not last else last[-1][1])
        last.append((low, *give_back(mine[slot : slot + 1, low:high, piece:], stacks, f"1_{slot}_{low}")))
    result = None
    for slot in range(SLOTS):
        stacks = [[(0, *first)], last[slot * len(lag_parts) : (slot + 1) * len(lag_parts)]]
        result = finish(meta, spread, stacks, slot, count, piece, scale, result)
    return result


def solution(mesh):
    in_specs = (P("src", "seg", None, None), P("src", None), P("src"))
    out_specs = P("src", "seg", None)
    return jax.shard_map(shards, mesh=mesh, in_specs=in_specs, out_specs=out_specs, check_vma=False)
```

time: 469 us -> 132 us (0.28)
  the two profiles are of different devices: /device:TPU:0 before, /device:TPU:6 now
where the time goes in v2:
time: 132 us; the launch traced here: 131 us
  waiting for transfers between devices  55.9 us (42%)
  starting transfers between devices  33.8 us (26%)
  Pallas kernels  25.7 us (19%)
  other arithmetic  7.51 us (6%)
  local copies, waits for them, and re-layouts  7.46 us (6%)
    ppermute x7, waiting for transfers between devices, to_pair(): return lax.ppermute(value, 'src', routes('src', lambda d: d ^ 1))  20.9 us
    pallas_call x2, Pallas kernels, correlate(): pl.pallas_call(functools.partial(corr_kernel, count, stage, first, sets,...  18.8 us
    ppermute x5, starting transfers between devices, to_site(): lax.ppermute(value, 'src', routes('src', lambda d: (d + REACH) % size if...  14.2 us
    ppermute x4, waiting for transfers between devices, to_row(): return lax.ppermute(value, 'src', routes('src', lambda d: d ^ 2))  12.3 us
    ppermute x5, waiting for transfers between devices, to_owner(): lax.ppermute(value, 'src', routes('src', lambda d: (d - REACH) % size if...  9.92 us
    ppermute x5, starting transfers between devices, to_owner(): lax.ppermute(value, 'src', routes('src', lambda d: (d - REACH) % size if...  9.88 us
    ppermute x7, starting transfers between devices, to_pair(): return lax.ppermute(value, 'src', routes('src', lambda d: d ^ 1))  7.64 us
    ppermute x5, waiting for transfers between devices, to_site(): lax.ppermute(value, 'src', routes('src', lambda d: (d + REACH) % size if...  7.47 us
  transfers between devices with their start and end apart: 25, of which 14 were waited for; matrix products, arithmetic and copies ran while one was open for 8% of the time, Pallas kernels for 17%

profile of v2, /device:TPU:6, one launch (start us, length us, event | category | flops | bytes accessed | tf_op | source)
XLA Modules:
  0.0 131.4 jit_solution(35920594950055329)
XLA Ops:
  0.0 3.5 %collective-permute-start.1 = (s32[2,2]{1,0:T(2,128)}, s32[2,2]{1,0:T(2,128)S(1)}, u32[]{:S(2)}, u32[]{:S(2)}) collective-permute-start(s32[2,2]{1,0:T(2,128)} %param.4), channel_id=1, source_target_pairs={{4,12},{6,14},{8,0},{10,2},{12,20},{14,22},{16,8},{18,10},{20,28},... | collective-permute-start | bytes 56 | tf_op jit(solution)/shard_map/pairs_along/ppermute | solution.py:33
  3.5 1.6 %collective-permute-start = (s32[2,2]{1,0:T(2,128)}, s32[2,2]{1,0:T(2,128)S(1)}, u32[]{:S(2)}, u32[]{:S(2)}) collective-permute-start(s32[2,2]{1,0:T(2,128)} %param.4), channel_id=1, source_target_pairs={{0,2},{2,0},{4,14},{6,12},{8,10},{10,8},{12,22},{14,20},{16,18},{1... | collective-permute-start | bytes 56 | tf_op jit(solution)/shard_map/pairs_across/ppermute | solution.py:38
  5.1 2.5 %copy.6 = bf16[2,2,64,2,2048]{4,2,0,1,3:T(8,128)(2,1)S(1)} copy(bf16[2,2,64,2,2048]{4,3,2,1,0:T(2,128)(2,1)} %bitcast.8) | data formatting | bytes 4194304 | tf_op jit(solution)/shard_map/reshape | solution.py:257
  7.7 1.6 %collective-permute-start.2 = (bf16[2,128,1024]{2,1,0:T(8,128)(2,1)S(1)}, bf16[2,128,1024]{2,1,0:T(8,128)(2,1)}, u32[]{:S(2)}, u32[]{:S(2)}) collective-permute-start(bf16[2,128,1024]{2,1,0:T(8,128)(2,1)S(1)} %get-tuple-element.50), channel_id=1, source_target_pairs={{0,2},{2,0},{4,6},{6,4},{8,10},{10,8},{12,14},{14,12},{16,18},{18,... | collective-permute-start | bytes 1572872 | tf_op jit(solution)/shard_map/swap0/ppermute | solution.py:24
  10.9 3.2 %collective-permute-start.5 = (bf16[2,128,1024]{2,1,0:T(8,128)(2,1)S(1)}, bf16[2,128,1024]{2,1,0:T(8,128)(2,1)S(1)}, u32[]{:S(2)}, u32[]{:S(2)}) collective-permute-start(bf16[2,128,1024]{2,1,0:T(8,128)(2,1)S(1)} %get-tuple-element.56.refs_0_), channel_id=1, source_target_pairs={{4,12},{6,14},{8,0},{10,2},{12,20},{14,22},{16,8},{18,10},{20,28},... | collective-permute-start | bytes 1572872 | tf_op jit(solution)/shard_map/along_0_0/ppermute | solution.py:33
  14.1 6.8 %collective-permute-done.2.refs_1_.refs_2_ = bf16[2,128,1024]{2,1,0:T(8,128)(2,1)} collective-permute-done((bf16[2,128,1024]{2,1,0:T(8,128)(2,1)S(1)}, bf16[2,128,1024]{2,1,0:T(8,128)(2,1)}, u32[]{:S(2)}, u32[]{:S(2)}) %collective-permute-start.2) | collective-permute-done | bytes 524320 | tf_op jit(solution)/shard_map/swap0/ppermute | solution.py:24
  22.4 3.5 %collective-permute-start.6 = (bf16[2,128,1024]{2,1,0:T(8,128)(2,1)}, bf16[2,128,1024]{2,1,0:T(8,128)(2,1)}, u32[]{:S(2)}, u32[]{:S(2)}) collective-permute-start(bf16[2,128,1024]{2,1,0:T(8,128)(2,1)} %collective-permute-done.2.refs_1_.refs_2_), channel_id=1, source_target_pairs={{4,12},{6,14},{8,0},{10,2},{12,20},{14,22},{16,8},{18,10},{20,28},... | collective-permute-start | bytes 1572872 | tf_op jit(solution)/shard_map/along_1_0/ppermute | solution.py:33
  27.4 2.2 %collective-permute-start.11 = (bf16[2,128,1024]{2,1,0:T(8,128)(2,1)}, bf16[2,128,1024]{2,1,0:T(8,128)(2,1)}, u32[]{:S(2)}, u32[]{:S(2)}) collective-permute-start(bf16[2,128,1024]{2,1,0:T(8,128)(2,1)} %get-tuple-element.35.refs_1_), channel_id=1, source_target_pairs={{4,12},{6,14},{8,0},{10,2},{12,20},{14,22},{16,8},{18,10},{20,28},... | collective-permute-start | bytes 1572872 | tf_op jit(solution)/shard_map/along_0_1/ppermute | solution.py:33
  29.7 7.8 %collective-permute-done.4.refs_3_.refs_6_ = bf16[2,128,1024]{2,1,0:T(8,128)(2,1)S(1)} collective-permute-done((bf16[2,128,1024]{2,1,0:T(8,128)(2,1)}, bf16[2,128,1024]{2,1,0:T(8,128)(2,1)S(1)}, u32[]{:S(2)}, u32[]{:S(2)}) %collective-permute-start.4) | collective-permute-done | bytes 524320 | tf_op jit(solution)/shard_map/beside_1_0/ppermute | solution.py:28
  37.5 3.8 %collective-permute-done.6.refs_5_.refs_10_ = bf16[2,128,1024]{2,1,0:T(8,128)(2,1)} collective-permute-done((bf16[2,128,1024]{2,1,0:T(8,128)(2,1)}, bf16[2,128,1024]{2,1,0:T(8,128)(2,1)}, u32[]{:S(2)}, u32[]{:S(2)}) %collective-permute-start.6) | collective-permute-done | bytes 524320 | tf_op jit(solution)/shard_map/along_1_0/ppermute | solution.py:33
  41.3 1.9 %collective-permute-start.12 = (bf16[2,128,1024]{2,1,0:T(8,128)(2,1)}, bf16[2,128,1024]{2,1,0:T(8,128)(2,1)}, u32[]{:S(2)}, u32[]{:S(2)}) collective-permute-start(bf16[2,128,1024]{2,1,0:T(8,128)(2,1)} %collective-permute-done.8.refs_3_), channel_id=1, source_target_pairs={{4,12},{6,14},{8,0},{10,2},{12,20},{14,22},{16,8},{18,10},{20,28},... | collective-permute-start | bytes 1572872 | tf_op jit(solution)/shard_map/along_1_1/ppermute | solution.py:33
  43.3 5.3 %shard_map.37 = (f32[2,6,64,128]{3,2,1,0:T(8,128)}, f32[2,6,64,128]{3,2,1,0:T(8,128)}) custom-call(s32[9]{0:T(128)} %pad_add_fusion.2.meta, f32[8,1024]{1,0:T(8,128)} %constant_dynamic-slice_fusion.2.table, bf16[2,128,1024]{2,1,0:T(8,128)(2,1)} %copy-done.7, bf16[2,128,1024]{2,1,0:T(8,128)(2,1)} %collective-permute-done.2.refs_1_.refs_2_, ...), custom_call_target="tpu_custom_call" | custom-call | flops 9999999827968 | bytes 10000000000 | tf_op jit(solution)/shard_map/pallas_call | solution.py:159
  48.6 1.9 %collective-permute-done.7 = f32[2,6,64,128]{3,2,1,0:T(8,128)S(1)} collective-permute-done((f32[2,6,64,128]{3,2,1,0:T(8,128)}, f32[2,6,64,128]{3,2,1,0:T(8,128)S(1)}, u32[]{:S(2)}, u32[]{:S(2)}) %collective-permute-start.7) | collective-permute-done | bytes 393248 | tf_op jit(solution)/shard_map/segments_0/ppermute | solution.py:242
  50.6 1.8 %add.94 = f32[2,6,64,128]{3,2,1,0:T(8,128)} add(f32[2,6,64,128]{3,2,1,0:T(8,128)} %get-tuple-element.29, f32[2,6,64,128]{3,2,1,0:T(8,128)S(1)} %collective-permute-done.7) | non-fusion elementwise | flops 98304 | bytes 1179648 | tf_op jit(solution)/shard_map/segments_0/add | solution.py:296
  52.8 4.5 %collective-permute-done.10.refs_7_ = bf16[2,128,1024]{2,1,0:T(8,128)(2,1)} collective-permute-done((bf16[2,128,1024]{2,1,0:T(8,128)(2,1)}, bf16[2,128,1024]{2,1,0:T(8,128)(2,1)}, u32[]{:S(2)}, u32[]{:S(2)}) %collective-permute-start.10) | collective-permute-done | bytes 524320 | tf_op jit(solution)/shard_map/beside_1_1/ppermute | solution.py:28
  57.3 3.7 %collective-permute-done.12.refs_11_ = bf16[2,128,1024]{2,1,0:T(8,128)(2,1)} collective-permute-done((bf16[2,128,1024]{2,1,0:T(8,128)(2,1)}, bf16[2,128,1024]{2,1,0:T(8,128)(2,1)}, u32[]{:S(2)}, u32[]{:S(2)}) %collective-permute-start.12) | collective-permute-done | bytes 524320 | tf_op jit(solution)/shard_map/along_1_1/ppermute | solution.py:33
  61.0 13.5 %shard_map.38 = (f32[2,6,192,128]{3,2,1,0:T(8,128)}, f32[2,6,192,128]{3,2,1,0:T(8,128)}, f32[2,6,256,128]{3,2,1,0:T(8,128)}, f32[2,6,256,128]{3,2,1,0:T(8,128)}) custom-call(s32[9]{0:T(128)} %pad_add_fusion.2.meta, f32[8,1024]{1,0:T(8,128)} %constant_dynamic-slice_fusion.2.table, bf16[2,128,1024]{2,1,0:T(8,128)(2,1)} %copy-done.7, ...), custom_call_target="tpu_custom_call" | custom-call | flops 9999999827968 | bytes 10000000000 | tf_op jit(solution)/shard_map/pallas_call | solution.py:159
  74.6 3.0 %collective-permute-done.14 = f32[2,6,192,128]{3,2,1,0:T(8,128)S(1)} collective-permute-done((f32[2,6,192,128]{3,2,1,0:T(8,128)}, f32[2,6,192,128]{3,2,1,0:T(8,128)S(1)}, u32[]{:S(2)}, u32[]{:S(2)}) %collective-permute-start.14) | collective-permute-done | bytes 1179680 | tf_op jit(solution)/shard_map/segments_1/ppermute | solution.py:242
  80.7 1.6 %collective-permute-start.18 = (f32[1,3,192,128]{3,2,1,0:T(8,128)S(1)}, f32[1,3,192,128]{3,2,1,0:T(8,128)S(1)}, u32[]{:S(2)}, u32[]{:S(2)}) collective-permute-start(f32[1,3,192,128]{3,2,1,0:T(8,128)S(1)} %get-tuple-element.53), channel_id=1, source_target_pairs={{0,2},{2,0},{4,6},{6,4},{8,10},{10,8},{12,14},{14,12},{16,18},{18,... | collective-permute-start | bytes 884744 | tf_op jit(solution)/shard_map/partner_stacks_1_0_3/ppermute | solution.py:24
  85.5 3.8 %collective-permute-done.17 = f32[1,3,192,128]{3,2,1,0:T(8,128)S(1)} collective-permute-done((f32[1,3,192,128]{3,2,1,0:T(8,128)S(1)}, f32[1,3,192,128]{3,2,1,0:T(8,128)S(1)}, u32[]{:S(2)}, u32[]{:S(2)}) %collective-permute-start.17) | collective-permute-done | bytes 294944 | tf_op jit(solution)/shard_map/partner_stacks_1_0_0/ppermute | solution.py:24
  89.3 1.9 %collective-permute-start.23 = (f32[1,3,192,128]{3,2,1,0:T(8,128)S(1)}, f32[1,3,192,128]{3,2,1,0:T(8,128)S(1)}, u32[]{:S(2)}, u32[]{:S(2)}) collective-permute-start(f32[1,3,192,128]{3,2,1,0:T(8,128)S(1)} %slice_add_fusion.4.refs_2_), channel_id=1, source_target_pairs={{4,28},{6,30},{12,4},{14,6},{20,12},{22,14},{28,20},{30,22},{5,29}... | collective-permute-start | bytes 884744 | tf_op jit(solution)/shard_map/stacks_back_1_0_0/ppermute | solution.py:43
  91.3 2.2 %collective-permute-start.16 = (f32[2,6,64,128]{3,2,1,0:T(8,128)S(1)}, f32[2,6,64,128]{3,2,1,0:T(8,128)S(1)}, u32[]{:S(2)}, u32[]{:S(2)}) collective-permute-start(f32[2,6,64,128]{3,2,1,0:T(8,128)S(1)} %slice_add_fusion.refs_0_), channel_id=1, source_target_pairs={{4,28},{6,30},{12,4},{14,6},{20,12},{22,14},{28,20},{30,22},{5,29}... | collective-permute-start | bytes 1179656 | tf_op jit(solution)/shard_map/stacks_back_0/ppermute | solution.py:43
  93.5 2.1 %collective-permute-done.18 = f32[1,3,192,128]{3,2,1,0:T(8,128)S(1)} collective-permute-done((f32[1,3,192,128]{3,2,1,0:T(8,128)S(1)}, f32[1,3,192,128]{3,2,1,0:T(8,128)S(1)}, u32[]{:S(2)}, u32[]{:S(2)}) %collective-permute-start.18) | collective-permute-done | bytes 294944 | tf_op jit(solution)/shard_map/partner_stacks_1_0_3/ppermute | solution.py:24
  95.7 1.9 %collective-permute-start.24 = (f32[1,3,192,128]{3,2,1,0:T(8,128)S(1)}, f32[1,3,192,128]{3,2,1,0:T(8,128)S(1)}, u32[]{:S(2)}, u32[]{:S(2)}) collective-permute-start(f32[1,3,192,128]{3,2,1,0:T(8,128)S(1)} %slice_add_fusion.3.refs_4_), channel_id=1, source_target_pairs={{4,28},{6,30},{12,4},{14,6},{20,12},{22,14},{28,20},{30,22},{5,29}... | collective-permute-start | bytes 884744 | tf_op jit(solution)/shard_map/stacks_back_1_0_3/ppermute | solution.py:43
  97.6 4.3 %collective-permute-done.19 = f32[1,3,192,128]{3,2,1,0:T(8,128)S(1)} collective-permute-done((f32[1,3,192,128]{3,2,1,0:T(8,128)S(1)}, f32[1,3,192,128]{3,2,1,0:T(8,128)S(1)}, u32[]{:S(2)}, u32[]{:S(2)}) %collective-permute-start.19) | collective-permute-done | bytes 294944 | tf_op jit(solution)/shard_map/partner_stacks_1_1_0/ppermute | solution.py:24
  102.0 1.9 %collective-permute-start.20 = (f32[1,3,192,128]{3,2,1,0:T(8,128)S(1)}, f32[1,3,192,128]{3,2,1,0:T(8,128)S(1)}, u32[]{:S(2)}, u32[]{:S(2)}) collective-permute-start(f32[1,3,192,128]{3,2,1,0:T(8,128)S(1)} %slice_add_fusion.2.refs_2_), channel_id=1, source_target_pairs={{4,28},{6,30},{12,4},{14,6},{20,12},{22,14},{28,20},{30,22},{5,29}... | collective-permute-start | bytes 884744 | tf_op jit(solution)/shard_map/stacks_back_1_1_0/ppermute | solution.py:43
  103.9 3.8 %collective-permute-done.21 = f32[1,3,192,128]{3,2,1,0:T(8,128)S(1)} collective-permute-done((f32[1,3,192,128]{3,2,1,0:T(8,128)S(1)}, f32[1,3,192,128]{3,2,1,0:T(8,128)S(1)}, u32[]{:S(2)}, u32[]{:S(2)}) %collective-permute-start.21) | collective-permute-done | bytes 294944 | tf_op jit(solution)/shard_map/partner_stacks_1_1_3/ppermute | solution.py:24
  107.8 1.9 %collective-permute-start.22 = (f32[1,3,192,128]{3,2,1,0:T(8,128)S(1)}, f32[1,3,192,128]{3,2,1,0:T(8,128)S(1)}, u32[]{:S(2)}, u32[]{:S(2)}) collective-permute-start(f32[1,3,192,128]{3,2,1,0:T(8,128)S(1)} %slice_add_fusion.1.refs_4_), channel_id=1, source_target_pairs={{4,28},{6,30},{12,4},{14,6},{20,12},{22,14},{28,20},{30,22},{5,29}... | collective-permute-start | bytes 884744 | tf_op jit(solution)/shard_map/stacks_back_1_1_3/ppermute | solution.py:43
  111.6 4.3 %collective-permute-done.24.refs_5_ = f32[1,3,192,128]{3,2,1,0:T(8,128)S(1)} collective-permute-done((f32[1,3,192,128]{3,2,1,0:T(8,128)S(1)}, f32[1,3,192,128]{3,2,1,0:T(8,128)S(1)}, u32[]{:S(2)}, u32[]{:S(2)}) %collective-permute-start.24) | collective-permute-done | bytes 294944 | tf_op jit(solution)/shard_map/stacks_back_1_0_3/ppermute | solution.py:43
  117.5 3.4 %shard_map.39.refs_6_ = f32[2,128,1536]{2,1,0:T(8,128)} custom-call(s32[2]{0:T(128)} %pad_add_fusion.1.meta, bf16[768,768]{1,0:T(8,128)(2,1)} %fusion.spread, f32[2,6,64,128]{3,2,1,0:T(8,128)} %copy-done, f32[2,6,64,128]{3,2,1,0:T(8,128)} %copy-done.1, f32[1,3,192,128]{3,2,1,0:T(8,128)} %copy-done.3, f32[1,3,192,128]{3,2,1,0:T(8,128)} %copy-done.8, ...), custom_call_target="tpu_custom_call" | custom-call | flops 1 | bytes 1 | tf_op jit(solution)/shard_map/pallas_call | solution.py:221
  120.9 5.6 %collective-permute-done.22.refs_5_ = f32[1,3,192,128]{3,2,1,0:T(8,128)S(1)} collective-permute-done((f32[1,3,192,128]{3,2,1,0:T(8,128)S(1)}, f32[1,3,192,128]{3,2,1,0:T(8,128)S(1)}, u32[]{:S(2)}, u32[]{:S(2)}) %collective-permute-start.22) | collective-permute-done | bytes 294944 | tf_op jit(solution)/shard_map/stacks_back_1_1_3/ppermute | solution.py:43
  128.0 3.4 %shard_map.40 = f32[2,128,1536]{2,1,0:T(8,128)} custom-call(s32[2]{0:T(128)} %pad_add_fusion.1.meta, bf16[768,768]{1,0:T(8,128)(2,1)} %fusion.spread, f32[2,6,64,128]{3,2,1,0:T(8,128)} %copy-done, f32[2,6,64,128]{3,2,1,0:T(8,128)} %copy-done.1, f32[1,3,192,128]{3,2,1,0:T(8,128)} %copy-done.4, ...), custom_call_target="tpu_custom_call", output_to_operand_aliasing={{}: (8, {})} | custom-call | flops 1 | bytes 1 | tf_op jit(solution)/shard_map/pallas_call | solution.py:221
  (85 shorter events, 16.0 us)
Async XLA Ops:
  0.0 9.7 %collective-permute-start.1 = (s32[2,2]{1,0:T(2,128)}, s32[2,2]{1,0:T(2,128)S(1)}, u32[]{:S(2)}, u32[]{:S(2)}) collective-permute-start(s32[2,2]{1,0:T(2,128)} %param.4), channel_id=1, source_target_pairs={{4,12},{6,14},{8,0},{10,2},{12,20},{14,22},{16,8},{18,10},{20,28},... | collective-permute-start | bytes 56 | tf_op jit(solution)/shard_map/pairs_along/ppermute | solution.py:33
  3.5 6.5 %collective-permute-start = (s32[2,2]{1,0:T(2,128)}, s32[2,2]{1,0:T(2,128)S(1)}, u32[]{:S(2)}, u32[]{:S(2)}) collective-permute-start(s32[2,2]{1,0:T(2,128)} %param.4), channel_id=1, source_target_pairs={{0,2},{2,0},{4,14},{6,12},{8,10},{10,8},{12,22},{14,20},{16,18},{1... | collective-permute-start | bytes 56 | tf_op jit(solution)/shard_map/pairs_across/ppermute | solution.py:38
  7.7 13.3 %collective-permute-start.2 = (bf16[2,128,1024]{2,1,0:T(8,128)(2,1)S(1)}, bf16[2,128,1024]{2,1,0:T(8,128)(2,1)}, u32[]{:S(2)}, u32[]{:S(2)}) collective-permute-start(bf16[2,128,1024]{2,1,0:T(8,128)(2,1)S(1)} %get-tuple-element.50), channel_id=1, source_target_pairs={{0,2},{2,0},{4,6},{6,4},{8,10},{10,8},{12,14},{14,12},{16,18},{18,... | collective-permute-start | bytes 1572872 | tf_op jit(solution)/shard_map/swap0/ppermute | solution.py:24
  10.9 32.3 %copy-start.7 = (bf16[2,128,1024]{2,1,0:T(8,128)(2,1)}, bf16[2,128,1024]{2,1,0:T(8,128)(2,1)S(1)}, u32[]{:S(2)}) copy-start(bf16[2,128,1024]{2,1,0:T(8,128)(2,1)S(1)} %get-tuple-element.56.refs_0_) | copy-start | bytes 1572868
  10.9 18.7 %collective-permute-start.3 = (bf16[2,128,1024]{2,1,0:T(8,128)(2,1)S(1)}, bf16[2,128,1024]{2,1,0:T(8,128)(2,1)S(1)}, u32[]{:S(2)}, u32[]{:S(2)}) collective-permute-start(bf16[2,128,1024]{2,1,0:T(8,128)(2,1)S(1)} %get-tuple-element.56.refs_0_), channel_id=1, source_target_pairs={{0,4},{2,6},{4,0},{6,2},{8,12},{10,14},{12,8},{14,10},{16,20},{18,... | collective-permute-start | bytes 1572872 | tf_op jit(solution)/shard_map/beside_0_0/ppermute | solution.py:28
  10.9 16.5 %collective-permute-start.5 = (bf16[2,128,1024]{2,1,0:T(8,128)(2,1)S(1)}, bf16[2,128,1024]{2,1,0:T(8,128)(2,1)S(1)}, u32[]{:S(2)}, u32[]{:S(2)}) collective-permute-start(bf16[2,128,1024]{2,1,0:T(8,128)(2,1)S(1)} %get-tuple-element.56.refs_0_), channel_id=1, source_target_pairs={{4,12},{6,14},{8,0},{10,2},{12,20},{14,22},{16,8},{18,10},{20,28},... | collective-permute-start | bytes 1572872 | tf_op jit(solution)/shard_map/along_0_0/ppermute | solution.py:33
  21.0 16.6 %collective-permute-start.8 = (bf16[2,128,1024]{2,1,0:T(8,128)(2,1)S(1)}, bf16[2,128,1024]{2,1,0:T(8,128)(2,1)}, u32[]{:S(2)}, u32[]{:S(2)}) collective-permute-start(bf16[2,128,1024]{2,1,0:T(8,128)(2,1)S(1)} %get-tuple-element.32), channel_id=1, source_target_pairs={{0,2},{2,0},{4,6},{6,4},{8,10},{10,8},{12,14},{14,12},{16,18},{18,... | collective-permute-start | bytes 1572872 | tf_op jit(solution)/shard_map/swap1/ppermute | solution.py:24
  22.4 15.1 %collective-permute-start.4 = (bf16[2,128,1024]{2,1,0:T(8,128)(2,1)}, bf16[2,128,1024]{2,1,0:T(8,128)(2,1)S(1)}, u32[]{:S(2)}, u32[]{:S(2)}) collective-permute-start(bf16[2,128,1024]{2,1,0:T(8,128)(2,1)} %collective-permute-done.2.refs_1_.refs_2_), channel_id=1, source_target_pairs={{0,4},{2,6},{4,0},{6,2},{8,12},{10,14},{12,8},{14,10},{16,20},{18,... | collective-permute-start | bytes 1572872 | tf_op jit(solution)/shard_map/beside_1_0/ppermute | solution.py:28
  22.4 18.9 %collective-permute-start.6 = (bf16[2,128,1024]{2,1,0:T(8,128)(2,1)}, bf16[2,128,1024]{2,1,0:T(8,128)(2,1)}, u32[]{:S(2)}, u32[]{:S(2)}) collective-permute-start(bf16[2,128,1024]{2,1,0:T(8,128)(2,1)} %collective-permute-done.2.refs_1_.refs_2_), channel_id=1, source_target_pairs={{4,12},{6,14},{8,0},{10,2},{12,20},{14,22},{16,8},{18,10},{20,28},... | collective-permute-start | bytes 1572872 | tf_op jit(solution)/shard_map/along_1_0/ppermute | solution.py:33
  27.4 15.8 %copy-start.15 = (bf16[2,128,1024]{2,1,0:T(8,128)(2,1)}, bf16[2,128,1024]{2,1,0:T(8,128)(2,1)S(1)}, u32[]{:S(2)}) copy-start(bf16[2,128,1024]{2,1,0:T(8,128)(2,1)S(1)} %collective-permute-done.5.refs_4_.refs_8_) | copy-start | bytes 1572868
  27.4 25.4 %collective-permute-start.11 = (bf16[2,128,1024]{2,1,0:T(8,128)(2,1)}, bf16[2,128,1024]{2,1,0:T(8,128)(2,1)}, u32[]{:S(2)}, u32[]{:S(2)}) collective-permute-start(bf16[2,128,1024]{2,1,0:T(8,128)(2,1)} %get-tuple-element.35.refs_1_), channel_id=1, source_target_pairs={{4,12},{6,14},{8,0},{10,2},{12,20},{14,22},{16,8},{18,10},{20,28},... | collective-permute-start | bytes 1572872 | tf_op jit(solution)/shard_map/along_0_1/ppermute | solution.py:33
  29.6 13.6 %copy-start.14 = (bf16[2,128,1024]{2,1,0:T(8,128)(2,1)}, bf16[2,128,1024]{2,1,0:T(8,128)(2,1)S(1)}, u32[]{:S(2)}) copy-start(bf16[2,128,1024]{2,1,0:T(8,128)(2,1)S(1)} %collective-permute-done.3.refs_2_.refs_4_) | copy-start | bytes 1572868
  29.6 23.1 %collective-permute-start.9 = (bf16[2,128,1024]{2,1,0:T(8,128)(2,1)}, bf16[2,128,1024]{2,1,0:T(8,128)(2,1)}, u32[]{:S(2)}, u32[]{:S(2)}) collective-permute-start(bf16[2,128,1024]{2,1,0:T(8,128)(2,1)} %get-tuple-element.35.refs_1_), channel_id=1, source_target_pairs={{0,4},{2,6},{4,0},{6,2},{8,12},{10,14},{12,8},{14,10},{16,20},{18,... | collective-permute-start | bytes 1572872 | tf_op jit(solution)/shard_map/beside_0_1/ppermute | solution.py:28
  37.5 19.8 %collective-permute-start.10 = (bf16[2,128,1024]{2,1,0:T(8,128)(2,1)}, bf16[2,128,1024]{2,1,0:T(8,128)(2,1)}, u32[]{:S(2)}, u32[]{:S(2)}) collective-permute-start(bf16[2,128,1024]{2,1,0:T(8,128)(2,1)} %collective-permute-done.8.refs_3_), channel_id=1, source_target_pairs={{0,4},{2,6},{4,0},{6,2},{8,12},{10,14},{12,8},{14,10},{16,20},{18,... | collective-permute-start | bytes 1572872 | tf_op jit(solution)/shard_map/beside_1_1/ppermute | solution.py:28
  41.3 19.7 %collective-permute-start.12 = (bf16[2,128,1024]{2,1,0:T(8,128)(2,1)}, bf16[2,128,1024]{2,1,0:T(8,128)(2,1)}, u32[]{:S(2)}, u32[]{:S(2)}) collective-permute-start(bf16[2,128,1024]{2,1,0:T(8,128)(2,1)} %collective-permute-done.8.refs_3_), channel_id=1, source_target_pairs={{4,12},{6,14},{8,0},{10,2},{12,20},{14,22},{16,8},{18,10},{20,28},... | collective-permute-start | bytes 1572872 | tf_op jit(solution)/shard_map/along_1_1/ppermute | solution.py:33
  48.6 2.0 %collective-permute-start.7 = (f32[2,6,64,128]{3,2,1,0:T(8,128)}, f32[2,6,64,128]{3,2,1,0:T(8,128)S(1)}, u32[]{:S(2)}, u32[]{:S(2)}) collective-permute-start(f32[2,6,64,128]{3,2,1,0:T(8,128)} %get-tuple-element.30), channel_id=1, source_target_pairs={{0,1},{1,0},{2,3},{3,2},{4,5},{5,4},{6,7},{7,6},{8,9},{9,8},{10,11... | collective-permute-start | bytes 1179656 | tf_op jit(solution)/shard_map/segments_0/ppermute | solution.py:242
  52.4 22.2 %collective-permute-start.13 = (f32[2,6,64,128]{3,2,1,0:T(8,128)}, f32[2,6,64,128]{3,2,1,0:T(8,128)}, u32[]{:S(2)}, u32[]{:S(2)}) collective-permute-start(f32[2,6,64,128]{3,2,1,0:T(8,128)} %add.94), channel_id=1, source_target_pairs={{0,2},{2,0},{4,6},{6,4},{8,10},{10,8},{12,14},{14,12},{16,18},{18,... | collective-permute-start | bytes 1179656 | tf_op jit(solution)/shard_map/partner_stacks_0/ppermute | solution.py:24
  74.5 3.1 %collective-permute-start.14 = (f32[2,6,192,128]{3,2,1,0:T(8,128)}, f32[2,6,192,128]{3,2,1,0:T(8,128)S(1)}, u32[]{:S(2)}, u32[]{:S(2)}) collective-permute-start(f32[2,6,192,128]{3,2,1,0:T(8,128)} %get-tuple-element.41), channel_id=1, source_target_pairs={{0,1},{1,0},{2,3},{3,2},{4,5},{5,4},{6,7},{7,6},{8,9},{9,8},{10,11... | collective-permute-start | bytes 3538952 | tf_op jit(solution)/shard_map/segments_1/ppermute | solution.py:242
  79.1 5.1 %collective-permute-start.15 = (f32[2,6,256,128]{3,2,1,0:T(8,128)S(1)}, f32[2,6,256,128]{3,2,1,0:T(8,128)S(1)}, u32[]{:S(2)}, u32[]{:S(2)}) collective-permute-start(f32[2,6,256,128]{3,2,1,0:T(8,128)S(1)} %copy-done.13), channel_id=1, source_target_pairs={{0,1},{1,0},{2,3},{3,2},{4,5},{5,4},{6,7},{7,6},{8,9},{9,8},{10,11... | collective-permute-start | bytes 4718600 | tf_op jit(solution)/shard_map/segments_own/ppermute | solution.py:242
  79.4 9.9 %collective-permute-start.17 = (f32[1,3,192,128]{3,2,1,0:T(8,128)S(1)}, f32[1,3,192,128]{3,2,1,0:T(8,128)S(1)}, u32[]{:S(2)}, u32[]{:S(2)}) collective-permute-start(f32[1,3,192,128]{3,2,1,0:T(8,128)S(1)} %get-tuple-element.54), channel_id=1, source_target_pairs={{0,2},{2,0},{4,6},{6,4},{8,10},{10,8},{12,14},{14,12},{16,18},{18,... | collective-permute-start | bytes 884744 | tf_op jit(solution)/shard_map/partner_stacks_1_0_0/ppermute | solution.py:24
  80.7 15.0 %collective-permute-start.18 = (f32[1,3,192,128]{3,2,1,0:T(8,128)S(1)}, f32[1,3,192,128]{3,2,1,0:T(8,128)S(1)}, u32[]{:S(2)}, u32[]{:S(2)}) collective-permute-start(f32[1,3,192,128]{3,2,1,0:T(8,128)S(1)} %get-tuple-element.53), channel_id=1, source_target_pairs={{0,2},{2,0},{4,6},{6,4},{8,10},{10,8},{12,14},{14,12},{16,18},{18,... | collective-permute-start | bytes 884744 | tf_op jit(solution)/shard_map/partner_stacks_1_0_3/ppermute | solution.py:24
  82.2 19.7 %collective-permute-start.19 = (f32[1,3,192,128]{3,2,1,0:T(8,128)S(1)}, f32[1,3,192,128]{3,2,1,0:T(8,128)S(1)}, u32[]{:S(2)}, u32[]{:S(2)}) collective-permute-start(f32[1,3,192,128]{3,2,1,0:T(8,128)S(1)} %get-tuple-element.52), channel_id=1, source_target_pairs={{0,2},{2,0},{4,6},{6,4},{8,10},{10,8},{12,14},{14,12},{16,18},{18,... | collective-permute-start | bytes 884744 | tf_op jit(solution)/shard_map/partner_stacks_1_1_0/ppermute | solution.py:24
  82.7 25.0 %collective-permute-start.21 = (f32[1,3,192,128]{3,2,1,0:T(8,128)S(1)}, f32[1,3,192,128]{3,2,1,0:T(8,128)S(1)}, u32[]{:S(2)}, u32[]{:S(2)}) collective-permute-start(f32[1,3,192,128]{3,2,1,0:T(8,128)S(1)} %get-tuple-element.51), channel_id=1, source_target_pairs={{0,2},{2,0},{4,6},{6,4},{8,10},{10,8},{12,14},{14,12},{16,18},{18,... | collective-permute-start | bytes 884744 | tf_op jit(solution)/shard_map/partner_stacks_1_1_3/ppermute | solution.py:24
  85.5 22.3 %copy-start = (f32[2,6,64,128]{3,2,1,0:T(8,128)}, f32[2,6,64,128]{3,2,1,0:T(8,128)S(1)}, u32[]{:S(2)}) copy-start(f32[2,6,64,128]{3,2,1,0:T(8,128)S(1)} %slice_add_fusion.refs_0_) | copy-start | bytes 1179652
  89.3 22.3 %copy-start.3 = (f32[1,3,192,128]{3,2,1,0:T(8,128)}, f32[1,3,192,128]{3,2,1,0:T(8,128)S(1)}, u32[]{:S(2)}) copy-start(f32[1,3,192,128]{3,2,1,0:T(8,128)S(1)} %slice_add_fusion.4.refs_2_) | copy-start | bytes 884740
  89.3 26.6 %collective-permute-start.23 = (f32[1,3,192,128]{3,2,1,0:T(8,128)S(1)}, f32[1,3,192,128]{3,2,1,0:T(8,128)S(1)}, u32[]{:S(2)}, u32[]{:S(2)}) collective-permute-start(f32[1,3,192,128]{3,2,1,0:T(8,128)S(1)} %slice_add_fusion.4.refs_2_), channel_id=1, source_target_pairs={{4,28},{6,30},{12,4},{14,6},{20,12},{22,14},{28,20},{30,22},{5,29}... | collective-permute-start | bytes 884744 | tf_op jit(solution)/shard_map/stacks_back_1_0_0/ppermute | solution.py:43
  91.3 24.7 %collective-permute-start.16 = (f32[2,6,64,128]{3,2,1,0:T(8,128)S(1)}, f32[2,6,64,128]{3,2,1,0:T(8,128)S(1)}, u32[]{:S(2)}, u32[]{:S(2)}) collective-permute-start(f32[2,6,64,128]{3,2,1,0:T(8,128)S(1)} %slice_add_fusion.refs_0_), channel_id=1, source_target_pairs={{4,28},{6,30},{12,4},{14,6},{20,12},{22,14},{28,20},{30,22},{5,29}... | collective-permute-start | bytes 1179656 | tf_op jit(solution)/shard_map/stacks_back_0/ppermute | solution.py:43
  95.7 20.3 %copy-start.5 = (f32[1,3,192,128]{3,2,1,0:T(8,128)}, f32[1,3,192,128]{3,2,1,0:T(8,128)S(1)}, u32[]{:S(2)}) copy-start(f32[1,3,192,128]{3,2,1,0:T(8,128)S(1)} %slice_add_fusion.3.refs_4_) | copy-start | bytes 884740
  95.7 20.3 %collective-permute-start.24 = (f32[1,3,192,128]{3,2,1,0:T(8,128)S(1)}, f32[1,3,192,128]{3,2,1,0:T(8,128)S(1)}, u32[]{:S(2)}, u32[]{:S(2)}) collective-permute-start(f32[1,3,192,128]{3,2,1,0:T(8,128)S(1)} %slice_add_fusion.3.refs_4_), channel_id=1, source_target_pairs={{4,28},{6,30},{12,4},{14,6},{20,12},{22,14},{28,20},{30,22},{5,29}... | collective-permute-start | bytes 884744 | tf_op jit(solution)/shard_map/stacks_back_1_0_3/ppermute | solution.py:43
  102.0 18.9 %copy-start.4 = (f32[1,3,192,128]{3,2,1,0:T(8,128)}, f32[1,3,192,128]{3,2,1,0:T(8,128)S(1)}, u32[]{:S(2)}) copy-start(f32[1,3,192,128]{3,2,1,0:T(8,128)S(1)} %slice_add_fusion.2.refs_2_) | copy-start | bytes 884740
  102.0 24.6 %collective-permute-start.20 = (f32[1,3,192,128]{3,2,1,0:T(8,128)S(1)}, f32[1,3,192,128]{3,2,1,0:T(8,128)S(1)}, u32[]{:S(2)}, u32[]{:S(2)}) collective-permute-start(f32[1,3,192,128]{3,2,1,0:T(8,128)S(1)} %slice_add_fusion.2.refs_2_), channel_id=1, source_target_pairs={{4,28},{6,30},{12,4},{14,6},{20,12},{22,14},{28,20},{30,22},{5,29}... | collective-permute-start | bytes 884744 | tf_op jit(solution)/shard_map/stacks_back_1_1_0/ppermute | solution.py:43
  107.8 18.8 %collective-permute-start.22 = (f32[1,3,192,128]{3,2,1,0:T(8,128)S(1)}, f32[1,3,192,128]{3,2,1,0:T(8,128)S(1)}, u32[]{:S(2)}, u32[]{:S(2)}) collective-permute-start(f32[1,3,192,128]{3,2,1,0:T(8,128)S(1)} %slice_add_fusion.1.refs_4_), channel_id=1, source_target_pairs={{4,28},{6,30},{12,4},{14,6},{20,12},{22,14},{28,20},{30,22},{5,29}... | collective-permute-start | bytes 884744 | tf_op jit(solution)/shard_map/stacks_back_1_1_3/ppermute | solution.py:43
  (10 other events, 34.4 us)

commit v3 on v2

--- a/solution.py
+++ b/solution.py
@@ -28,19 +28,8 @@
     return lax.ppermute(value, "src", routes("src", lambda d: d ^ 2))
 
 
-def to_site(value):
-    size = lax.axis_size("src")
-    return lax.ppermute(value, "src", routes("src", lambda d: (d + REACH) % size if d >> 1 & 1 else d - REACH))
-
-
-def to_partner_site(value):
-    size = lax.axis_size("src")
-    return lax.ppermute(value, "src", routes("src", lambda d: ((d + REACH) % size if d >> 1 & 1 else d) ^ 1))
-
-
-def to_owner(value):
-    size = lax.axis_size("src")
-    return lax.ppermute(value, "src", routes("src", lambda d: (d - REACH) % size if d >> 1 & 1 else -1))
+def to_below(value):
+    return lax.ppermute(value, "src", routes("src", lambda d: d - REACH))
 
 
 def lag_tables(freqs, lags):
@@ -129,9 +118,9 @@
     product = lax.dot_general(
         x_ref[...], right[now], (((1,), (1,)), ((), ())), preferred_element_type=jnp.float32
     )
-    for n, tiles in enumerate(sets):
-
-        @pl.when(at // SLOTS == n)
+    for n, (which, slot, tiles) in enumerate(sets):
+
+        @pl.when((at // SLOTS == which) if slot is None else (at == which * SLOTS + slot))
         def _():
             for k in range(count):
                 for tile, (a, b) in enumerate(tiles):
@@ -155,15 +144,18 @@
                 items.append((at, source, start, rows))
                 start += rows
         layout.append(tuple(items))
-    shapes = [(SLOTS, LAGS, len(tiles) * piece, size) for tiles in sets for _ in range(count)]
+    shapes = [
+        (SLOTS if slot is None else 1, LAGS, len(tiles) * piece, size) for _, slot, tiles in sets for _ in range(count)
+    ]
+    steps = SLOTS * (1 + max(which for which, _, _ in sets))
     outs = pl.pallas_call(
         functools.partial(corr_kernel, count, stage, first, sets, tuple(layout)),
         out_shape=[jax.ShapeDtypeStruct(shape, jnp.float32) for shape in shapes],
-        grid=(SLOTS * len(sets),),
+        grid=(steps,),
         in_specs=[pl.BlockSpec(memory_space=pltpu.SMEM), pl.BlockSpec(memory_space=pltpu.VMEM)]
         + [pl.BlockSpec(memory_space=pl.ANY)] * len(blocks),
         out_specs=[
-            pl.BlockSpec((1,) + shape[1:], lambda s, n=n // count: (jnp.clip(s - n * SLOTS, 0, SLOTS - 1), 0, 0, 0))
+            pl.BlockSpec((1,) + shape[1:], lambda s, n=sets[n // count][0], top=shape[0] - 1: (jnp.clip(s - n * SLOTS, 0, top), 0, 0, 0))
             for n, shape in enumerate(shapes)
         ],
         scratch_shapes=[
@@ -178,24 +170,19 @@
     return [outs[n * count : (n + 1) * count] for n in range(len(sets))]
 
 
-def finish_kernel(count, piece, stages, slot, scale, layout, meta, spread, *refs):
+def finish_kernel(count, piece, stages, slot, scale, pair_count, spread, *refs):
     out = refs[-1]
-    away = meta[0] > 0
-
-    def find(stage, lag, at):
-        ref, first = layout[stage][lag]
-        return jnp.where(away, refs[2 * ref + 1][0, lag - first, at], refs[2 * ref][0, lag - first, at])
-
     tiles = [(stage, t, a, b) for stage in range(stages) for t, (a, b) in enumerate(stage_tiles(stage))]
+    own, came = refs[: len(tiles)], refs[len(tiles) : len(tiles) + stages]
     high, low = [], []
-    for stage, t, _, _ in tiles:
+    for n, (stage, t, _, _) in enumerate(tiles):
         at = slice(t * piece, (t + 1) * piece)
-        total = jnp.concatenate([find(stage, lag, at) for lag in range(LAGS)], axis=1)
+        total = jnp.concatenate([own[n][0, lag] + came[stage][0, lag, at] for lag in range(LAGS)], axis=1)
         top = total.astype(jnp.bfloat16)
         high.append(top)
         low.append((total - top.astype(jnp.float32)).astype(jnp.bfloat16))
     moved = jnp.dot(jnp.concatenate(high + low, axis=0), spread[...], preferred_element_type=jnp.float32)
-    keep = slot < meta[1]
+    keep = slot < pair_count[0]
     run = piece * LAGS
     for n, (_, _, a, b) in enumerate(tiles):
         m = n + len(tiles)
@@ -206,20 +193,14 @@
             out[0, a * piece : (a + 1) * piece, col : col + run] = both[:, seg * run : (seg + 1) * run]
 
 
-def finish(meta, spread, stacks, slot, count, piece, scale, result):
-    layout, arrays = [], []
-    for pieces in stacks:
-        where = []
-        for first, here, back in pieces:
-            where += [(len(arrays) // 2, first)] * here.shape[1]
-            arrays += [here, back]
-        layout.append(tuple(where))
-    stages = len(stacks)
+def finish(pair_count, spread, own, came, slot, count, piece, scale, result):
+    stages = len(came)
+    arrays = [*own, *came]
     shape = (SLOTS, stages * piece, stages * piece * count * LAGS)
     specs = [pl.BlockSpec((1,) + x.shape[1:], lambda i, at=min(slot, x.shape[0] - 1): (at, 0, 0, 0)) for x in arrays]
     more = [] if result is None else [result]
     return pl.pallas_call(
-        functools.partial(finish_kernel, count, piece, stages, slot, scale, tuple(layout)),
+        functools.partial(finish_kernel, count, piece, stages, slot, scale),
         out_shape=jax.ShapeDtypeStruct(shape, jnp.float32),
         grid=(1,),
         in_specs=[pl.BlockSpec(memory_space=pltpu.SMEM), pl.BlockSpec(memory_space=pltpu.VMEM)]
@@ -229,7 +210,7 @@
         input_output_aliases={2 + len(arrays): 0} if more else {},
         compiler_params=pltpu.CompilerParams(vmem_limit_bytes=VMEM),
         cost_estimate=pl.CostEstimate(flops=1, bytes_accessed=1, transcendentals=0),
-    )(meta, spread, *arrays, *more)
+    )(pair_count, spread, *arrays, *more)
 
 
 def after(value, *done):
@@ -258,32 +239,27 @@
     rows = lax.optimization_barrier(rows)
     own, theirs = [lax.dynamic_slice_in_dim(rows, which * half, half, 2) for which in (side, 1 - side)]
 
-    with jax.named_scope("pairs_along"):
-        site_pairs = jnp.where(row == 1, to_site(pairs), pairs)
-    with jax.named_scope("pairs_across"):
-        named = jnp.concatenate([to_partner_site(pairs), site_pairs], axis=0)
-    own, named = lax.optimization_barrier((own, named))
-
     sources = [[] for _ in range(WINDOW)]
-    swapped, beside, along = [], [], []
-    for c in range(stages):
-        with jax.named_scope(f"swap{c}"):
-            swapped.append(to_pair(after(theirs[:, c * width : (c + 1) * width], *swapped)))
+    along, beside = [], []
+    with jax.named_scope("swap"):
+        swapped = [to_pair(theirs[:, c * width : (c + 1) * width]) for c in range(stages)]
     for c in range(stages):
         for kind in range(2):
             block = (own[:, c * width : (c + 1) * width], swapped[c])[kind]
             with jax.named_scope(f"along_{kind}_{c}"):
-                along.append(to_site(after(block, *along[-2:-1])))
+                along.append(to_below(after(block, *along[-2:-1])))
+            if len(along) == 2:
+                with jax.named_scope("pairs"):
+                    named = to_pair(after(pairs, along[1]))
             with jax.named_scope(f"beside_{kind}_{c}"):
-                beside.append(to_row(after(block, *beside[-2:-1])))
+                beside.append(to_row(after(jnp.where(row == 1, block, along[-1]), *beside[-2:-1])))
             for group, array in enumerate((block, beside[-1], along[-1])):
                 sources[2 * group + kind].append((array, 0, width))
 
-    owners = lax.axis_size("src")
-    owner = jnp.where(row == 1, (me + owners - REACH) % owners, me)
-    named = jnp.clip(named - (owner & ~1), 0, WINDOW - 1)
-    group = jnp.where(row == 1, 2 - (named >> 1), named >> 1)
-    meta = jnp.concatenate([(2 * group + ((named & 1) ^ side)).reshape(-1), seg[None]]).astype(jnp.int32)
+    named = jnp.clip(jnp.concatenate([named, pairs], axis=0) - (me & ~1), 0, WINDOW - 1)
+    local = 2 * (named >> 1) + ((named & 1) ^ side)
+    meta = jnp.concatenate([local.reshape(-1), seg[None]]).astype(jnp.int32)
+    meta = after(meta, along[-1])
 
     cosine, sine = lag_tables(freqs, LAGS)
     table = jnp.concatenate([part[at : at + 1] for part in (cosine, sine) for at in (0, 4, 5)] + [cosine[:2]], axis=0)
@@ -299,35 +275,26 @@
         with jax.named_scope(f"partner_stacks_{name}"):
             return to_pair(total)
 
-    def give_back(mine, came, name):
-        total = mine + came
-        with jax.named_scope(f"stacks_back_{name}"):
-            return total, to_owner(total)
-
-    (partner,) = correlate(meta, table, sources, count, 0, width, 0, (stage_tiles(0),))
-    sent = over_all(partner, "0")
-    came = [exchange(sent, "0")]
-    meta = after(meta, sent)
-    every = stage_tiles(0) + stage_tiles(1)
-    partner, mine = correlate(meta, table, sources, count, 1, width, 0, (stage_tiles(1), every))
-    total = over_all([after(x, came[0]) for x in partner], "1")
-    lag_parts = ((0, LAGS // 2), (LAGS // 2, LAGS))
-    pieces = [(slot, *lags) for slot in range(SLOTS) for lags in lag_parts]
-    came += [exchange(total[slot : slot + 1, low:high], f"1_{slot}_{low}") for slot, low, high in pieces]
-    mine = over_all([after(x, total) for x in mine], "own")
+    (partner,) = correlate(meta, table, sources, count, 0, width, 0, ((0, None, stage_tiles(0)),))
+    total = over_all(partner, "0")
+    came = [exchange(total, "0")]
+    meta = after(meta, total)
+    tiles = stage_tiles(1)
+    groups = correlate(meta, table, sources, count, 1, width, 0, tuple((0, slot, tiles) for slot in range(SLOTS)))
+    totals = [over_all([after(x, came[0]) for x in shares], f"1_{slot}") for slot, shares in enumerate(groups)]
+    came.append(exchange(totals[0], "1_0"))
+    meta = after(meta, *totals)
+    tiles = stage_tiles(0) + tiles
+    groups = correlate(meta, table, sources, count, 1, width, SLOTS, tuple((0, None, (tile,)) for tile in tiles))
+    for slot in range(1, SLOTS):
+        came.append(exchange(after(totals[slot], came[-1], groups[0][0]), f"1_{slot}"))
+    mine = [over_all(shares, f"own_{n}") for n, shares in enumerate(groups)]
     place = jnp.arange(LAGS * width)
     spread = (place[None, :] == (place % width * LAGS + place // width)[:, None]).astype(jnp.bfloat16)
     scale = float(count * spectra.shape[1] * freqs) ** (-0.5)
-    meta = jnp.stack([row, pair_count[0]]).astype(jnp.int32)
-    first = give_back(mine[:, :, :piece], came[0], "0")
-    last = []
-    for (slot, low, high), stacks in zip(pieces, came[1:]):
-        mine = after(mine, first[0] if not last else last[-1][1])
-        last.append((low, *give_back(mine[slot : slot + 1, low:high, piece:], stacks, f"1_{slot}_{low}")))
     result = None
     for slot in range(SLOTS):
-        stacks = [[(0, *first)], last[slot * len(lag_parts) : (slot + 1) * len(lag_parts)]]
-        result = finish(meta, spread, stacks, slot, count, piece, scale, result)
+        result = finish(pair_count, spread, mine, came[:1] + came[1 + slot : 2 + slot], slot, count, piece, scale, result)
     return result
 
 

time: 132 us -> 118 us (0.89)
  the two profiles are of different devices: /device:TPU:6 before, /device:TPU:0 now
where the time goes in v3:
time: 118 us; the launch traced here: 117 us
  waiting for transfers between devices  46.4 us (39%)
  Pallas kernels  27.9 us (24%)
  starting transfers between devices  22 us (19%)
  other arithmetic  14.9 us (13%)
  local copies, waits for them, and re-layouts  5.2 us (4%)
    ppermute x6, waiting for transfers between devices, to_pair(): return lax.ppermute(value, 'src', routes('src', lambda d: d ^ 1))  25.7 us
    pallas_call x3, Pallas kernels, correlate(): pl.pallas_call(functools.partial(corr_kernel, count, stage, first, sets,...  20.9 us
    ppermute x4, waiting for transfers between devices, to_below(): return lax.ppermute(value, 'src', routes('src', lambda d: d - REACH))  15.6 us
    ppermute x6, starting transfers between devices, to_pair(): return lax.ppermute(value, 'src', routes('src', lambda d: d ^ 1))  8.97 us
    add x7, other arithmetic, over_all(): return sum(over_segments(shares, count))  8.92 us
    pallas_call x2, Pallas kernels, finish(): pl.pallas_call(functools.partial(finish_kernel, count, piece, stages, slo...  6.99 us
    ppermute x4, starting transfers between devices, to_row(): return lax.ppermute(value, 'src', routes('src', lambda d: d ^ 2))  6.19 us
    ppermute x4, starting transfers between devices, to_below(): return lax.ppermute(value, 'src', routes('src', lambda d: d - REACH))  5.25 us
  transfers between devices with their start and end apart: 21, of which 13 were waited for; matrix products, arithmetic and copies ran while one was open for 13% of the time, Pallas kernels for 21%

profile of v3, /device:TPU:0, one launch (start us, length us, event | category | flops | bytes accessed | tf_op | source)
XLA Modules:
  0.0 117.4 jit_solution(4872620476281119997)
XLA Ops:
  0.0 2.5 %copy.6 = bf16[2,2,64,2,2048]{4,2,0,1,3:T(8,128)(2,1)S(1)} copy(bf16[2,2,64,2,2048]{4,3,2,1,0:T(2,128)(2,1)} %bitcast.6) | data formatting | bytes 4194304 | tf_op jit(solution)/shard_map/reshape | solution.py:238
  3.5 2.9 %collective-permute-start = (bf16[2,128,1024]{2,1,0:T(8,128)(2,1)S(1)}, bf16[2,128,1024]{2,1,0:T(8,128)(2,1)S(1)}, u32[]{:S(2)}, u32[]{:S(2)}) collective-permute-start(bf16[2,128,1024]{2,1,0:T(8,128)(2,1)S(1)} %get-tuple-element.61), channel_id=1, source_target_pairs={{0,2},{2,0},{4,6},{6,4},{8,10},{10,8},{12,14},{14,12},{16,18},{18,... | collective-permute-start | bytes 1572872 | tf_op jit(solution)/shard_map/swap/ppermute | solution.py:24
  8.1 11.1 %collective-permute-done.refs_1_.refs_2_ = bf16[2,128,1024]{2,1,0:T(8,128)(2,1)S(1)} collective-permute-done((bf16[2,128,1024]{2,1,0:T(8,128)(2,1)S(1)}, bf16[2,128,1024]{2,1,0:T(8,128)(2,1)S(1)}, u32[]{:S(2)}, u32[]{:S(2)}) %collective-permute-start) | collective-permute-done | bytes 524320 | tf_op jit(solution)/shard_map/swap/ppermute | solution.py:24
  19.2 1.3 %collective-permute-start.1 = (bf16[2,128,1024]{2,1,0:T(8,128)(2,1)S(1)}, bf16[2,128,1024]{2,1,0:T(8,128)(2,1)S(1)}, u32[]{:S(2)}, u32[]{:S(2)}) collective-permute-start(bf16[2,128,1024]{2,1,0:T(8,128)(2,1)S(1)} %collective-permute-done.refs_1_.refs_2_), channel_id=1, source_target_pairs={{8,0},{10,2},{12,4},{14,6},{16,8},{18,10},{20,12},{22,14},{24,16},... | collective-permute-start | bytes 1572872 | tf_op jit(solution)/shard_map/along_1_0/ppermute | solution.py:32
  21.8 1.4 %collective-permute-start.9 = (bf16[2,128,1024]{2,1,0:T(8,128)(2,1)S(1)}, bf16[2,128,1024]{2,1,0:T(8,128)(2,1)S(1)}, u32[]{:S(2)}, u32[]{:S(2)}) collective-permute-start(bf16[2,128,1024]{2,1,0:T(8,128)(2,1)S(1)} %get-tuple-element.38.refs_1_), channel_id=1, source_target_pairs={{8,0},{10,2},{12,4},{14,6},{16,8},{18,10},{20,12},{22,14},{24,16},... | collective-permute-start | bytes 1572872 | tf_op jit(solution)/shard_map/along_0_1/ppermute | solution.py:32
  23.3 1.7 %collective-permute-start.6 = (bf16[2,128,1024]{2,1,0:T(8,128)(2,1)S(1)}, bf16[2,128,1024]{2,1,0:T(8,128)(2,1)S(1)}, u32[]{:S(2)}, u32[]{:S(2)}) collective-permute-start(bf16[2,128,1024]{2,1,0:T(8,128)(2,1)S(1)} %broadcast_select_fusion.3), channel_id=1, source_target_pairs={{0,4},{2,6},{4,0},{6,2},{8,12},{10,14},{12,8},{14,10},{16,20},{18,... | collective-permute-start | bytes 1572872 | tf_op jit(solution)/shard_map/beside_0_0/ppermute | solution.py:28
  25.0 4.6 %collective-permute-done.3.refs_3_ = bf16[2,128,1024]{2,1,0:T(8,128)(2,1)S(1)} collective-permute-done((bf16[2,128,1024]{2,1,0:T(8,128)(2,1)}, bf16[2,128,1024]{2,1,0:T(8,128)(2,1)S(1)}, u32[]{:S(2)}, u32[]{:S(2)}) %collective-permute-start.3) | collective-permute-done | bytes 524320 | tf_op jit(solution)/shard_map/swap/ppermute | solution.py:24
  29.6 6.5 %collective-permute-done.1.refs_5_.refs_10_ = bf16[2,128,1024]{2,1,0:T(8,128)(2,1)S(1)} collective-permute-done((bf16[2,128,1024]{2,1,0:T(8,128)(2,1)S(1)}, bf16[2,128,1024]{2,1,0:T(8,128)(2,1)S(1)}, u32[]{:S(2)}, u32[]{:S(2)}) %collective-permute-start.1) | collective-permute-done | bytes 524320 | tf_op jit(solution)/shard_map/along_1_0/ppermute | solution.py:32
  38.2 2.0 %collective-permute-start.7 = (bf16[2,128,1024]{2,1,0:T(8,128)(2,1)}, bf16[2,128,1024]{2,1,0:T(8,128)(2,1)}, u32[]{:S(2)}, u32[]{:S(2)}) collective-permute-start(bf16[2,128,1024]{2,1,0:T(8,128)(2,1)} %broadcast_select_fusion.2), channel_id=1, source_target_pairs={{0,4},{2,6},{4,0},{6,2},{8,12},{10,14},{12,8},{14,10},{16,20},{18,... | collective-permute-start | bytes 1572872 | tf_op jit(solution)/shard_map/beside_1_0/ppermute | solution.py:28
  40.1 7.2 %collective-permute-done.9.refs_9_ = bf16[2,128,1024]{2,1,0:T(8,128)(2,1)S(1)} collective-permute-done((bf16[2,128,1024]{2,1,0:T(8,128)(2,1)S(1)}, bf16[2,128,1024]{2,1,0:T(8,128)(2,1)S(1)}, u32[]{:S(2)}, u32[]{:S(2)}) %collective-permute-start.9) | collective-permute-done | bytes 524320 | tf_op jit(solution)/shard_map/along_0_1/ppermute | solution.py:32
  48.3 2.0 %collective-permute-start.10 = (bf16[2,128,1024]{2,1,0:T(8,128)(2,1)}, bf16[2,128,1024]{2,1,0:T(8,128)(2,1)}, u32[]{:S(2)}, u32[]{:S(2)}) collective-permute-start(bf16[2,128,1024]{2,1,0:T(8,128)(2,1)} %broadcast_select_fusion.1), channel_id=1, source_target_pairs={{0,4},{2,6},{4,0},{6,2},{8,12},{10,14},{12,8},{14,10},{16,20},{18,... | collective-permute-start | bytes 1572872 | tf_op jit(solution)/shard_map/beside_0_1/ppermute | solution.py:28
  50.3 1.5 %collective-permute-start.2 = (s32[2,2]{1,0:T(2,128)S(1)}, s32[2,2]{1,0:T(2,128)S(1)}, u32[]{:S(2)}, u32[]{:S(2)}) collective-permute-start(s32[2,2]{1,0:T(2,128)S(1)} %copy-done.13), channel_id=1, source_target_pairs={{0,2},{2,0},{4,6},{6,4},{8,10},{10,8},{12,14},{14,12},{16,18},{18,... | collective-permute-start | bytes 56 | tf_op jit(solution)/shard_map/pairs/ppermute | solution.py:24
  51.8 2.1 %collective-permute-done.2 = s32[2,2]{1,0:T(2,128)S(1)} collective-permute-done((s32[2,2]{1,0:T(2,128)S(1)}, s32[2,2]{1,0:T(2,128)S(1)}, u32[]{:S(2)}, u32[]{:S(2)}) %collective-permute-start.2) | collective-permute-done | bytes 48 | tf_op jit(solution)/shard_map/pairs/ppermute | solution.py:24
  54.6 1.4 %collective-permute-done.4.refs_11_ = bf16[2,128,1024]{2,1,0:T(8,128)(2,1)} collective-permute-done((bf16[2,128,1024]{2,1,0:T(8,128)(2,1)S(1)}, bf16[2,128,1024]{2,1,0:T(8,128)(2,1)}, u32[]{:S(2)}, u32[]{:S(2)}) %collective-permute-start.4) | collective-permute-done | bytes 524320 | tf_op jit(solution)/shard_map/along_1_1/ppermute | solution.py:32
  55.9 1.9 %broadcast_select_fusion = bf16[2,128,1024]{2,1,0:T(8,128)(2,1)} fusion(bf16[2,128,1024]{2,1,0:T(8,128)(2,1)S(1)} %collective-permute-done.3.refs_3_, bf16[2,128,1024]{2,1,0:T(8,128)(2,1)} %collective-permute-done.4.refs_11_, pred[]{:T(512)S(6)} %eq.32), kind=kLoop, calls=%fused_computation.2 | loop fusion | flops 262144 | bytes 1572865 | tf_op jit(solution)/shard_map/beside_1_1/jit(_where)/select_n | solution.py:255
  58.3 4.9 %shard_map.37 = (f32[2,6,64,128]{3,2,1,0:T(8,128)}, f32[2,6,64,128]{3,2,1,0:T(8,128)}) custom-call(s32[9]{0:T(128)} %pad_add_fusion.meta, f32[8,1024]{1,0:T(8,128)} %constant_dynamic-slice_fusion.3.table, bf16[2,128,1024]{2,1,0:T(8,128)(2,1)} %copy-done.1, bf16[2,128,1024]{2,1,0:T(8,128)(2,1)} %copy-done.5, bf16[2,128,1024]{2,1,0:T(8,128)(2,1)} %copy-done.14, ...), custom_call_target="tpu_custom_call" | custom-call | flops 9999999827968 | bytes 10000000000 | tf_op jit(solution)/shard_map/pallas_call | solution.py:151
  63.4 1.9 %collective-permute-done.8 = f32[2,6,64,128]{3,2,1,0:T(8,128)S(1)} collective-permute-done((f32[2,6,64,128]{3,2,1,0:T(8,128)}, f32[2,6,64,128]{3,2,1,0:T(8,128)S(1)}, u32[]{:S(2)}, u32[]{:S(2)}) %collective-permute-start.8) | collective-permute-done | bytes 393248 | tf_op jit(solution)/shard_map/segments_0/ppermute | solution.py:223
  65.3 1.8 %add.83 = f32[2,6,64,128]{3,2,1,0:T(8,128)} add(f32[2,6,64,128]{3,2,1,0:T(8,128)} %get-tuple-element.35, f32[2,6,64,128]{3,2,1,0:T(8,128)S(1)} %collective-permute-done.8) | non-fusion elementwise | flops 98304 | bytes 1179648 | tf_op jit(solution)/shard_map/segments_0/add | solution.py:272
  67.1 1.5 %collective-permute-start.12 = (f32[2,6,64,128]{3,2,1,0:T(8,128)}, f32[2,6,64,128]{3,2,1,0:T(8,128)}, u32[]{:S(2)}, u32[]{:S(2)}) collective-permute-start(f32[2,6,64,128]{3,2,1,0:T(8,128)} %add.83), channel_id=1, source_target_pairs={{0,2},{2,0},{4,6},{6,4},{8,10},{10,8},{12,14},{14,12},{16,18},{18,... | collective-permute-start | bytes 1179656 | tf_op jit(solution)/shard_map/partner_stacks_0/ppermute | solution.py:24
  68.6 1.6 %collective-permute-done.11.refs_7_ = bf16[2,128,1024]{2,1,0:T(8,128)(2,1)} collective-permute-done((bf16[2,128,1024]{2,1,0:T(8,128)(2,1)}, bf16[2,128,1024]{2,1,0:T(8,128)(2,1)}, u32[]{:S(2)}, u32[]{:S(2)}) %collective-permute-start.11) | collective-permute-done | bytes 524320 | tf_op jit(solution)/shard_map/beside_1_1/ppermute | solution.py:28
  70.2 7.9 %shard_map.38 = (f32[1,6,192,128]{3,2,1,0:T(8,128)}, f32[1,6,192,128]{3,2,1,0:T(8,128)}, f32[1,6,192,128]{3,2,1,0:T(8,128)}, f32[1,6,192,128]{3,2,1,0:T(8,128)}) custom-call(s32[9]{0:T(128)} %pad_add_fusion.meta, f32[8,1024]{1,0:T(8,128)} %constant_dynamic-slice_fusion.3.table, bf16[2,128,1024]{2,1,0:T(8,128)(2,1)} %copy-done.1, ...), custom_call_target="tpu_custom_call" | custom-call | flops 9999999827968 | bytes 10000000000 | tf_op jit(solution)/shard_map/pallas_call | solution.py:151
  79.1 1.7 %collective-permute-done.13 = f32[1,6,192,128]{3,2,1,0:T(8,128)S(1)} collective-permute-done((f32[1,6,192,128]{3,2,1,0:T(8,128)}, f32[1,6,192,128]{3,2,1,0:T(8,128)S(1)}, u32[]{:S(2)}, u32[]{:S(2)}) %collective-permute-start.13) | collective-permute-done | bytes 589856 | tf_op jit(solution)/shard_map/segments_1_0/ppermute | solution.py:223
  80.8 2.0 %add.84 = f32[1,6,192,128]{3,2,1,0:T(8,128)} add(f32[1,6,192,128]{3,2,1,0:T(8,128)} %get-tuple-element.42, f32[1,6,192,128]{3,2,1,0:T(8,128)S(1)} %collective-permute-done.13) | non-fusion elementwise | flops 147456 | bytes 1769472 | tf_op jit(solution)/shard_map/segments_1_0/add | solution.py:272
  82.8 1.5 %collective-permute-start.19 = (f32[1,6,192,128]{3,2,1,0:T(8,128)}, f32[1,6,192,128]{3,2,1,0:T(8,128)}, u32[]{:S(2)}, u32[]{:S(2)}) collective-permute-start(f32[1,6,192,128]{3,2,1,0:T(8,128)} %add.84), channel_id=1, source_target_pairs={{0,2},{2,0},{4,6},{6,4},{8,10},{10,8},{12,14},{14,12},{16,18},{18,... | collective-permute-start | bytes 1769480 | tf_op jit(solution)/shard_map/partner_stacks_1_0/ppermute | solution.py:24
  85.2 8.1 %shard_map.39 = (f32[2,6,64,128]{3,2,1,0:T(8,128)}, f32[2,6,64,128]{3,2,1,0:T(8,128)}, f32[2,6,64,128]{3,2,1,0:T(8,128)}, f32[2,6,64,128]{3,2,1,0:T(8,128)}, f32...) custom-call(s32[9]{0:T(128)} %pad_add_fusion.meta, ...), custom_call_target="tpu_custom_call" | custom-call | flops 9999999827968 | bytes 10000000000 | tf_op jit(solution)/shard_map/pallas_call | solution.py:151
  93.3 5.2 %collective-permute-done.19.refs_5_ = f32[1,6,192,128]{3,2,1,0:T(8,128)} collective-permute-done((f32[1,6,192,128]{3,2,1,0:T(8,128)}, f32[1,6,192,128]{3,2,1,0:T(8,128)}, u32[]{:S(2)}, u32[]{:S(2)}) %collective-permute-start.19) | collective-permute-done | bytes 589856 | tf_op jit(solution)/shard_map/partner_stacks_1_0/ppermute | solution.py:24
  98.5 1.5 %collective-permute-start.20 = (f32[1,6,192,128]{3,2,1,0:T(8,128)S(1)}, f32[1,6,192,128]{3,2,1,0:T(8,128)S(1)}, u32[]{:S(2)}, u32[]{:S(2)}) collective-permute-start(f32[1,6,192,128]{3,2,1,0:T(8,128)S(1)} %copy-done.2), channel_id=1, source_target_pairs={{0,2},{2,0},{4,6},{6,4},{8,10},{10,8},{12,14},{14,12},{16,18},{18,... | collective-permute-start | bytes 1769480 | tf_op jit(solution)/shard_map/partner_stacks_1_1/ppermute | solution.py:24
  101.7 1.3 %fusion.spread = bf16[768,768]{1,0:T(8,128)(2,1)} fusion(s32[768]{0:T(1024)S(1)} %fusion.15), kind=kLoop, calls=%fused_computation.1 | loop fusion | flops 1179648 | bytes 1182720 | tf_op jit(solution)/shard_map/convert_element_type | solution.py:293
  103.0 1.8 %add.86.refs_0_ = f32[2,6,64,128]{3,2,1,0:T(8,128)} add(f32[2,6,64,128]{3,2,1,0:T(8,128)} %get-tuple-element.50, f32[2,6,64,128]{3,2,1,0:T(8,128)S(1)} %collective-permute-done.15) | non-fusion elementwise | flops 98304 | bytes 1179648 | tf_op jit(solution)/shard_map/segments_own_0/add | solution.py:272
  107.3 3.5 %shard_map.40.refs_6_ = f32[2,128,1536]{2,1,0:T(8,128)} custom-call(s32[1]{0:T(128)S(6)} %copy.8.pair_count, bf16[768,768]{1,0:T(8,128)(2,1)} %fusion.spread, f32[2,6,64,128]{3,2,1,0:T(8,128)} %add.86.refs_0_, f32[2,6,64,128]{3,2,1,0:T(8,128)} %add.87.refs_1_, f32[2,6,64,128]{3,2,1,0:T(8,128)} %add.88.refs_2_, f32[2,6,64,128]{3,2,1,0:T(8,128)} %add.89.refs_3_, ...), custom_call_target="tpu_custom_call" | custom-call | flops 1 | bytes 1 | tf_op jit(solution)/shard_map/pallas_call | solution.py:202
  110.7 2.3 %collective-permute-done.20.refs_5_ = f32[1,6,192,128]{3,2,1,0:T(8,128)S(1)} collective-permute-done((f32[1,6,192,128]{3,2,1,0:T(8,128)S(1)}, f32[1,6,192,128]{3,2,1,0:T(8,128)S(1)}, u32[]{:S(2)}, u32[]{:S(2)}) %collective-permute-start.20) | collective-permute-done | bytes 589856 | tf_op jit(solution)/shard_map/partner_stacks_1_1/ppermute | solution.py:24
  113.9 3.5 %shard_map.41 = f32[2,128,1536]{2,1,0:T(8,128)} custom-call(s32[1]{0:T(128)S(6)} %copy.8.pair_count, bf16[768,768]{1,0:T(8,128)(2,1)} %fusion.spread, f32[2,6,64,128]{3,2,1,0:T(8,128)} %add.86.refs_0_, f32[2,6,64,128]{3,2,1,0:T(8,128)} %add.87.refs_1_, f32[2,6,64,128]{3,2,1,0:T(8,128)} %add.88.refs_2_, ...), custom_call_target="tpu_custom_call", output_to_operand_aliasing={{}: (8, {})} | custom-call | flops 1 | bytes 1 | tf_op jit(solution)/shard_map/pallas_call | solution.py:202
  (71 shorter events, 14.5 us)
Async XLA Ops:
  3.5 44.7 %copy-start = (bf16[2,128,1024]{2,1,0:T(8,128)(2,1)}, bf16[2,128,1024]{2,1,0:T(8,128)(2,1)S(1)}, u32[]{:S(2)}) copy-start(bf16[2,128,1024]{2,1,0:T(8,128)(2,1)S(1)} %get-tuple-element.38.refs_1_) | copy-start | bytes 1572868
  3.5 44.7 %copy-start.1 = (bf16[2,128,1024]{2,1,0:T(8,128)(2,1)}, bf16[2,128,1024]{2,1,0:T(8,128)(2,1)S(1)}, u32[]{:S(2)}) copy-start(bf16[2,128,1024]{2,1,0:T(8,128)(2,1)S(1)} %get-tuple-element.60.refs_0_) | copy-start | bytes 1572868
  3.5 15.7 %collective-permute-start = (bf16[2,128,1024]{2,1,0:T(8,128)(2,1)S(1)}, bf16[2,128,1024]{2,1,0:T(8,128)(2,1)S(1)}, u32[]{:S(2)}, u32[]{:S(2)}) collective-permute-start(bf16[2,128,1024]{2,1,0:T(8,128)(2,1)S(1)} %get-tuple-element.61), channel_id=1, source_target_pairs={{0,2},{2,0},{4,6},{6,4},{8,10},{10,8},{12,14},{14,12},{16,18},{18,... | collective-permute-start | bytes 1572872 | tf_op jit(solution)/shard_map/swap/ppermute | solution.py:24
  6.4 23.2 %collective-permute-start.3 = (bf16[2,128,1024]{2,1,0:T(8,128)(2,1)}, bf16[2,128,1024]{2,1,0:T(8,128)(2,1)S(1)}, u32[]{:S(2)}, u32[]{:S(2)}) collective-permute-start(bf16[2,128,1024]{2,1,0:T(8,128)(2,1)} %get-tuple-element.62), channel_id=1, source_target_pairs={{0,2},{2,0},{4,6},{6,4},{8,10},{10,8},{12,14},{14,12},{16,18},{18,... | collective-permute-start | bytes 1572872 | tf_op jit(solution)/shard_map/swap/ppermute | solution.py:24
  6.5 15.3 %collective-permute-start.5 = (bf16[2,128,1024]{2,1,0:T(8,128)(2,1)S(1)}, bf16[2,128,1024]{2,1,0:T(8,128)(2,1)S(1)}, u32[]{:S(2)}, u32[]{:S(2)}) collective-permute-start(bf16[2,128,1024]{2,1,0:T(8,128)(2,1)S(1)} %get-tuple-element.60.refs_0_), channel_id=1, source_target_pairs={{8,0},{10,2},{12,4},{14,6},{16,8},{18,10},{20,12},{22,14},{24,16},... | collective-permute-start | bytes 1572872 | tf_op jit(solution)/shard_map/along_0_0/ppermute | solution.py:32
  19.2 29.1 %copy-start.5 = (bf16[2,128,1024]{2,1,0:T(8,128)(2,1)}, bf16[2,128,1024]{2,1,0:T(8,128)(2,1)S(1)}, u32[]{:S(2)}) copy-start(bf16[2,128,1024]{2,1,0:T(8,128)(2,1)S(1)} %collective-permute-done.refs_1_.refs_2_) | copy-start | bytes 1572868
  19.2 16.9 %collective-permute-start.1 = (bf16[2,128,1024]{2,1,0:T(8,128)(2,1)S(1)}, bf16[2,128,1024]{2,1,0:T(8,128)(2,1)S(1)}, u32[]{:S(2)}, u32[]{:S(2)}) collective-permute-start(bf16[2,128,1024]{2,1,0:T(8,128)(2,1)S(1)} %collective-permute-done.refs_1_.refs_2_), channel_id=1, source_target_pairs={{8,0},{10,2},{12,4},{14,6},{16,8},{18,10},{20,12},{22,14},{24,16},... | collective-permute-start | bytes 1572872 | tf_op jit(solution)/shard_map/along_1_0/ppermute | solution.py:32
  21.8 26.4 %copy-start.7 = (bf16[2,128,1024]{2,1,0:T(8,128)(2,1)}, bf16[2,128,1024]{2,1,0:T(8,128)(2,1)S(1)}, u32[]{:S(2)}) copy-start(bf16[2,128,1024]{2,1,0:T(8,128)(2,1)S(1)} %collective-permute-done.5.refs_4_.refs_8_) | copy-start | bytes 1572868
  21.8 28.5 %copy-start.13 = (s32[2,2]{1,0:T(2,128)S(1)}, s32[2,2]{1,0:T(2,128)}, u32[]{:S(2)}) copy-start(s32[2,2]{1,0:T(2,128)} %param.4) | copy-start | bytes 52
  21.8 25.5 %collective-permute-start.9 = (bf16[2,128,1024]{2,1,0:T(8,128)(2,1)S(1)}, bf16[2,128,1024]{2,1,0:T(8,128)(2,1)S(1)}, u32[]{:S(2)}, u32[]{:S(2)}) collective-permute-start(bf16[2,128,1024]{2,1,0:T(8,128)(2,1)S(1)} %get-tuple-element.38.refs_1_), channel_id=1, source_target_pairs={{8,0},{10,2},{12,4},{14,6},{16,8},{18,10},{20,12},{22,14},{24,16},... | collective-permute-start | bytes 1572872 | tf_op jit(solution)/shard_map/along_0_1/ppermute | solution.py:32
  23.3 25.0 %collective-permute-start.6 = (bf16[2,128,1024]{2,1,0:T(8,128)(2,1)S(1)}, bf16[2,128,1024]{2,1,0:T(8,128)(2,1)S(1)}, u32[]{:S(2)}, u32[]{:S(2)}) collective-permute-start(bf16[2,128,1024]{2,1,0:T(8,128)(2,1)S(1)} %broadcast_select_fusion.3), channel_id=1, source_target_pairs={{0,4},{2,6},{4,0},{6,2},{8,12},{10,14},{12,8},{14,10},{16,20},{18,... | collective-permute-start | bytes 1572872 | tf_op jit(solution)/shard_map/beside_0_0/ppermute | solution.py:28
  29.6 28.2 %copy-start.6 = (bf16[2,128,1024]{2,1,0:T(8,128)(2,1)}, bf16[2,128,1024]{2,1,0:T(8,128)(2,1)S(1)}, u32[]{:S(2)}) copy-start(bf16[2,128,1024]{2,1,0:T(8,128)(2,1)S(1)} %collective-permute-done.3.refs_3_) | copy-start | bytes 1572868
  36.1 21.8 %copy-start.8 = (bf16[2,128,1024]{2,1,0:T(8,128)(2,1)}, bf16[2,128,1024]{2,1,0:T(8,128)(2,1)S(1)}, u32[]{:S(2)}) copy-start(bf16[2,128,1024]{2,1,0:T(8,128)(2,1)S(1)} %collective-permute-done.1.refs_5_.refs_10_) | copy-start | bytes 1572868
  36.1 19.9 %collective-permute-start.4 = (bf16[2,128,1024]{2,1,0:T(8,128)(2,1)S(1)}, bf16[2,128,1024]{2,1,0:T(8,128)(2,1)}, u32[]{:S(2)}, u32[]{:S(2)}) collective-permute-start(bf16[2,128,1024]{2,1,0:T(8,128)(2,1)S(1)} %collective-permute-done.3.refs_3_), channel_id=1, source_target_pairs={{8,0},{10,2},{12,4},{14,6},{16,8},{18,10},{20,12},{22,14},{24,16},... | collective-permute-start | bytes 1572872 | tf_op jit(solution)/shard_map/along_1_1/ppermute | solution.py:32
  38.2 19.6 %collective-permute-start.7 = (bf16[2,128,1024]{2,1,0:T(8,128)(2,1)}, bf16[2,128,1024]{2,1,0:T(8,128)(2,1)}, u32[]{:S(2)}, u32[]{:S(2)}) collective-permute-start(bf16[2,128,1024]{2,1,0:T(8,128)(2,1)} %broadcast_select_fusion.2), channel_id=1, source_target_pairs={{0,4},{2,6},{4,0},{6,2},{8,12},{10,14},{12,8},{14,10},{16,20},{18,... | collective-permute-start | bytes 1572872 | tf_op jit(solution)/shard_map/beside_1_0/ppermute | solution.py:28
  48.3 20.3 %collective-permute-start.10 = (bf16[2,128,1024]{2,1,0:T(8,128)(2,1)}, bf16[2,128,1024]{2,1,0:T(8,128)(2,1)}, u32[]{:S(2)}, u32[]{:S(2)}) collective-permute-start(bf16[2,128,1024]{2,1,0:T(8,128)(2,1)} %broadcast_select_fusion.1), channel_id=1, source_target_pairs={{0,4},{2,6},{4,0},{6,2},{8,12},{10,14},{12,8},{14,10},{16,20},{18,... | collective-permute-start | bytes 1572872 | tf_op jit(solution)/shard_map/beside_0_1/ppermute | solution.py:28
  50.3 3.6 %collective-permute-start.2 = (s32[2,2]{1,0:T(2,128)S(1)}, s32[2,2]{1,0:T(2,128)S(1)}, u32[]{:S(2)}, u32[]{:S(2)}) collective-permute-start(s32[2,2]{1,0:T(2,128)S(1)} %copy-done.13), channel_id=1, source_target_pairs={{0,2},{2,0},{4,6},{6,4},{8,10},{10,8},{12,14},{14,12},{16,18},{18,... | collective-permute-start | bytes 56 | tf_op jit(solution)/shard_map/pairs/ppermute | solution.py:24
  57.8 12.3 %collective-permute-start.11 = (bf16[2,128,1024]{2,1,0:T(8,128)(2,1)}, bf16[2,128,1024]{2,1,0:T(8,128)(2,1)}, u32[]{:S(2)}, u32[]{:S(2)}) collective-permute-start(bf16[2,128,1024]{2,1,0:T(8,128)(2,1)} %broadcast_select_fusion), channel_id=1, source_target_pairs={{0,4},{2,6},{4,0},{6,2},{8,12},{10,14},{12,8},{14,10},{16,20},{18,... | collective-permute-start | bytes 1572872 | tf_op jit(solution)/shard_map/beside_1_1/ppermute | solution.py:28
  63.3 2.0 %collective-permute-start.8 = (f32[2,6,64,128]{3,2,1,0:T(8,128)}, f32[2,6,64,128]{3,2,1,0:T(8,128)S(1)}, u32[]{:S(2)}, u32[]{:S(2)}) collective-permute-start(f32[2,6,64,128]{3,2,1,0:T(8,128)} %get-tuple-element.36), channel_id=1, source_target_pairs={{0,1},{1,0},{2,3},{3,2},{4,5},{5,4},{6,7},{7,6},{8,9},{9,8},{10,11... | collective-permute-start | bytes 1179656 | tf_op jit(solution)/shard_map/segments_0/ppermute | solution.py:223
  67.1 11.5 %collective-permute-start.12 = (f32[2,6,64,128]{3,2,1,0:T(8,128)}, f32[2,6,64,128]{3,2,1,0:T(8,128)}, u32[]{:S(2)}, u32[]{:S(2)}) collective-permute-start(f32[2,6,64,128]{3,2,1,0:T(8,128)} %add.83), channel_id=1, source_target_pairs={{0,2},{2,0},{4,6},{6,4},{8,10},{10,8},{12,14},{14,12},{16,18},{18,... | collective-permute-start | bytes 1179656 | tf_op jit(solution)/shard_map/partner_stacks_0/ppermute | solution.py:24
  78.1 6.2 %copy-start.3 = (f32[1,6,192,128]{3,2,1,0:T(8,128)S(1)}, f32[1,6,192,128]{3,2,1,0:T(8,128)}, u32[]{:S(2)}) copy-start(f32[1,6,192,128]{3,2,1,0:T(8,128)} %get-tuple-element.46) | copy-start | bytes 1769476
  78.6 2.2 %collective-permute-start.13 = (f32[1,6,192,128]{3,2,1,0:T(8,128)}, f32[1,6,192,128]{3,2,1,0:T(8,128)S(1)}, u32[]{:S(2)}, u32[]{:S(2)}) collective-permute-start(f32[1,6,192,128]{3,2,1,0:T(8,128)} %get-tuple-element.44), channel_id=1, source_target_pairs={{0,1},{1,0},{2,3},{3,2},{4,5},{5,4},{6,7},{7,6},{8,9},{9,8},{10,11... | collective-permute-start | bytes 1769480 | tf_op jit(solution)/shard_map/segments_1_0/ppermute | solution.py:223
  78.6 5.7 %collective-permute-start.14 = (f32[1,6,192,128]{3,2,1,0:T(8,128)}, f32[1,6,192,128]{3,2,1,0:T(8,128)S(1)}, u32[]{:S(2)}, u32[]{:S(2)}) collective-permute-start(f32[1,6,192,128]{3,2,1,0:T(8,128)} %get-tuple-element.48), channel_id=1, source_target_pairs={{0,1},{1,0},{2,3},{3,2},{4,5},{5,4},{6,7},{7,6},{8,9},{9,8},{10,11... | collective-permute-start | bytes 1769480 | tf_op jit(solution)/shard_map/segments_1_1/ppermute | solution.py:223
  82.8 15.7 %collective-permute-start.19 = (f32[1,6,192,128]{3,2,1,0:T(8,128)}, f32[1,6,192,128]{3,2,1,0:T(8,128)}, u32[]{:S(2)}, u32[]{:S(2)}) collective-permute-start(f32[1,6,192,128]{3,2,1,0:T(8,128)} %add.84), channel_id=1, source_target_pairs={{0,2},{2,0},{4,6},{6,4},{8,10},{10,8},{12,14},{14,12},{16,18},{18,... | collective-permute-start | bytes 1769480 | tf_op jit(solution)/shard_map/partner_stacks_1_0/ppermute | solution.py:24
  85.2 13.3 %copy-start.2 = (f32[1,6,192,128]{3,2,1,0:T(8,128)S(1)}, f32[1,6,192,128]{3,2,1,0:T(8,128)}, u32[]{:S(2)}) copy-start(f32[1,6,192,128]{3,2,1,0:T(8,128)} %add.85) | copy-start | bytes 1769476
  93.3 11.5 %copy-start.12 = (f32[2,6,64,128]{3,2,1,0:T(8,128)S(1)}, f32[2,6,64,128]{3,2,1,0:T(8,128)}, u32[]{:S(2)}) copy-start(f32[2,6,64,128]{3,2,1,0:T(8,128)} %get-tuple-element.56) | copy-start | bytes 1179652
  93.3 12.4 %copy-start.11 = (f32[2,6,64,128]{3,2,1,0:T(8,128)S(1)}, f32[2,6,64,128]{3,2,1,0:T(8,128)}, u32[]{:S(2)}) copy-start(f32[2,6,64,128]{3,2,1,0:T(8,128)} %get-tuple-element.54) | copy-start | bytes 1179652
  98.5 14.5 %collective-permute-start.20 = (f32[1,6,192,128]{3,2,1,0:T(8,128)S(1)}, f32[1,6,192,128]{3,2,1,0:T(8,128)S(1)}, u32[]{:S(2)}, u32[]{:S(2)}) collective-permute-start(f32[1,6,192,128]{3,2,1,0:T(8,128)S(1)} %copy-done.2), channel_id=1, source_target_pairs={{0,2},{2,0},{4,6},{6,4},{8,10},{10,8},{12,14},{14,12},{16,18},{18,... | collective-permute-start | bytes 1769480 | tf_op jit(solution)/shard_map/partner_stacks_1_1/ppermute | solution.py:24
  100.0 3.0 %collective-permute-start.15 = (f32[2,6,64,128]{3,2,1,0:T(8,128)}, f32[2,6,64,128]{3,2,1,0:T(8,128)S(1)}, u32[]{:S(2)}, u32[]{:S(2)}) collective-permute-start(f32[2,6,64,128]{3,2,1,0:T(8,128)} %get-tuple-element.51), channel_id=1, source_target_pairs={{0,1},{1,0},{2,3},{3,2},{4,5},{5,4},{6,7},{7,6},{8,9},{9,8},{10,11... | collective-permute-start | bytes 1179656 | tf_op jit(solution)/shard_map/segments_own_0/ppermute | solution.py:223
  100.0 4.8 %collective-permute-start.18 = (f32[2,6,64,128]{3,2,1,0:T(8,128)}, f32[2,6,64,128]{3,2,1,0:T(8,128)S(1)}, u32[]{:S(2)}, u32[]{:S(2)}) collective-permute-start(f32[2,6,64,128]{3,2,1,0:T(8,128)} %get-tuple-element.57), channel_id=1, source_target_pairs={{0,1},{1,0},{2,3},{3,2},{4,5},{5,4},{6,7},{7,6},{8,9},{9,8},{10,11... | collective-permute-start | bytes 1179656 | tf_op jit(solution)/shard_map/segments_own_3/ppermute | solution.py:223
  100.5 5.1 %collective-permute-start.17 = (f32[2,6,64,128]{3,2,1,0:T(8,128)}, f32[2,6,64,128]{3,2,1,0:T(8,128)S(1)}, u32[]{:S(2)}, u32[]{:S(2)}) collective-permute-start(f32[2,6,64,128]{3,2,1,0:T(8,128)} %get-tuple-element.55), channel_id=1, source_target_pairs={{0,1},{1,0},{2,3},{3,2},{4,5},{5,4},{6,7},{7,6},{8,9},{9,8},{10,11... | collective-permute-start | bytes 1179656 | tf_op jit(solution)/shard_map/segments_own_2/ppermute | solution.py:223
  100.5 5.9 %collective-permute-start.16 = (f32[2,6,64,128]{3,2,1,0:T(8,128)}, f32[2,6,64,128]{3,2,1,0:T(8,128)S(1)}, u32[]{:S(2)}, u32[]{:S(2)}) collective-permute-start(f32[2,6,64,128]{3,2,1,0:T(8,128)} %get-tuple-element.53), channel_id=1, source_target_pairs={{0,1},{1,0},{2,3},{3,2},{4,5},{5,4},{6,7},{7,6},{8,9},{9,8},{10,11... | collective-permute-start | bytes 1179656 | tf_op jit(solution)/shard_map/segments_own_1/ppermute | solution.py:223
  (4 other events, 12.2 us)

commit v4 on v3

--- a/solution.py
+++ b/solution.py
@@ -170,14 +170,17 @@
     return [outs[n * count : (n + 1) * count] for n in range(len(sets))]
 
 
-def finish_kernel(count, piece, stages, slot, scale, pair_count, spread, *refs):
+def finish_kernel(count, piece, layout, slot, scale, pair_count, spread, *refs):
     out = refs[-1]
+    stages = len(layout)
     tiles = [(stage, t, a, b) for stage in range(stages) for t, (a, b) in enumerate(stage_tiles(stage))]
-    own, came = refs[: len(tiles)], refs[len(tiles) : len(tiles) + stages]
+    own, came = refs[: len(tiles) // 2], refs[len(tiles) // 2 :]
     high, low = [], []
     for n, (stage, t, _, _) in enumerate(tiles):
         at = slice(t * piece, (t + 1) * piece)
-        total = jnp.concatenate([own[n][0, lag] + came[stage][0, lag, at] for lag in range(LAGS)], axis=1)
+        rows = slice(n % 2 * piece, (n % 2 + 1) * piece)
+        lags = [own[n // 2][0, lag, rows] + came[ref][0, lag - first, at] for lag, (ref, first) in enumerate(layout[stage])]
+        total = jnp.concatenate(lags, axis=1)
         top = total.astype(jnp.bfloat16)
         high.append(top)
         low.append((total - top.astype(jnp.float32)).astype(jnp.bfloat16))
@@ -195,12 +198,17 @@
 
 def finish(pair_count, spread, own, came, slot, count, piece, scale, result):
     stages = len(came)
-    arrays = [*own, *came]
+    arrays, layout = [*own], []
+    for pieces in came:
+        layout.append([])
+        for first, array in pieces:
+            layout[-1] += [(len(arrays) - len(own), first)] * array.shape[1]
+            arrays.append(array)
     shape = (SLOTS, stages * piece, stages * piece * count * LAGS)
     specs = [pl.BlockSpec((1,) + x.shape[1:], lambda i, at=min(slot, x.shape[0] - 1): (at, 0, 0, 0)) for x in arrays]
     more = [] if result is None else [result]
     return pl.pallas_call(
-        functools.partial(finish_kernel, count, piece, stages, slot, scale),
+        functools.partial(finish_kernel, count, piece, layout, slot, scale),
         out_shape=jax.ShapeDtypeStruct(shape, jnp.float32),
         grid=(1,),
         in_specs=[pl.BlockSpec(memory_space=pltpu.SMEM), pl.BlockSpec(memory_space=pltpu.VMEM)]
@@ -285,16 +293,18 @@
     came.append(exchange(totals[0], "1_0"))
     meta = after(meta, *totals)
     tiles = stage_tiles(0) + tiles
-    groups = correlate(meta, table, sources, count, 1, width, SLOTS, tuple((0, None, (tile,)) for tile in tiles))
-    for slot in range(1, SLOTS):
-        came.append(exchange(after(totals[slot], came[-1], groups[0][0]), f"1_{slot}"))
+    groups = correlate(meta, table, sources, count, 1, width, SLOTS, tuple((0, None, tiles[n : n + 2]) for n in range(0, len(tiles), 2)))
+    half_lags = LAGS // 2
+    total = after(totals[1], groups[0][0])
+    halves = [exchange(total[:, :half_lags], "1_1a"), exchange(after(total[:, half_lags:], came[1]), "1_1b")]
+    arrived = [[(0, came[0])], [(0, came[1])]], [[(0, came[0])], [(0, halves[0]), (half_lags, halves[1])]]
     mine = [over_all(shares, f"own_{n}") for n, shares in enumerate(groups)]
     place = jnp.arange(LAGS * width)
     spread = (place[None, :] == (place % width * LAGS + place // width)[:, None]).astype(jnp.bfloat16)
     scale = float(count * spectra.shape[1] * freqs) ** (-0.5)
     result = None
     for slot in range(SLOTS):
-        result = finish(pair_count, spread, mine, came[:1] + came[1 + slot : 2 + slot], slot, count, piece, scale, result)
+        result = finish(pair_count, spread, mine, arrived[slot], slot, count, piece, scale, result)
     return result
 
 

time: 118 us -> 116 us (0.983)
  other arithmetic: 14.9 us -> 12.6 us
    add x7 -> x5, other arithmetic: 8.92 us -> 6.62 us  [over_all(): return sum(over_segments(shares, count))]
    ppermute x6 -> x7, starting transfers between devices: 8.97 us -> 10.5 us  [to_pair(): return lax.ppermute(value, 'src', routes('src', lambda d: d ^ 1))]
    ppermute x6 -> x7, waiting for transfers between devices: 25.7 us -> 25 us  [to_pair(): return lax.ppermute(value, 'src', routes('src', lambda d: d ^ 1))]
    ppermute x7 -> x5, waiting for transfers between devices: 3.64 us -> 3.63 us  [over_segments(): lax.ppermute(shares[k], 'seg', routes('seg', lambda i: (i + k) % count))]
  transfers between devices with their start and end apart: 21 -> 20, of which waited for: 13 -> 13; matrix products, arithmetic and copies ran while one was open for 13% -> 12% of each run, Pallas kernels for 21% -> 21%
where the time goes in v4:
time: 116 us; the launch traced here: 115 us
  waiting for transfers between devices  45.5 us (39%)
  Pallas kernels  28.2 us (24%)
  starting transfers between devices  23.1 us (20%)
  other arithmetic  12.6 us (11%)
  local copies, waits for them, and re-layouts  5.12 us (4%)
    ppermute x7, waiting for transfers between devices, to_pair(): return lax.ppermute(value, 'src', routes('src', lambda d: d ^ 1))  25 us
    pallas_call x3, Pallas kernels, correlate(): pl.pallas_call(functools.partial(corr_kernel, count, stage, first, sets,...  21.3 us
    ppermute x4, waiting for transfers between devices, to_below(): return lax.ppermute(value, 'src', routes('src', lambda d: d - REACH))  15.5 us
    ppermute x7, starting transfers between devices, to_pair(): return lax.ppermute(value, 'src', routes('src', lambda d: d ^ 1))  10.5 us
    pallas_call x2, Pallas kernels, finish(): pl.pallas_call(functools.partial(finish_kernel, count, piece, layout, slo...  6.82 us
    add x5, other arithmetic, over_all(): return sum(over_segments(shares, count))  6.62 us
    ppermute x4, starting transfers between devices, to_row(): return lax.ppermute(value, 'src', routes('src', lambda d: d ^ 2))  6.2 us
    ppermute x4, starting transfers between devices, to_below(): return lax.ppermute(value, 'src', routes('src', lambda d: d - REACH))  5.25 us
  transfers between devices with their start and end apart: 20, of which 13 were waited for; matrix products, arithmetic and copies ran while one was open for 12% of the time, Pallas kernels for 21%

profile of v4, /device:TPU:0, one launch (start us, length us, event | category | flops | bytes accessed | tf_op | source)
XLA Modules:
  0.0 115.5 jit_solution(13819279379491251745)
XLA Ops:
  0.0 2.5 %copy.6 = bf16[2,2,64,2,2048]{4,2,0,1,3:T(8,128)(2,1)S(1)} copy(bf16[2,2,64,2,2048]{4,3,2,1,0:T(2,128)(2,1)} %bitcast.6) | data formatting | bytes 4194304 | tf_op jit(solution)/shard_map/reshape | solution.py:246
  3.5 2.9 %collective-permute-start = (bf16[2,128,1024]{2,1,0:T(8,128)(2,1)S(1)}, bf16[2,128,1024]{2,1,0:T(8,128)(2,1)S(1)}, u32[]{:S(2)}, u32[]{:S(2)}) collective-permute-start(bf16[2,128,1024]{2,1,0:T(8,128)(2,1)S(1)} %get-tuple-element.55), channel_id=1, source_target_pairs={{0,2},{2,0},{4,6},{6,4},{8,10},{10,8},{12,14},{14,12},{16,18},{18,... | collective-permute-start | bytes 1572872 | tf_op jit(solution)/shard_map/swap/ppermute | solution.py:24
  8.1 11.1 %collective-permute-done.refs_1_.refs_2_ = bf16[2,128,1024]{2,1,0:T(8,128)(2,1)S(1)} collective-permute-done((bf16[2,128,1024]{2,1,0:T(8,128)(2,1)S(1)}, bf16[2,128,1024]{2,1,0:T(8,128)(2,1)S(1)}, u32[]{:S(2)}, u32[]{:S(2)}) %collective-permute-start) | collective-permute-done | bytes 524320 | tf_op jit(solution)/shard_map/swap/ppermute | solution.py:24
  19.2 1.3 %collective-permute-start.1 = (bf16[2,128,1024]{2,1,0:T(8,128)(2,1)S(1)}, bf16[2,128,1024]{2,1,0:T(8,128)(2,1)S(1)}, u32[]{:S(2)}, u32[]{:S(2)}) collective-permute-start(bf16[2,128,1024]{2,1,0:T(8,128)(2,1)S(1)} %collective-permute-done.refs_1_.refs_2_), channel_id=1, source_target_pairs={{8,0},{10,2},{12,4},{14,6},{16,8},{18,10},{20,12},{22,14},{24,16},... | collective-permute-start | bytes 1572872 | tf_op jit(solution)/shard_map/along_1_0/ppermute | solution.py:32
  21.8 1.4 %collective-permute-start.9 = (bf16[2,128,1024]{2,1,0:T(8,128)(2,1)S(1)}, bf16[2,128,1024]{2,1,0:T(8,128)(2,1)S(1)}, u32[]{:S(2)}, u32[]{:S(2)}) collective-permute-start(bf16[2,128,1024]{2,1,0:T(8,128)(2,1)S(1)} %get-tuple-element.35.refs_1_), channel_id=1, source_target_pairs={{8,0},{10,2},{12,4},{14,6},{16,8},{18,10},{20,12},{22,14},{24,16},... | collective-permute-start | bytes 1572872 | tf_op jit(solution)/shard_map/along_0_1/ppermute | solution.py:32
  23.3 1.7 %collective-permute-start.6 = (bf16[2,128,1024]{2,1,0:T(8,128)(2,1)S(1)}, bf16[2,128,1024]{2,1,0:T(8,128)(2,1)S(1)}, u32[]{:S(2)}, u32[]{:S(2)}) collective-permute-start(bf16[2,128,1024]{2,1,0:T(8,128)(2,1)S(1)} %broadcast_select_fusion.3), channel_id=1, source_target_pairs={{0,4},{2,6},{4,0},{6,2},{8,12},{10,14},{12,8},{14,10},{16,20},{18,... | collective-permute-start | bytes 1572872 | tf_op jit(solution)/shard_map/beside_0_0/ppermute | solution.py:28
  25.0 4.6 %collective-permute-done.3.refs_3_ = bf16[2,128,1024]{2,1,0:T(8,128)(2,1)S(1)} collective-permute-done((bf16[2,128,1024]{2,1,0:T(8,128)(2,1)}, bf16[2,128,1024]{2,1,0:T(8,128)(2,1)S(1)}, u32[]{:S(2)}, u32[]{:S(2)}) %collective-permute-start.3) | collective-permute-done | bytes 524320 | tf_op jit(solution)/shard_map/swap/ppermute | solution.py:24
  29.6 6.5 %collective-permute-done.1.refs_5_.refs_10_ = bf16[2,128,1024]{2,1,0:T(8,128)(2,1)S(1)} collective-permute-done((bf16[2,128,1024]{2,1,0:T(8,128)(2,1)S(1)}, bf16[2,128,1024]{2,1,0:T(8,128)(2,1)S(1)}, u32[]{:S(2)}, u32[]{:S(2)}) %collective-permute-start.1) | collective-permute-done | bytes 524320 | tf_op jit(solution)/shard_map/along_1_0/ppermute | solution.py:32
  36.1 1.3 %collective-permute-start.4 = (bf16[2,128,1024]{2,1,0:T(8,128)(2,1)S(1)}, bf16[2,128,1024]{2,1,0:T(8,128)(2,1)}, u32[]{:S(2)}, u32[]{:S(2)}) collective-permute-start(bf16[2,128,1024]{2,1,0:T(8,128)(2,1)S(1)} %collective-permute-done.3.refs_3_), channel_id=1, source_target_pairs={{8,0},{10,2},{12,4},{14,6},{16,8},{18,10},{20,12},{22,14},{24,16},... | collective-permute-start | bytes 1572872 | tf_op jit(solution)/shard_map/along_1_1/ppermute | solution.py:32
  38.2 2.0 %collective-permute-start.7 = (bf16[2,128,1024]{2,1,0:T(8,128)(2,1)}, bf16[2,128,1024]{2,1,0:T(8,128)(2,1)}, u32[]{:S(2)}, u32[]{:S(2)}) collective-permute-start(bf16[2,128,1024]{2,1,0:T(8,128)(2,1)} %broadcast_select_fusion.2), channel_id=1, source_target_pairs={{0,4},{2,6},{4,0},{6,2},{8,12},{10,14},{12,8},{14,10},{16,20},{18,... | collective-permute-start | bytes 1572872 | tf_op jit(solution)/shard_map/beside_1_0/ppermute | solution.py:28
  40.2 7.1 %collective-permute-done.9.refs_9_ = bf16[2,128,1024]{2,1,0:T(8,128)(2,1)S(1)} collective-permute-done((bf16[2,128,1024]{2,1,0:T(8,128)(2,1)S(1)}, bf16[2,128,1024]{2,1,0:T(8,128)(2,1)S(1)}, u32[]{:S(2)}, u32[]{:S(2)}) %collective-permute-start.9) | collective-permute-done | bytes 524320 | tf_op jit(solution)/shard_map/along_0_1/ppermute | solution.py:32
  48.3 2.0 %collective-permute-start.10 = (bf16[2,128,1024]{2,1,0:T(8,128)(2,1)}, bf16[2,128,1024]{2,1,0:T(8,128)(2,1)}, u32[]{:S(2)}, u32[]{:S(2)}) collective-permute-start(bf16[2,128,1024]{2,1,0:T(8,128)(2,1)} %broadcast_select_fusion.1), channel_id=1, source_target_pairs={{0,4},{2,6},{4,0},{6,2},{8,12},{10,14},{12,8},{14,10},{16,20},{18,... | collective-permute-start | bytes 1572872 | tf_op jit(solution)/shard_map/beside_0_1/ppermute | solution.py:28
  50.3 1.5 %collective-permute-start.2 = (s32[2,2]{1,0:T(2,128)S(1)}, s32[2,2]{1,0:T(2,128)S(1)}, u32[]{:S(2)}, u32[]{:S(2)}) collective-permute-start(s32[2,2]{1,0:T(2,128)S(1)} %copy-done.13), channel_id=1, source_target_pairs={{0,2},{2,0},{4,6},{6,4},{8,10},{10,8},{12,14},{14,12},{16,18},{18,... | collective-permute-start | bytes 56 | tf_op jit(solution)/shard_map/pairs/ppermute | solution.py:24
  51.8 2.1 %collective-permute-done.2 = s32[2,2]{1,0:T(2,128)S(1)} collective-permute-done((s32[2,2]{1,0:T(2,128)S(1)}, s32[2,2]{1,0:T(2,128)S(1)}, u32[]{:S(2)}, u32[]{:S(2)}) %collective-permute-start.2) | collective-permute-done | bytes 48 | tf_op jit(solution)/shard_map/pairs/ppermute | solution.py:24
  54.6 1.3 %collective-permute-done.4.refs_11_ = bf16[2,128,1024]{2,1,0:T(8,128)(2,1)} collective-permute-done((bf16[2,128,1024]{2,1,0:T(8,128)(2,1)S(1)}, bf16[2,128,1024]{2,1,0:T(8,128)(2,1)}, u32[]{:S(2)}, u32[]{:S(2)}) %collective-permute-start.4) | collective-permute-done | bytes 524320 | tf_op jit(solution)/shard_map/along_1_1/ppermute | solution.py:32
  55.9 1.9 %broadcast_select_fusion = bf16[2,128,1024]{2,1,0:T(8,128)(2,1)} fusion(bf16[2,128,1024]{2,1,0:T(8,128)(2,1)S(1)} %collective-permute-done.3.refs_3_, bf16[2,128,1024]{2,1,0:T(8,128)(2,1)} %collective-permute-done.4.refs_11_, pred[]{:T(512)S(6)} %eq.32), kind=kLoop, calls=%fused_computation.2 | loop fusion | flops 262144 | bytes 1572865 | tf_op jit(solution)/shard_map/beside_1_1/jit(_where)/select_n | solution.py:263
  58.3 4.9 %shard_map.37 = (f32[2,6,64,128]{3,2,1,0:T(8,128)}, f32[2,6,64,128]{3,2,1,0:T(8,128)}) custom-call(s32[9]{0:T(128)} %pad_add_fusion.meta, f32[8,1024]{1,0:T(8,128)} %constant_dynamic-slice_fusion.3.table, bf16[2,128,1024]{2,1,0:T(8,128)(2,1)} %copy-done.2, bf16[2,128,1024]{2,1,0:T(8,128)(2,1)} %copy-done.6, bf16[2,128,1024]{2,1,0:T(8,128)(2,1)} %copy-done.14, ...), custom_call_target="tpu_custom_call" | custom-call | flops 9999999827968 | bytes 10000000000 | tf_op jit(solution)/shard_map/pallas_call | solution.py:151
  63.3 1.9 %collective-permute-done.8 = f32[2,6,64,128]{3,2,1,0:T(8,128)S(1)} collective-permute-done((f32[2,6,64,128]{3,2,1,0:T(8,128)}, f32[2,6,64,128]{3,2,1,0:T(8,128)S(1)}, u32[]{:S(2)}, u32[]{:S(2)}) %collective-permute-start.8) | collective-permute-done | bytes 393248 | tf_op jit(solution)/shard_map/segments_0/ppermute | solution.py:231
  65.2 1.8 %add.77 = f32[2,6,64,128]{3,2,1,0:T(8,128)} add(f32[2,6,64,128]{3,2,1,0:T(8,128)} %get-tuple-element.32, f32[2,6,64,128]{3,2,1,0:T(8,128)S(1)} %collective-permute-done.8) | non-fusion elementwise | flops 98304 | bytes 1179648 | tf_op jit(solution)/shard_map/segments_0/add | solution.py:280
  67.0 1.8 %collective-permute-start.12 = (f32[2,6,64,128]{3,2,1,0:T(8,128)}, f32[2,6,64,128]{3,2,1,0:T(8,128)}, u32[]{:S(2)}, u32[]{:S(2)}) collective-permute-start(f32[2,6,64,128]{3,2,1,0:T(8,128)} %add.77), channel_id=1, source_target_pairs={{0,2},{2,0},{4,6},{6,4},{8,10},{10,8},{12,14},{14,12},{16,18},{18,... | collective-permute-start | bytes 1179656 | tf_op jit(solution)/shard_map/partner_stacks_0/ppermute | solution.py:24
  68.8 1.4 %collective-permute-done.11.refs_7_ = bf16[2,128,1024]{2,1,0:T(8,128)(2,1)} collective-permute-done((bf16[2,128,1024]{2,1,0:T(8,128)(2,1)}, bf16[2,128,1024]{2,1,0:T(8,128)(2,1)}, u32[]{:S(2)}, u32[]{:S(2)}) %collective-permute-start.11) | collective-permute-done | bytes 524320 | tf_op jit(solution)/shard_map/beside_1_1/ppermute | solution.py:28
  70.2 8.0 %shard_map.38 = (f32[1,6,192,128]{3,2,1,0:T(8,128)}, f32[1,6,192,128]{3,2,1,0:T(8,128)}, f32[1,6,192,128]{3,2,1,0:T(8,128)}, f32[1,6,192,128]{3,2,1,0:T(8,128)}) custom-call(s32[9]{0:T(128)} %pad_add_fusion.meta, f32[8,1024]{1,0:T(8,128)} %constant_dynamic-slice_fusion.3.table, bf16[2,128,1024]{2,1,0:T(8,128)(2,1)} %copy-done.2, ...), custom_call_target="tpu_custom_call" | custom-call | flops 9999999827968 | bytes 10000000000 | tf_op jit(solution)/shard_map/pallas_call | solution.py:151
  79.0 1.7 %collective-permute-done.13 = f32[1,6,192,128]{3,2,1,0:T(8,128)S(1)} collective-permute-done((f32[1,6,192,128]{3,2,1,0:T(8,128)}, f32[1,6,192,128]{3,2,1,0:T(8,128)S(1)}, u32[]{:S(2)}, u32[]{:S(2)}) %collective-permute-start.13) | collective-permute-done | bytes 589856 | tf_op jit(solution)/shard_map/segments_1_0/ppermute | solution.py:231
  80.7 1.9 %add.78 = f32[1,6,192,128]{3,2,1,0:T(8,128)} add(f32[1,6,192,128]{3,2,1,0:T(8,128)} %get-tuple-element.39, f32[1,6,192,128]{3,2,1,0:T(8,128)S(1)} %collective-permute-done.13) | non-fusion elementwise | flops 147456 | bytes 1769472 | tf_op jit(solution)/shard_map/segments_1_0/add | solution.py:280
  82.7 2.2 %collective-permute-start.18 = (f32[1,6,192,128]{3,2,1,0:T(8,128)}, f32[1,6,192,128]{3,2,1,0:T(8,128)}, u32[]{:S(2)}, u32[]{:S(2)}) collective-permute-start(f32[1,6,192,128]{3,2,1,0:T(8,128)} %add.78), channel_id=1, source_target_pairs={{0,2},{2,0},{4,6},{6,4},{8,10},{10,8},{12,14},{14,12},{16,18},{18,... | collective-permute-start | bytes 1769480 | tf_op jit(solution)/shard_map/partner_stacks_1_0/ppermute | solution.py:24
  85.8 8.5 %shard_map.39 = (f32[2,6,128,128]{3,2,1,0:T(8,128)}, f32[2,6,128,128]{3,2,1,0:T(8,128)}, f32[2,6,128,128]{3,2,1,0:T(8,128)}, f32[2,6,128,128]{3,2,1,0:T(8,128)}) custom-call(s32[9]{0:T(128)} %pad_add_fusion.meta, f32[8,1024]{1,0:T(8,128)} %constant_dynamic-slice_fusion.3.table, bf16[2,128,1024]{2,1,0:T(8,128)(2,1)} %copy-done.2, ...), custom_call_target="tpu_custom_call" | custom-call | flops 9999999827968 | bytes 10000000000 | tf_op jit(solution)/shard_map/pallas_call | solution.py:151
  95.0 4.3 %collective-permute-done.18.refs_3_ = f32[1,6,192,128]{3,2,1,0:T(8,128)} collective-permute-done((f32[1,6,192,128]{3,2,1,0:T(8,128)}, f32[1,6,192,128]{3,2,1,0:T(8,128)}, u32[]{:S(2)}, u32[]{:S(2)}) %collective-permute-start.18) | collective-permute-done | bytes 589856 | tf_op jit(solution)/shard_map/partner_stacks_1_0/ppermute | solution.py:24
  99.3 2.1 %collective-permute-start.19 = (f32[1,3,192,128]{3,2,1,0:T(8,128)S(1)}, f32[1,3,192,128]{3,2,1,0:T(8,128)S(1)}, u32[]{:S(2)}, u32[]{:S(2)}) collective-permute-start(f32[1,3,192,128]{3,2,1,0:T(8,128)S(1)} %get-tuple-element.52), channel_id=1, source_target_pairs={{0,2},{2,0},{4,6},{6,4},{8,10},{10,8},{12,14},{14,12},{16,18},{18,... | collective-permute-start | bytes 884744 | tf_op jit(solution)/shard_map/partner_stacks_1_1b/ppermute | solution.py:24
  102.0 1.3 %fusion.spread = bf16[768,768]{1,0:T(8,128)(2,1)} fusion(s32[768]{0:T(1024)S(1)} %fusion.15), kind=kLoop, calls=%fused_computation.1 | loop fusion | flops 1179648 | bytes 1182720 | tf_op jit(solution)/shard_map/convert_element_type | solution.py:303
  105.3 3.4 %shard_map.40.refs_5_ = f32[2,128,1536]{2,1,0:T(8,128)} custom-call(s32[1]{0:T(128)S(6)} %copy.8.pair_count, bf16[768,768]{1,0:T(8,128)(2,1)} %fusion.spread, f32[2,6,128,128]{3,2,1,0:T(8,128)} %add.80.refs_0_, f32[2,6,128,128]{3,2,1,0:T(8,128)} %add.81.refs_1_, f32[2,6,64,128]{3,2,1,0:T(8,128)} %collective-permute-done.12.refs_2_, ...), custom_call_target="tpu_custom_call" | custom-call | flops 1 | bytes 1 | tf_op jit(solution)/shard_map/pallas_call | solution.py:210
  108.7 2.6 %collective-permute-done.19.refs_4_ = f32[1,3,192,128]{3,2,1,0:T(8,128)S(1)} collective-permute-done((f32[1,3,192,128]{3,2,1,0:T(8,128)S(1)}, f32[1,3,192,128]{3,2,1,0:T(8,128)S(1)}, u32[]{:S(2)}, u32[]{:S(2)}) %collective-permute-start.19) | collective-permute-done | bytes 294944 | tf_op jit(solution)/shard_map/partner_stacks_1_1b/ppermute | solution.py:24
  112.1 3.4 %shard_map.41 = f32[2,128,1536]{2,1,0:T(8,128)} custom-call(s32[1]{0:T(128)S(6)} %copy.8.pair_count, bf16[768,768]{1,0:T(8,128)(2,1)} %fusion.spread, f32[2,6,128,128]{3,2,1,0:T(8,128)} %add.80.refs_0_, f32[2,6,128,128]{3,2,1,0:T(8,128)} %add.81.refs_1_, f32[2,6,64,128]{3,2,1,0:T(8,128)} %collective-permute-done.12.refs_2_, ...), custom_call_target="tpu_custom_call", output_to_operand_aliasing={{}: (7, {})} | custom-call | flops 1 | bytes 1 | tf_op jit(solution)/shard_map/pallas_call | solution.py:210
  (68 shorter events, 12.3 us)
Async XLA Ops:
  3.5 44.7 %copy-start.1 = (bf16[2,128,1024]{2,1,0:T(8,128)(2,1)}, bf16[2,128,1024]{2,1,0:T(8,128)(2,1)S(1)}, u32[]{:S(2)}) copy-start(bf16[2,128,1024]{2,1,0:T(8,128)(2,1)S(1)} %get-tuple-element.35.refs_1_) | copy-start | bytes 1572868
  3.5 44.7 %copy-start.2 = (bf16[2,128,1024]{2,1,0:T(8,128)(2,1)}, bf16[2,128,1024]{2,1,0:T(8,128)(2,1)S(1)}, u32[]{:S(2)}) copy-start(bf16[2,128,1024]{2,1,0:T(8,128)(2,1)S(1)} %get-tuple-element.54.refs_0_) | copy-start | bytes 1572868
  3.5 15.7 %collective-permute-start = (bf16[2,128,1024]{2,1,0:T(8,128)(2,1)S(1)}, bf16[2,128,1024]{2,1,0:T(8,128)(2,1)S(1)}, u32[]{:S(2)}, u32[]{:S(2)}) collective-permute-start(bf16[2,128,1024]{2,1,0:T(8,128)(2,1)S(1)} %get-tuple-element.55), channel_id=1, source_target_pairs={{0,2},{2,0},{4,6},{6,4},{8,10},{10,8},{12,14},{14,12},{16,18},{18,... | collective-permute-start | bytes 1572872 | tf_op jit(solution)/shard_map/swap/ppermute | solution.py:24
  6.4 23.2 %collective-permute-start.3 = (bf16[2,128,1024]{2,1,0:T(8,128)(2,1)}, bf16[2,128,1024]{2,1,0:T(8,128)(2,1)S(1)}, u32[]{:S(2)}, u32[]{:S(2)}) collective-permute-start(bf16[2,128,1024]{2,1,0:T(8,128)(2,1)} %get-tuple-element.56), channel_id=1, source_target_pairs={{0,2},{2,0},{4,6},{6,4},{8,10},{10,8},{12,14},{14,12},{16,18},{18,... | collective-permute-start | bytes 1572872 | tf_op jit(solution)/shard_map/swap/ppermute | solution.py:24
  6.5 15.3 %collective-permute-start.5 = (bf16[2,128,1024]{2,1,0:T(8,128)(2,1)S(1)}, bf16[2,128,1024]{2,1,0:T(8,128)(2,1)S(1)}, u32[]{:S(2)}, u32[]{:S(2)}) collective-permute-start(bf16[2,128,1024]{2,1,0:T(8,128)(2,1)S(1)} %get-tuple-element.54.refs_0_), channel_id=1, source_target_pairs={{8,0},{10,2},{12,4},{14,6},{16,8},{18,10},{20,12},{22,14},{24,16},... | collective-permute-start | bytes 1572872 | tf_op jit(solution)/shard_map/along_0_0/ppermute | solution.py:32
  19.2 29.1 %copy-start.6 = (bf16[2,128,1024]{2,1,0:T(8,128)(2,1)}, bf16[2,128,1024]{2,1,0:T(8,128)(2,1)S(1)}, u32[]{:S(2)}) copy-start(bf16[2,128,1024]{2,1,0:T(8,128)(2,1)S(1)} %collective-permute-done.refs_1_.refs_2_) | copy-start | bytes 1572868
  19.2 16.9 %collective-permute-start.1 = (bf16[2,128,1024]{2,1,0:T(8,128)(2,1)S(1)}, bf16[2,128,1024]{2,1,0:T(8,128)(2,1)S(1)}, u32[]{:S(2)}, u32[]{:S(2)}) collective-permute-start(bf16[2,128,1024]{2,1,0:T(8,128)(2,1)S(1)} %collective-permute-done.refs_1_.refs_2_), channel_id=1, source_target_pairs={{8,0},{10,2},{12,4},{14,6},{16,8},{18,10},{20,12},{22,14},{24,16},... | collective-permute-start | bytes 1572872 | tf_op jit(solution)/shard_map/along_1_0/ppermute | solution.py:32
  21.8 26.4 %copy-start.8 = (bf16[2,128,1024]{2,1,0:T(8,128)(2,1)}, bf16[2,128,1024]{2,1,0:T(8,128)(2,1)S(1)}, u32[]{:S(2)}) copy-start(bf16[2,128,1024]{2,1,0:T(8,128)(2,1)S(1)} %collective-permute-done.5.refs_4_.refs_8_) | copy-start | bytes 1572868
  21.8 28.5 %copy-start.13 = (s32[2,2]{1,0:T(2,128)S(1)}, s32[2,2]{1,0:T(2,128)}, u32[]{:S(2)}) copy-start(s32[2,2]{1,0:T(2,128)} %param.4) | copy-start | bytes 52
  21.8 25.5 %collective-permute-start.9 = (bf16[2,128,1024]{2,1,0:T(8,128)(2,1)S(1)}, bf16[2,128,1024]{2,1,0:T(8,128)(2,1)S(1)}, u32[]{:S(2)}, u32[]{:S(2)}) collective-permute-start(bf16[2,128,1024]{2,1,0:T(8,128)(2,1)S(1)} %get-tuple-element.35.refs_1_), channel_id=1, source_target_pairs={{8,0},{10,2},{12,4},{14,6},{16,8},{18,10},{20,12},{22,14},{24,16},... | collective-permute-start | bytes 1572872 | tf_op jit(solution)/shard_map/along_0_1/ppermute | solution.py:32
  23.3 25.0 %collective-permute-start.6 = (bf16[2,128,1024]{2,1,0:T(8,128)(2,1)S(1)}, bf16[2,128,1024]{2,1,0:T(8,128)(2,1)S(1)}, u32[]{:S(2)}, u32[]{:S(2)}) collective-permute-start(bf16[2,128,1024]{2,1,0:T(8,128)(2,1)S(1)} %broadcast_select_fusion.3), channel_id=1, source_target_pairs={{0,4},{2,6},{4,0},{6,2},{8,12},{10,14},{12,8},{14,10},{16,20},{18,... | collective-permute-start | bytes 1572872 | tf_op jit(solution)/shard_map/beside_0_0/ppermute | solution.py:28
  29.6 28.2 %copy-start.7 = (bf16[2,128,1024]{2,1,0:T(8,128)(2,1)}, bf16[2,128,1024]{2,1,0:T(8,128)(2,1)S(1)}, u32[]{:S(2)}) copy-start(bf16[2,128,1024]{2,1,0:T(8,128)(2,1)S(1)} %collective-permute-done.3.refs_3_) | copy-start | bytes 1572868
  36.1 21.7 %copy-start.9 = (bf16[2,128,1024]{2,1,0:T(8,128)(2,1)}, bf16[2,128,1024]{2,1,0:T(8,128)(2,1)S(1)}, u32[]{:S(2)}) copy-start(bf16[2,128,1024]{2,1,0:T(8,128)(2,1)S(1)} %collective-permute-done.1.refs_5_.refs_10_) | copy-start | bytes 1572868
  36.1 19.9 %collective-permute-start.4 = (bf16[2,128,1024]{2,1,0:T(8,128)(2,1)S(1)}, bf16[2,128,1024]{2,1,0:T(8,128)(2,1)}, u32[]{:S(2)}, u32[]{:S(2)}) collective-permute-start(bf16[2,128,1024]{2,1,0:T(8,128)(2,1)S(1)} %collective-permute-done.3.refs_3_), channel_id=1, source_target_pairs={{8,0},{10,2},{12,4},{14,6},{16,8},{18,10},{20,12},{22,14},{24,16},... | collective-permute-start | bytes 1572872 | tf_op jit(solution)/shard_map/along_1_1/ppermute | solution.py:32
  38.2 19.6 %collective-permute-start.7 = (bf16[2,128,1024]{2,1,0:T(8,128)(2,1)}, bf16[2,128,1024]{2,1,0:T(8,128)(2,1)}, u32[]{:S(2)}, u32[]{:S(2)}) collective-permute-start(bf16[2,128,1024]{2,1,0:T(8,128)(2,1)} %broadcast_select_fusion.2), channel_id=1, source_target_pairs={{0,4},{2,6},{4,0},{6,2},{8,12},{10,14},{12,8},{14,10},{16,20},{18,... | collective-permute-start | bytes 1572872 | tf_op jit(solution)/shard_map/beside_1_0/ppermute | solution.py:28
  48.3 5.6 %copy-start.14 = (bf16[2,128,1024]{2,1,0:T(8,128)(2,1)}, bf16[2,128,1024]{2,1,0:T(8,128)(2,1)S(1)}, u32[]{:S(2)}) copy-start(bf16[2,128,1024]{2,1,0:T(8,128)(2,1)S(1)} %collective-permute-done.6.refs_2_.refs_4_) | copy-start | bytes 1572868
  48.3 20.5 %collective-permute-start.10 = (bf16[2,128,1024]{2,1,0:T(8,128)(2,1)}, bf16[2,128,1024]{2,1,0:T(8,128)(2,1)}, u32[]{:S(2)}, u32[]{:S(2)}) collective-permute-start(bf16[2,128,1024]{2,1,0:T(8,128)(2,1)} %broadcast_select_fusion.1), channel_id=1, source_target_pairs={{0,4},{2,6},{4,0},{6,2},{8,12},{10,14},{12,8},{14,10},{16,20},{18,... | collective-permute-start | bytes 1572872 | tf_op jit(solution)/shard_map/beside_0_1/ppermute | solution.py:28
  50.3 3.6 %collective-permute-start.2 = (s32[2,2]{1,0:T(2,128)S(1)}, s32[2,2]{1,0:T(2,128)S(1)}, u32[]{:S(2)}, u32[]{:S(2)}) collective-permute-start(s32[2,2]{1,0:T(2,128)S(1)} %copy-done.13), channel_id=1, source_target_pairs={{0,2},{2,0},{4,6},{6,4},{8,10},{10,8},{12,14},{14,12},{16,18},{18,... | collective-permute-start | bytes 56 | tf_op jit(solution)/shard_map/pairs/ppermute | solution.py:24
  57.8 12.4 %collective-permute-start.11 = (bf16[2,128,1024]{2,1,0:T(8,128)(2,1)}, bf16[2,128,1024]{2,1,0:T(8,128)(2,1)}, u32[]{:S(2)}, u32[]{:S(2)}) collective-permute-start(bf16[2,128,1024]{2,1,0:T(8,128)(2,1)} %broadcast_select_fusion), channel_id=1, source_target_pairs={{0,4},{2,6},{4,0},{6,2},{8,12},{10,14},{12,8},{14,10},{16,20},{18,... | collective-permute-start | bytes 1572872 | tf_op jit(solution)/shard_map/beside_1_1/ppermute | solution.py:28
  63.2 2.0 %collective-permute-start.8 = (f32[2,6,64,128]{3,2,1,0:T(8,128)}, f32[2,6,64,128]{3,2,1,0:T(8,128)S(1)}, u32[]{:S(2)}, u32[]{:S(2)}) collective-permute-start(f32[2,6,64,128]{3,2,1,0:T(8,128)} %get-tuple-element.33), channel_id=1, source_target_pairs={{0,1},{1,0},{2,3},{3,2},{4,5},{5,4},{6,7},{7,6},{8,9},{9,8},{10,11... | collective-permute-start | bytes 1179656 | tf_op jit(solution)/shard_map/segments_0/ppermute | solution.py:231
  67.0 11.5 %collective-permute-start.12 = (f32[2,6,64,128]{3,2,1,0:T(8,128)}, f32[2,6,64,128]{3,2,1,0:T(8,128)}, u32[]{:S(2)}, u32[]{:S(2)}) collective-permute-start(f32[2,6,64,128]{3,2,1,0:T(8,128)} %add.77), channel_id=1, source_target_pairs={{0,2},{2,0},{4,6},{6,4},{8,10},{10,8},{12,14},{14,12},{16,18},{18,... | collective-permute-start | bytes 1179656 | tf_op jit(solution)/shard_map/partner_stacks_0/ppermute | solution.py:24
  78.2 6.7 %copy-start.5 = (f32[1,6,192,128]{3,2,1,0:T(8,128)S(1)}, f32[1,6,192,128]{3,2,1,0:T(8,128)}, u32[]{:S(2)}) copy-start(f32[1,6,192,128]{3,2,1,0:T(8,128)} %get-tuple-element.43) | copy-start | bytes 1769476
  78.5 2.2 %collective-permute-start.13 = (f32[1,6,192,128]{3,2,1,0:T(8,128)}, f32[1,6,192,128]{3,2,1,0:T(8,128)S(1)}, u32[]{:S(2)}, u32[]{:S(2)}) collective-permute-start(f32[1,6,192,128]{3,2,1,0:T(8,128)} %get-tuple-element.41), channel_id=1, source_target_pairs={{0,1},{1,0},{2,3},{3,2},{4,5},{5,4},{6,7},{7,6},{8,9},{9,8},{10,11... | collective-permute-start | bytes 1769480 | tf_op jit(solution)/shard_map/segments_1_0/ppermute | solution.py:231
  78.5 6.3 %collective-permute-start.14 = (f32[1,6,192,128]{3,2,1,0:T(8,128)}, f32[1,6,192,128]{3,2,1,0:T(8,128)S(1)}, u32[]{:S(2)}, u32[]{:S(2)}) collective-permute-start(f32[1,6,192,128]{3,2,1,0:T(8,128)} %get-tuple-element.45), channel_id=1, source_target_pairs={{0,1},{1,0},{2,3},{3,2},{4,5},{5,4},{6,7},{7,6},{8,9},{9,8},{10,11... | collective-permute-start | bytes 1769480 | tf_op jit(solution)/shard_map/segments_1_1/ppermute | solution.py:231
  82.7 16.6 %collective-permute-start.18 = (f32[1,6,192,128]{3,2,1,0:T(8,128)}, f32[1,6,192,128]{3,2,1,0:T(8,128)}, u32[]{:S(2)}, u32[]{:S(2)}) collective-permute-start(f32[1,6,192,128]{3,2,1,0:T(8,128)} %add.78), channel_id=1, source_target_pairs={{0,2},{2,0},{4,6},{6,4},{8,10},{10,8},{12,14},{14,12},{16,18},{18,... | collective-permute-start | bytes 1769480 | tf_op jit(solution)/shard_map/partner_stacks_1_0/ppermute | solution.py:24
  85.8 9.1 %copy-start = (f32[1,6,192,128]{3,2,1,0:T(8,128)S(1)}, f32[1,6,192,128]{3,2,1,0:T(8,128)}, u32[]{:S(2)}) copy-start(f32[1,6,192,128]{3,2,1,0:T(8,128)} %add.79) | copy-start | bytes 1769476
  94.2 9.1 %copy-start.4 = (f32[2,6,128,128]{3,2,1,0:T(8,128)S(1)}, f32[2,6,128,128]{3,2,1,0:T(8,128)}, u32[]{:S(2)}) copy-start(f32[2,6,128,128]{3,2,1,0:T(8,128)} %get-tuple-element.47) | copy-start | bytes 2359300
  94.3 10.0 %copy-start.3 = (f32[2,6,128,128]{3,2,1,0:T(8,128)S(1)}, f32[2,6,128,128]{3,2,1,0:T(8,128)}, u32[]{:S(2)}) copy-start(f32[2,6,128,128]{3,2,1,0:T(8,128)} %get-tuple-element.49) | copy-start | bytes 2359300
  94.3 9.0 %collective-permute-start.15 = (f32[2,6,128,128]{3,2,1,0:T(8,128)}, f32[2,6,128,128]{3,2,1,0:T(8,128)S(1)}, u32[]{:S(2)}, u32[]{:S(2)}) collective-permute-start(f32[2,6,128,128]{3,2,1,0:T(8,128)} %get-tuple-element.48), channel_id=1, source_target_pairs={{0,1},{1,0},{2,3},{3,2},{4,5},{5,4},{6,7},{7,6},{8,9},{9,8},{10,11... | collective-permute-start | bytes 2359304 | tf_op jit(solution)/shard_map/segments_own_0/ppermute | solution.py:231
  94.3 9.9 %collective-permute-start.16 = (f32[2,6,128,128]{3,2,1,0:T(8,128)}, f32[2,6,128,128]{3,2,1,0:T(8,128)S(1)}, u32[]{:S(2)}, u32[]{:S(2)}) collective-permute-start(f32[2,6,128,128]{3,2,1,0:T(8,128)} %get-tuple-element.50), channel_id=1, source_target_pairs={{0,1},{1,0},{2,3},{3,2},{4,5},{5,4},{6,7},{7,6},{8,9},{9,8},{10,11... | collective-permute-start | bytes 2359304 | tf_op jit(solution)/shard_map/segments_own_1/ppermute | solution.py:231
  94.9 13.8 %collective-permute-start.17 = (f32[1,3,192,128]{3,2,1,0:T(8,128)S(1)}, f32[1,3,192,128]{3,2,1,0:T(8,128)S(1)}, u32[]{:S(2)}, u32[]{:S(2)}) collective-permute-start(f32[1,3,192,128]{3,2,1,0:T(8,128)S(1)} %get-tuple-element.58), channel_id=1, source_target_pairs={{0,2},{2,0},{4,6},{6,4},{8,10},{10,8},{12,14},{14,12},{16,18},{18,... | collective-permute-start | bytes 884744 | tf_op jit(solution)/shard_map/partner_stacks_1_1a/ppermute | solution.py:24
  99.3 12.1 %collective-permute-start.19 = (f32[1,3,192,128]{3,2,1,0:T(8,128)S(1)}, f32[1,3,192,128]{3,2,1,0:T(8,128)S(1)}, u32[]{:S(2)}, u32[]{:S(2)}) collective-permute-start(f32[1,3,192,128]{3,2,1,0:T(8,128)S(1)} %get-tuple-element.52), channel_id=1, source_target_pairs={{0,2},{2,0},{4,6},{6,4},{8,10},{10,8},{12,14},{14,12},{16,18},{18,... | collective-permute-start | bytes 884744 | tf_op jit(solution)/shard_map/partner_stacks_1_1b/ppermute | solution.py:24
  (3 other events, 4.3 us)
